TPU v7x, 32 devices: a whole 2x2x4 slice. The times are simulated.
32 devices in a mesh: grp: 4 (over x, core), dev: 8 (over z, y).
Axes of the slice: x: 2, y: 2, z: 4, core: 2. Of those that a mesh axis runs over, the one named last changes fastest.
Arguments:
- student: bfloat16 [4096, 1024], P(('grp', 'dev')), may hold values from -0.19921875 to 0.19921875
- teacher: bfloat16 [4096, 1024], P(('grp', 'dev')), may hold values from -0.19921875 to 0.19921875
- labels: int32 [4096], P(('grp', 'dev')), may hold values from 0 to 999, as said below
Outputs:
- supcon_loss: float32 [], replicated
- relation_loss: float32 [], replicated
- feature_grad: float32 [4096, 1024], P(('grp', 'dev'))
Inputs may be any that keep to these rules, and one draw needn't show every extreme that they name: `labels`: each label from 875 upward belongs to exactly one view of the batch; every other view has a label below 875.
All inputs are finite; a program needn't handle non-finite values.
Results may differ from a plain program's by a relative error of at most 0.0003.
The roundings to bfloat16 on the way count: a program that leaves them out, or rounds other values in their place, can miss the bound.
Values may be sent and summed in bfloat16 or wider, within the bound.
No kernel may reach another device: no remote copies, remote signals or barrier semaphores. Data moves between devices by JAX's collectives and lax.ppermute only.
A program may use at most 128 MiB of HBM per device.

v0:
```python
import math

import jax
import jax.numpy as jnp
from jax import lax
from jax.sharding import PartitionSpec as P

temp_sup = 0.1
temp_student = 0.2
temp_teacher = 0.05
epsilon = 1e-06


def unit_rows(raw):
    values = raw.astype(jnp.float32)
    scaling = lax.rsqrt(jnp.sum(values * values, axis=1, keepdims=True) + epsilon)
    return (values * scaling, scaling)


def inner_rows(left, right):
    return lax.dot_general(
        left, right, (((1,), (1,)), ((), ())), preferred_element_type=jnp.float32
    )


def tile_terms(
    anchor_unit,
    anchor_teacher,
    anchor_label,
    anchor_place,
    key_unit,
    key_teacher,
    key_label,
    key_place,
):
    similar = inner_rows(anchor_unit, key_unit)
    teacher_sim = inner_rows(anchor_teacher, key_teacher)
    distinct = anchor_place[:, None] != key_place[None, :]
    positive = jnp.logical_and(anchor_label[:, None] == key_label[None, :], distinct).astype(
        jnp.float32
    )
    empty = jnp.zeros_like(similar)
    sup_exp = jnp.where(distinct, jnp.exp((similar - 1.0) / temp_sup), empty)
    rel_exp = jnp.where(distinct, jnp.exp((similar - 1.0) / temp_student), empty)
    teacher_exp = jnp.where(distinct, jnp.exp((teacher_sim - 1.0) / temp_teacher), empty)
    return (similar, positive, sup_exp, rel_exp, teacher_exp)


def tile_stats(terms):
    similar, positive, sup_exp, rel_exp, teacher_exp = terms
    return (
        jnp.sum(sup_exp, axis=1),
        jnp.sum(rel_exp, axis=1),
        jnp.sum(teacher_exp, axis=1),
        jnp.sum(teacher_exp * similar, axis=1),
        jnp.sum(positive * similar, axis=1),
        jnp.sum(positive, axis=1),
    )


def coefficient(terms, sup_total, rel_total, teacher_total, positives):
    similar, positive, sup_exp, rel_exp, teacher_exp = terms
    return (sup_exp / sup_total - positive / positives) / temp_sup + (
        rel_exp / rel_total - teacher_exp / teacher_total
    ) / temp_student


def row_losses(stats):
    sup_total, rel_total, teacher_total, teacher_mix, positive_sum, positive_count = stats
    positives = jnp.maximum(positive_count, 1.0)
    contrast = (1.0 - positive_sum / positives) / temp_sup + jnp.log(sup_total)
    relation = (1.0 - teacher_mix / teacher_total) / temp_student + jnp.log(rel_total)
    return (contrast, relation)


def coef_inputs(stats):
    return (stats[0], stats[1], stats[2], jnp.maximum(stats[5], 1.0))


def body(student, teacher, labels):
    row_count = student.shape[0]
    width = student.shape[1]
    groups = lax.axis_size("grp")
    members = lax.axis_size("dev")
    unit_student, scaling = unit_rows(student)
    unit_rounded = unit_student.astype(jnp.bfloat16)
    teacher_rounded = unit_rows(teacher)[0].astype(jnp.bfloat16)
    anchor_unit, anchor_teacher, anchor_label = (
        lax.all_gather(unit_rounded, "dev", axis=0, tiled=True),
        lax.all_gather(teacher_rounded, "dev", axis=0, tiled=True),
        lax.all_gather(labels, "dev", axis=0, tiled=True),
    )
    key_unit, key_teacher, key_label = (
        lax.all_gather(unit_rounded, "grp", axis=0, tiled=True),
        lax.all_gather(teacher_rounded, "grp", axis=0, tiled=True),
        lax.all_gather(labels, "grp", axis=0, tiled=True),
    )
    group_index = lax.axis_index("grp")
    member_index = lax.axis_index("dev")
    slab_rows = members * row_count
    key_count = groups * row_count
    view_count = row_count * groups * members
    anchor_place = group_index * slab_rows + jnp.arange(slab_rows, dtype=jnp.int32)
    key_place = (
        (jnp.arange(groups, dtype=jnp.int32)[:, None] * members + member_index) * row_count
        + jnp.arange(row_count, dtype=jnp.int32)[None, :]
    ).reshape(key_count)
    block_rows = math.gcd(slab_rows, 512)
    block_total = slab_rows // block_rows
    blocked = (
        anchor_unit.reshape(block_total, block_rows, width),
        anchor_teacher.reshape(block_total, block_rows, width),
        anchor_label.reshape(block_total, block_rows),
        anchor_place.reshape(block_total, block_rows),
    )

    def block_terms(operands):
        return tile_terms(
            operands[0],
            operands[1],
            operands[2],
            operands[3],
            key_unit,
            key_teacher,
            key_label,
            key_place,
        )

    def stats_block(operands):
        return tile_stats(block_terms(operands))

    partial_stats = lax.map(stats_block, blocked)
    local_stats = tuple((item.reshape(slab_rows) for item in partial_stats))
    slab_stats = lax.psum(local_stats, "dev")
    own_stats = tuple(
        (lax.dynamic_slice_in_dim(item, member_index * row_count, row_count) for item in slab_stats)
    )
    contrast, relation = row_losses(own_stats)
    loss_totals = lax.psum((jnp.sum(contrast), jnp.sum(relation)), ("grp", "dev"))
    supcon_loss = loss_totals[0] / view_count
    relation_loss = loss_totals[1] / view_count
    blocked_stats = tuple(
        (item.reshape(block_total, block_rows) for item in coef_inputs(slab_stats))
    )
    gathered_stats = lax.all_gather(own_stats, "grp", axis=0, tiled=True)
    key_stats = coef_inputs(gathered_stats)

    def pair_block(operands):
        terms = block_terms(operands)
        row_part = coefficient(
            terms,
            operands[4][:, None],
            operands[5][:, None],
            operands[6][:, None],
            operands[7][:, None],
        ).astype(jnp.bfloat16)
        column_part = coefficient(
            terms,
            key_stats[0][None, :],
            key_stats[1][None, :],
            key_stats[2][None, :],
            key_stats[3][None, :],
        ).astype(jnp.bfloat16)
        return (row_part, column_part)

    row_coef, column_coef = lax.map(pair_block, blocked + blocked_stats)
    row_coef = row_coef.reshape(slab_rows, key_count)
    column_coef = column_coef.reshape(slab_rows, key_count)
    first = lax.dot_general(
        row_coef, anchor_unit, (((0,), (0,)), ((), ())), preferred_element_type=jnp.float32
    )
    second = lax.dot_general(
        column_coef, anchor_unit, (((0,), (0,)), ((), ())), preferred_element_type=jnp.float32
    )
    grad = lax.psum_scatter(first + second, "grp", scatter_dimension=0, tiled=True)
    along = jnp.sum(unit_student * grad, axis=1, keepdims=True)
    feature_grad = scaling * (grad - unit_student * along)
    return (supcon_loss, relation_loss, feature_grad)


def solution(mesh):
    placed = (P(("grp", "dev"), None), P(("grp", "dev"), None), P(("grp", "dev")))
    return jax.shard_map(
        body,
        mesh=mesh,
        in_specs=placed,
        out_specs=(P(), P(), P(("grp", "dev"), None)),
        check_vma=False,
    )
```

profile of v0, /device:TPU:0, one launch (start us, length us, event | category | flops | bytes accessed | tf_op | source)
XLA Modules:
  0.0 280.1 jit_solution(14025700318690340708)
XLA Ops:
  7.2 0.0 all-gather.13.cloned.1.call-start
  7.2 1.1 fusion.37
  8.3 1.8 fusion.33
  10.1 0.0 all-gather.13.cloned.1.call-update
  10.1 0.0 all-gather.17.cloned.1.call-start
  10.2 1.1 fusion.38
  11.3 1.8 fusion.39
  13.0 0.0 all-gather.17.cloned.1.call-update
  13.0 0.0 all-gather.11.cloned.1.call-start
  13.1 0.7 all-gather.11.cloned.1.call-update
  13.8 0.0 all-gather.15.cloned.1.call-start
  13.8 0.5 all-gather.15.cloned.1.call-update
  14.4 0.0 reduce-scatter.2.cloned.1.call-start
  14.5 22.2 %all-gather = s32[8,1,128]{2,1,0:T(1,128)S(1)} all-gather(s32[1,1,128]{2,1,0:T(1,128)S(1)} %bitcast.157), channel_id=1, replica_groups=mesh['grp'=4,'dev'=8] {'dev'}, dimensions={0}, use_global_device_ids=true | all-gather | bytes 4608 | tf_op jit(solution)/shard_map/all_gather | solution.py:91
  36.7 0.5 broadcast.211
  37.2 0.6 reduce.3
  37.9 5.0 %all-gather.1 = s32[4,1,128]{2,1,0:T(1,128)S(1)} all-gather(s32[1,1,128]{2,1,0:T(1,128)S(1)} %bitcast.158), channel_id=1, replica_groups=mesh['grp'=4,'dev'=8] {'grp'}, dimensions={0}, use_global_device_ids=true | all-gather | bytes 2560 | tf_op jit(solution)/shard_map/all_gather | solution.py:96
  42.9 0.0 all-gather.13.cloned.1.call-done
  42.9 5.1 %all-gather.17.cloned.1.call-done = bf16[512,1024]{1,0:T(8,128)(2,1)} async-done(((bf16[128,1024]{1,0:T(8,128)(2,1)}), bf16[512,1024]{1,0:T(8,128)(2,1)}) %all-gather.17.cloned.1.call-update) | async-done | bytes 1048592 | tf_op jit(solution)/shard_map/all_gather | solution.py:95
  48.0 52.0 %all-gather.11.cloned.1.call-done = bf16[1024,1024]{1,0:T(8,128)(2,1)} async-done(((bf16[128,1024]{1,0:T(8,128)(2,1)}), bf16[1024,1024]{1,0:T(8,128)(2,1)}) %all-gather.11.cloned.1.call-update) | async-done | bytes 2097168 | tf_op jit(solution)/shard_map/all_gather | solution.py:89
  100.0 49.8 %all-gather.15.cloned.1.call-done = bf16[1024,1024]{1,0:T(8,128)(2,1)} async-done(((bf16[128,1024]{1,0:T(8,128)(2,1)}), bf16[1024,1024]{1,0:T(8,128)(2,1)}) %all-gather.15.cloned.1.call-update) | async-done | bytes 2097168 | tf_op jit(solution)/shard_map/all_gather | solution.py:90
  149.8 8.5 %while.40 = (s32[]{:T(128)}, f32[2,512]{1,0:T(2,128)S(1)}, f32[2,512]{1,0:T(2,128)S(1)}, f32[2,512]{1,0:T(2,128)S(1)}, f32[2,512]{1,0:T(2,128)S(1)}, /*index=5*/...) while((s32[]{:T(128)}, f32[2,512]{1,0:T(2,128)S(1)}, ...), condition=%wide.region_9.10_spmd.clone, body=%wide.region_2.9_spmd.clone.sunk | while | flops 1079244288 | bytes 18934532 | solution.py:132
  149.8 0.1 add_bitcast_fusion.4
  149.9 2.5 compare_select_fusion.7
  152.4 1.4 select_reduce_fusion.2
  154.1 0.1 add_bitcast_fusion.4
  154.2 2.5 compare_select_fusion.7
  156.7 1.4 select_reduce_fusion.2
  158.4 34.6 %all-reduce.1 = (f32[1024]{0:T(1024)S(1)}, f32[1024]{0:T(1024)S(1)}, f32[1024]{0:T(1024)S(1)}, f32[1024]{0:T(1024)S(1)}, f32[1024]{0:T(1024)S(1)}, /*index=5*/f32[1024]{0:T(1024)S(1)}) all-reduce(f32[1024]{0:T(1024)S(1)} %bitcast.145, f32[1024]{0:T(1024)S(1)} %bitcast.147, ...), channel_id=1, replica_groups=mesh['grp'=4,'dev'=8] {'dev'}, use_global_device_ids=true, to_apply=%region_10.11 | all-reduce | flops 6144 | bytes 49152 | tf_op jit(solution)/shard_map/psum | solution.py:134
  193.0 0.7 dynamic-slice_bitcast_fusion.3
  193.7 5.0 %all-gather.3 = f32[4,1,128]{2,1,0:T(1,128)S(1)} all-gather(f32[1,1,128]{2,1,0:T(1,128)S(1)} %get-tuple-element.684), channel_id=1, replica_groups=mesh['grp'=4,'dev'=8] {'grp'}, dimensions={0}, use_global_device_ids=true | all-gather | bytes 2560 | tf_op jit(solution)/shard_map/all_gather | solution.py:145
  198.8 0.7 dynamic-slice_bitcast_fusion.1
  199.5 5.0 %all-gather.5 = f32[4,1,128]{2,1,0:T(1,128)S(1)} all-gather(f32[1,1,128]{2,1,0:T(1,128)S(1)} %get-tuple-element.681), channel_id=1, replica_groups=mesh['grp'=4,'dev'=8] {'grp'}, dimensions={0}, use_global_device_ids=true | all-gather | bytes 2560 | tf_op jit(solution)/shard_map/all_gather | solution.py:145
  204.5 5.0 %all-gather.4 = f32[4,1,128]{2,1,0:T(1,128)S(1)} all-gather(f32[1,1,128]{2,1,0:T(1,128)S(1)} %get-tuple-element.683), channel_id=1, replica_groups=mesh['grp'=4,'dev'=8] {'grp'}, dimensions={0}, use_global_device_ids=true | all-gather | bytes 2560 | tf_op jit(solution)/shard_map/all_gather | solution.py:145
  209.5 5.0 %all-gather.2 = f32[4,1,128]{2,1,0:T(1,128)S(1)} all-gather(f32[1,1,128]{2,1,0:T(1,128)S(1)} %get-tuple-element.686), channel_id=1, replica_groups=mesh['grp'=4,'dev'=8] {'grp'}, dimensions={0}, use_global_device_ids=true | all-gather | bytes 2560 | tf_op jit(solution)/shard_map/all_gather | solution.py:145
  214.5 9.2 %while.41 = (s32[]{:T(128)}, bf16[2,512,512]{2,1,0:T(8,128)(2,1)S(1)}, bf16[2,512,512]{2,1,0:T(8,128)(2,1)S(1)}, s32[2,512]{1,0:T(2,128)S(1)}, bf16[2,512,1024]{...) while((s32[]{:T(128)}, ...), condition=%wide.region_21.22_spmd.clone, body=%wide.region_20.21_spmd.clone.sunk | while | flops 1082130944 | bytes 19975944 | solution.py:166
  214.6 2.4 convolution_add_fusion.5
  217.0 0.1 add_bitcast_fusion.5
  217.1 2.0 bitcast_dynamic-update-slice_fusion.3
  219.2 2.4 convolution_add_fusion.5
  221.6 0.1 add_bitcast_fusion.5
  221.7 2.0 bitcast_dynamic-update-slice_fusion.3
  223.7 3.0 %fusion.40 = f32[512,1024]{1,0:T(8,128)S(1)} fusion(bf16[1024,512]{1,0:T(8,128)(2,1)S(1)} %bitcast.129, bf16[1024,1024]{1,0:T(8,128)(2,1)} %bitcast.127), kind=kOutput, calls=%fused_computation.85 | convolution fusion | flops 1073741824 | bytes 5242880 | tf_op jit(solution)/shard_map/dot_general | solution.py:169
  226.8 2.7 convolution_add_fusion.3
  229.4 37.2 %all-reduce = (f32[]{:T(128)}, f32[]{:T(128)}) all-reduce(f32[]{:T(128)} %get-tuple-element.685, f32[]{:T(128)} %get-tuple-element.682), channel_id=1, replica_groups=mesh['grp'=4,'dev'=8] {'grp','dev'}, use_global_device_ids=true, to_apply=%region_14.15 | all-reduce | flops 2 | bytes 16 | tf_op jit(solution)/shard_map/psum | solution.py:139
  267.9 0.0 reduce-scatter.2.cloned.1.call-done
  268.0 1.3 fusion.34
  269.2 2.1 fusion.36
  (68 shorter events, 0.8 us)
Async XLA Ops:
  7.2 7.3 %copy-start.3 = (s32[128]{0:T(128)S(1)}, s32[128]{0:T(128)}, u32[]{:S(2)}) copy-start(s32[128]{0:T(128)} %param.9) | copy-start | bytes 1540
  7.2 35.8 %all-gather.13.cloned.1.call-start = ((), (), s32[]{:S(2)}) async-start(), calls=%async_computation.2 | async-start | bytes 1310720 | tf_op jit(solution)/shard_map/all_gather | solution.py:94
  10.1 37.9 %all-gather.17.cloned.1.call-start = ((), (), s32[]{:S(2)}) async-start(), calls=%async_computation.4 | async-start | bytes 1310720 | tf_op jit(solution)/shard_map/all_gather | solution.py:95
  13.0 87.0 %all-gather.11.cloned.1.call-start = ((), (), s32[]{:S(2)}) async-start(), calls=%async_computation.1 | async-start | bytes 2359296 | tf_op jit(solution)/shard_map/all_gather | solution.py:89
  13.8 136.0 %all-gather.15.cloned.1.call-start = ((), (), s32[]{:S(2)}) async-start(), calls=%async_computation.3 | async-start | bytes 2359296 | tf_op jit(solution)/shard_map/all_gather | solution.py:90
  14.4 253.6 %reduce-scatter.2.cloned.1.call-start = ((), (), s32[]{:S(2)}) async-start(), calls=%async_computation.5 | async-start | bytes 2621440 | tf_op jit(solution)/shard_map/reduce_scatter | solution.py:175
  149.9 2.5 copy-start.1
  149.9 2.5 copy-start.5
  154.2 2.5 copy-start.1
  154.2 2.5 copy-start.5
  214.5 2.6 copy-start.4
  214.5 2.6 copy-start.6
  219.1 2.6 copy-start.4
  219.1 2.6 copy-start.6
  223.7 3.1 %copy-start.2 = (bf16[2,512,1024]{2,1,0:T(8,128)(2,1)S(1)}, bf16[2,512,1024]{2,1,0:T(8,128)(2,1)}, u32[]{:S(2)}) copy-start(bf16[2,512,1024]{2,1,0:T(8,128)(2,1)} %get-tuple-element.1051) | copy-start | bytes 6291460
  229.4 38.5 %copy-start = (bf16[128,1024]{1,0:T(8,128)(2,1)S(1)}, bf16[128,1024]{1,0:T(8,128)(2,1)}, u32[]{:S(2)}) copy-start(bf16[128,1024]{1,0:T(8,128)(2,1)} %param.7) | copy-start | bytes 786436
Sparse Core Ops, SparseCore 0:
  10.2 19.4 all-gather.12
  31.2 16.7 all-gather.16
  50.7 49.2 all-gather.10
  102.0 47.7 all-gather.14
  229.6 28.7 reduce-scatter.1
where the time goes:
time: 281 us; the launch traced here: 280 us
  blocking collectives  119 us (42%)
  waiting for transfers between devices  108 us (38%)
  matrix products  22.2 us (8%)
  between operations  17.6 us (6%)
  other arithmetic  11.4 us (4%)
    all_gather x1, waiting for transfers between devices, body(): lax.all_gather(unit_rounded, 'dev', axis=0, tiled=True)  52 us
    all_gather x1, waiting for transfers between devices, body(): lax.all_gather(teacher_rounded, 'dev', axis=0, tiled=True)  49.8 us
    psum x1, blocking collectives, body(): lax.psum((jnp.sum(contrast), jnp.sum(relation)), ('grp', 'dev'))  37.2 us
    psum x1, blocking collectives, body(): slab_stats = lax.psum(local_stats, 'dev')  34.6 us
    all_gather x1, blocking collectives, body(): lax.all_gather(labels, 'dev', axis=0, tiled=True)  22.2 us
    all_gather x4, blocking collectives, body(): gathered_stats = lax.all_gather(own_stats, 'grp', axis=0, tiled=True)  20.1 us
    dot_general x8, matrix products, inner_rows(): lax.dot_general(left, right, (((1,), (1,)), ((), ())), preferred_element_...  16.5 us
  transfers between devices with their start and end apart: 5, of which 3 were waited for; matrix products, arithmetic and copies ran while one was open for 1% of the time, Pallas kernels for 0%

commit v1 on v0

v1 whole, which is shorter than its diff:
```python
import functools

import jax
import jax.numpy as jnp
from jax import lax
from jax.experimental import pallas as pl
from jax.experimental.pallas import tpu as pltpu
from jax.sharding import PartitionSpec as P

temp_sup = 0.1
temp_student = 0.2
temp_teacher = 0.05
epsilon = 1e-06

AXES = ("grp", "dev")
PAD = 16
VMEM_LIMIT = 40 * 1024 * 1024


def swapped(value, axis, mask):
    size = lax.axis_size(axis)
    return lax.ppermute(value, axis, [(i, i ^ mask) for i in range(size)])


def bits_of(size):
    return [1 << i for i in range(size.bit_length() - 1)]


def unit_of(raw):
    values = raw.astype(jnp.float32)
    scaling = lax.rsqrt(jnp.sum(values * values, axis=1, keepdims=True) + epsilon)
    return (values * scaling).astype(jnp.bfloat16)


def label_row(block, rows):
    tail = block[rows : rows + PAD, 0:rows].astype(jnp.float32)
    return tail[0:1] * 256.0 + tail[1:2]


def column_of(row):
    rows = row.shape[1]
    return jnp.transpose(jnp.broadcast_to(row, (rows, rows)))


def inner_rows(left, right):
    return lax.dot_general(
        left, right, (((1,), (1,)), ((), ())), preferred_element_type=jnp.float32
    )


def call(kernel, out_shape, operands, smem=0, flops=0, name=None):
    specs = []
    for i, item in enumerate(operands):
        if i < smem:
            specs.append(pl.BlockSpec(memory_space=pltpu.SMEM))
        else:
            specs.append(pl.BlockSpec(memory_space=pltpu.VMEM))
    many = isinstance(out_shape, (tuple, list))
    out_specs = (
        tuple(pl.BlockSpec(memory_space=pltpu.VMEM) for _ in out_shape)
        if many
        else pl.BlockSpec(memory_space=pltpu.VMEM)
    )
    moved = sum(item.size * item.dtype.itemsize for item in operands)
    return pl.pallas_call(
        kernel,
        out_shape=tuple(out_shape) if many else out_shape,
        in_specs=specs,
        out_specs=out_specs,
        name=name,
        cost_estimate=pl.CostEstimate(flops=flops, bytes_accessed=moved, transcendentals=0),
        compiler_params=pltpu.CompilerParams(vmem_limit_bytes=VMEM_LIMIT),
    )(*operands)


def keys_kernel(count, rows, *refs):
    students, teachers = refs[:count], refs[count : 2 * count]
    unit_ref, teacher_ref, label_ref = refs[2 * count :]
    for k in range(count):
        place = slice(k * rows, (k + 1) * rows)
        unit_ref[place, :] = unit_of(students[k][...])
        teacher_ref[place, :] = unit_of(teachers[k][0:rows, :])
        label_ref[place, :] = column_of(label_row(teachers[k], rows))


def tile_kernel(count, rows, width, first, last, *refs):
    ids, unit_ref, teacher_ref, label_ref = refs[:4]
    students, teachers = refs[4:6], refs[6:8]
    rest = refs[8:]
    if not first:
        old_ref, rest = rest[0], rest[1:]
    anchor_ref, similar_ref, weight_ref, anchor_label_ref, stats_ref = rest[:5]
    teacher_units = []
    for n in range(2):
        anchor_ref[n * rows : (n + 1) * rows, :] = unit_of(students[n][...])
        teacher_units.append(unit_of(teachers[n][0:rows, :]))
        anchor_label_ref[:, n * rows : (n + 1) * rows] = jnp.broadcast_to(
            label_row(teachers[n], rows), (8, rows)
        )
    similar_ref[...] = inner_rows(unit_ref[...], anchor_ref[...])
    weight_ref[...] = inner_rows(teacher_ref[...], jnp.concatenate(teacher_units, axis=0))
    row_at = lax.broadcasted_iota(jnp.int32, (rows, rows), 0)
    lane_at = lax.broadcasted_iota(jnp.int32, (rows, rows), 1)
    for k in range(count):
        down = slice(k * rows, (k + 1) * rows)
        totals = [jnp.zeros((rows, rows), jnp.float32)] * 6
        for n in range(2):
            across = slice(n * rows, (n + 1) * rows)
            similar = similar_ref[down, across]
            offset = jnp.where(ids[k] == ids[count + n], 0, rows)
            distinct = row_at != lane_at - offset
            rel_exp = jnp.where(distinct, jnp.exp((similar - 1.0) / temp_student), 0.0)
            weight = jnp.where(
                distinct, jnp.exp((weight_ref[down, across] - 1.0) / temp_teacher), 0.0
            )
            weight_ref[down, across] = weight
            same = label_ref[down, :] == anchor_label_ref[0:1, across]
            positive = jnp.where(jnp.logical_and(same, distinct), 1.0, 0.0)
            terms = (
                rel_exp * rel_exp,
                rel_exp,
                weight,
                weight * similar,
                positive * similar,
                positive,
            )
            totals = [total + term for total, term in zip(totals, terms)]
        stats = jnp.zeros((rows, rows), jnp.float32)
        for i, total in enumerate(totals):
            stats = jnp.where(lane_at == i, jnp.sum(total, axis=1, keepdims=True), stats)
        if not first:
            stats = stats + old_ref[down, :]
        stats_ref[down, :] = stats
        if last:
            rest[5][:, down] = jnp.transpose(stats)[0:8, :]


def merge_kernel(dims, rows, *refs):
    groups, members, keys, pair_places = dims
    place, received_ref, own_ref = refs[:3]
    others = refs[3 : 2 + keys]
    anchor_ref, key_ref, loss_ref = refs[2 + keys :]
    c, p, q, r = place[0], place[1], place[2], place[3]
    quarter = members // 4
    for k in range(keys):
        total = own_ref[:, k * rows : (k + 1) * rows]
        for m, other in enumerate(others):
            at = (k ^ (m + 1)) * rows
            total = total + other[:, at : at + rows]
        positives = jnp.maximum(total[5:6], 1.0)
        if k == 0:
            contrast = (1.0 - total[4:5] / positives) / temp_sup + jnp.log(total[0:1])
            relation = (1.0 - total[3:4] / total[2:3]) / temp_student + jnp.log(total[1:2])
            both = jnp.concatenate([contrast, relation] + [jnp.zeros((6, rows), jnp.float32)], axis=0)
            loss_ref[...] = jnp.broadcast_to(jnp.sum(both, axis=1, keepdims=True), (8, rows))
        factors = jnp.concatenate(
            [
                (1.0 / temp_sup) / total[0:1],
                (1.0 / temp_student) / total[1:2],
                (1.0 / temp_student) / total[2:3],
                (1.0 / temp_sup) / positives,
                jnp.zeros((rows - 4, rows), jnp.float32),
            ],
            axis=0,
        )
        key_ref[k * rows : (k + 1) * rows, :] = jnp.transpose(factors)
    low = lax.broadcasted_iota(jnp.int32, (8, rows), 0)
    for i in range(quarter):
        for dc in range(2):
            total = jnp.zeros((8, rows), jnp.float32)
            for h in range(groups // 2):
                for qq in range(2):
                    source = (h * 2 + (c ^ dc)) * members + (q * 2 + qq) * quarter + (r ^ i)
                    total = total + received_ref[pl.ds(pl.multiple_of(source * 8, 8), 8), :]
            kind = low & 3
            factors = jnp.where(
                kind == 3,
                (1.0 / temp_sup) / jnp.maximum(total, 1.0),
                jnp.where(kind == 0, 1.0 / temp_sup, 1.0 / temp_student) / total,
            )
            turned = jnp.concatenate([factors[4:8], factors[0:4]], axis=0)
            near = jnp.where(p == 0, factors, turned)
            far = jnp.where(p == 0, turned, factors)
            for slot, value in enumerate((near, far)):
                at = ((i * 2 + slot) * 2 + dc) * rows
                anchor_ref[:, at : at + rows] = value


def grad_kernel(pairs, rows, width, k, count, *refs):
    ids, label_ref, key_ref, anchor_stats_ref = refs[:4]
    rest = refs[4:]
    similar, weights, labels, units = (rest[i * pairs : (i + 1) * pairs] for i in range(4))
    out_ref = rest[4 * pairs]
    down = slice(k * rows, (k + 1) * rows)
    row_at = lax.broadcasted_iota(jnp.int32, (rows, rows), 0)
    lane_at = lax.broadcasted_iota(jnp.int32, (rows, rows), 1)
    sup_key, rel_key, teacher_key, pos_key = (key_ref[down, i : i + 1] for i in range(4))
    total = None
    for i in range(pairs):
        row_parts, column_parts = [], []
        for n in range(2):
            across = slice(n * rows, (n + 1) * rows)
            at = (i * 2 + n) * rows
            sup_all, rel_all, teacher_all, pos_all = (
                anchor_stats_ref[j : j + 1, at : at + rows] for j in range(4)
            )
            offset = jnp.where(ids[k] == ids[count + i * 2 + n], 0, rows)
            distinct = row_at != lane_at - offset
            rel_exp = jnp.where(
                distinct, jnp.exp((similar[i][down, across] - 1.0) / temp_student), 0.0
            )
            sup_exp = rel_exp * rel_exp
            weight = weights[i][down, across]
            same = label_ref[down, :] == labels[i][0:1, across]
            positive = jnp.where(jnp.logical_and(same, distinct), 1.0, 0.0)
            row_parts.append(
                (
                    (sup_exp * sup_key - positive * pos_key)
                    + (rel_exp * rel_key - weight * teacher_key)
                ).astype(jnp.bfloat16)
            )
            column_parts.append(
                (
                    (sup_exp * sup_all - positive * pos_all)
                    + (rel_exp * rel_all - weight * teacher_all)
                ).astype(jnp.bfloat16)
            )
        both = jnp.concatenate(
            [jnp.concatenate(row_parts, axis=1), jnp.concatenate(column_parts, axis=1)], axis=0
        )
        part = jnp.dot(both, units[i][...], preferred_element_type=jnp.float32)
        total = part if total is None else total + part
    out_ref[...] = total[0:rows] + total[rows : 2 * rows]


def final_kernel(student_ref, *refs):
    out_ref = refs[-1]
    grad = refs[0][...]
    for ref in refs[1:-1]:
        grad = grad + ref[...]
    values = student_ref[...].astype(jnp.float32)
    scaling = lax.rsqrt(jnp.sum(values * values, axis=1, keepdims=True) + epsilon)
    unit = values * scaling
    along = jnp.sum(unit * grad, axis=1, keepdims=True)
    out_ref[...] = scaling * (grad - unit * along)


def by_xor(value, axis, index):
    for bit in bits_of(value.shape[axis]):
        order = [i ^ bit for i in range(value.shape[axis])]
        turned = jnp.concatenate([lax.slice_in_dim(value, i, i + 1, axis=axis) for i in order], axis=axis)
        value = jnp.where((index & bit) != 0, turned, value)
    return value


def body(student, teacher, labels):
    rows, width = student.shape
    groups, members = lax.axis_size("grp"), lax.axis_size("dev")
    halves, quarter = groups // 2, members // 4
    group, member = lax.axis_index("grp"), lax.axis_index("dev")
    h, c = group // 2, group % 2
    p, q, r = member // (2 * quarter), (member // quarter) % 2, member % quarter
    inner = p != q
    cross = [
        (d, d ^ (3 * quarter)) for d in range(members) if (d // (2 * quarter)) != (d // quarter) % 2
    ]

    digits = jnp.stack([labels // 256, labels % 256]).astype(jnp.bfloat16)
    tail = jnp.pad(digits, ((0, PAD - 2), (0, width - rows)))
    own = (student, jnp.concatenate([teacher, tail], axis=0))

    def both(move, block):
        return tuple(move(part) for part in block)

    near = both(lambda v: swapped(v, "dev", quarter), own)
    crossed = both(lambda v: lax.ppermute(v, "dev", cross), own)
    keys = [own, near]
    for bit in bits_of(halves):
        keys = keys + [both(lambda v: swapped(v, "grp", 2 * bit), item) for item in keys]
    far = both(lambda v: lax.ppermute(v, "dev", cross), near)
    anchors = [
        tuple(jnp.where(inner, a, b) for a, b in zip(crossed, own)),
        tuple(jnp.where(inner, a, b) for a, b in zip(far, near)),
    ]
    for bit in bits_of(quarter):
        anchors = anchors + [both(lambda v: swapped(v, "dev", bit), item) for item in anchors]
    pairs = [(item, both(lambda v: swapped(v, "grp", 1), item)) for item in anchors]

    key_count, pair_count = len(keys), len(pairs)
    key_rows = key_count * rows
    key_ids = [
        ((h ^ (k // 2)) * 2 + c) * members + (p * 2 + (q ^ (k % 2))) * quarter + r
        for k in range(key_count)
    ]
    anchor_ids = [
        (h * 2 + (c ^ dc)) * members + (q * 2 + (p ^ (i % 2))) * quarter + (r ^ (i // 2))
        for i in range(pair_count)
        for dc in range(2)
    ]
    ids = jnp.stack(key_ids + anchor_ids).astype(jnp.int32)
    f32 = functools.partial(jax.ShapeDtypeStruct, dtype=jnp.float32)
    b16 = functools.partial(jax.ShapeDtypeStruct, dtype=jnp.bfloat16)

    key_unit, key_teacher, key_label = call(
        functools.partial(keys_kernel, key_count, rows),
        (b16((key_rows, width)), b16((key_rows, width)), f32((key_rows, rows))),
        [k[0] for k in keys] + [k[1] for k in keys],
        flops=8 * key_rows * width,
        name="keys",
    )
    units, similar, weights, anchor_labels = [], [], [], []
    stats = None
    for i, (first, second) in enumerate(pairs):
        last = i == pair_count - 1
        tile_ids = jnp.concatenate([ids[:key_count], ids[key_count + 2 * i : key_count + 2 * i + 2]])
        outs = call(
            functools.partial(tile_kernel, key_count, rows, width, stats is None, last),
            (
                b16((2 * rows, width)),
                f32((key_rows, 2 * rows)),
                f32((key_rows, 2 * rows)),
                f32((8, 2 * rows)),
                f32((key_rows, rows)),
            )
            + ((f32((8, key_rows)),) if last else ()),
            [tile_ids, key_unit, key_teacher, key_label, first[0], second[0], first[1], second[1]]
            + ([] if stats is None else [stats]),
            smem=1,
            flops=8 * key_rows * rows * width,
            name="tile",
        )
        for held, value in zip((units, similar, weights, anchor_labels), outs[:4]):
            held.append(value)
        stats = outs[4]
    sums = outs[5]

    others = []
    for k in range(1, key_count):
        mask = (k // 2) * 2 * members + (k % 2) * quarter
        total = groups * members
        others.append(lax.ppermute(sums, AXES, [(i, i ^ mask) for i in range(total)]))
    blocks = jnp.stack([sums[0], sums[1], sums[2], sums[5]]).reshape(4, halves, 2, rows)
    blocks = by_xor(by_xor(blocks, 1, h), 2, q).transpose(1, 2, 0, 3).reshape(halves, 1, 8, rows)
    payload = jnp.broadcast_to(blocks, (halves, 2 * members, 8, rows)).reshape(-1, rows)
    received = lax.all_to_all(payload, AXES, 0, 0, tiled=True)
    anchor_stats, key_stats, loss = call(
        functools.partial(merge_kernel, (groups, members, key_count, pair_count), rows),
        (f32((8, members * rows)), f32((key_rows, rows)), f32((8, rows))),
        [jnp.stack([c, p, q, r]).astype(jnp.int32), received, sums] + others,
        smem=1,
        name="merge",
    )

    def grads(k):
        operands = [ids, key_label, key_stats, anchor_stats] + similar + weights + anchor_labels + units
        return call(
            functools.partial(grad_kernel, pair_count, rows, width, k, key_count),
            f32((rows, width)),
            operands,
            smem=1,
            flops=4 * rows * members * rows * width,
            name="grads",
        )

    parts = []
    for k in range(key_count - 1, -1, -1):
        part = grads(k)
        if k:
            mask = (k // 2) * 2 * members + (k % 2) * quarter
            part = lax.ppermute(part, AXES, [(i, i ^ mask) for i in range(groups * members)])
        parts.append(part)
    shared = lax.all_to_all(
        jnp.broadcast_to(loss[None], (groups * members, 8, rows)).reshape(-1, rows), AXES, 0, 0, tiled=True
    ).reshape(groups * members, 8, rows)
    losses = jnp.sum(shared[:, 0:2, 0], axis=0) / (groups * members * rows)
    feature_grad = call(
        final_kernel, f32((rows, width)), [student] + parts[::-1], flops=8 * rows * width, name="final"
    )
    return (losses[0], losses[1], feature_grad)


def solution(mesh):
    placed = (P(AXES, None), P(AXES, None), P(AXES))
    return jax.shard_map(
        body,
        mesh=mesh,
        in_specs=placed,
        out_specs=(P(), P(), P(AXES, None)),
        check_vma=False,
    )
```

time: 281 us -> 147 us (0.52)
  blocking collectives: 119 us -> 0 us
  waiting for transfers between devices: 108 us -> 38.6 us
  starting transfers between devices: 0.2 us -> 45.6 us
  local copies, waits for them, and re-layouts: 1.22 us -> 35.1 us
  matrix products: 22.2 us -> 0 us
  Pallas kernels: 0 us -> 22.1 us
  between operations: 17.6 us -> 1.05 us
  other arithmetic: 11.4 us -> 3.6 us
    all_gather x4 -> x0, waiting for transfers between devices: 107 us -> none  [the longest x1 52 us: body(): lax.all_gather(unit_rounded, 'dev', axis=0, tiled=True)]
    psum x2 -> x0, blocking collectives: 71.8 us -> none  [the longest x1 37.2 us: body(): lax.psum((jnp.sum(contrast), jnp.sum(relation)), ('grp', 'dev'))]
    all_gather x6 -> x0, blocking collectives: 47.3 us -> none  [the longest x1 22.2 us: body(): lax.all_gather(labels, 'dev', axis=0, tiled=True)]
    ppermute x0 -> x28, waiting for transfers between devices: none -> 38.6 us  [the longest x3 19.4 us: body(): lax.ppermute(part, AXES, [(i, i ^ mask) for i in range(groups * members)])]
    unnamed x12 -> x98, local copies, waits for them, and re-layouts: 0.03 us -> 31.1 us
    ppermute x0 -> x28, starting transfers between devices: none -> 29.1 us  [the longest x18 19.3 us: swapped(): return lax.ppermute(value, axis, [(i, i ^ mask) for i in range(size)])]
    dot_general x10 -> x0, matrix products: 22.2 us -> none  [the longest x8 16.5 us: inner_rows(): lax.dot_general(left, right, (((1,), (1,)), ((), ())), preferred_element_...]
    pallas_call x0 -> x11, Pallas kernels: none -> 22.1 us  [call(): pl.pallas_call(kernel, out_shape=tuple(out_shape) if many else out_shape,...]
  transfers between devices with their start and end apart: 5 -> 30, of which waited for: 3 -> 11; matrix products, arithmetic and copies ran while one was open for 1% -> 3% of each run, Pallas kernels for 0% -> 11%
where the time goes in v1:
time: 147 us; the launch traced here: 146 us
  starting transfers between devices  45.6 us (31%)
  waiting for transfers between devices  38.6 us (26%)
  local copies, waits for them, and re-layouts  35.1 us (24%)
  Pallas kernels  22.1 us (15%)
  other arithmetic  3.6 us (2%)
    unnamed x98, local copies, waits for them, and re-layouts  31.1 us
    pallas_call x11, Pallas kernels, call(): pl.pallas_call(kernel, out_shape=tuple(out_shape) if many else out_shape,...  22.1 us
    ppermute x3, waiting for transfers between devices, body(): lax.ppermute(part, AXES, [(i, i ^ mask) for i in range(groups * members)])  19.4 us
    ppermute x18, starting transfers between devices, swapped(): return lax.ppermute(value, axis, [(i, i ^ mask) for i in range(size)])  19.3 us
    ppermute x18, waiting for transfers between devices, swapped(): return lax.ppermute(value, axis, [(i, i ^ mask) for i in range(size)])  17.2 us
    all_to_all x1, starting transfers between devices, body(): received = lax.all_to_all(payload, AXES, 0, 0, tiled=True)  11.7 us
    all_to_all x1, starting transfers between devices, body(): lax.all_to_all(jnp.broadcast_to(loss[None], (groups * members, 8, rows))....  4.86 us
    ppermute x3, starting transfers between devices, body(): lax.ppermute(sums, AXES, [(i, i ^ mask) for i in range(total)])  3.55 us
  transfers between devices with their start and end apart: 30, of which 11 were waited for; matrix products, arithmetic and copies ran while one was open for 3% of the time, Pallas kernels for 11%

profile of v1, /device:TPU:0, one launch (start us, length us, event | category | flops | bytes accessed | tf_op | source)
XLA Modules:
  0.0 146.1 jit_solution(13753262199578410293)
XLA Ops:
  1.3 1.0 pad_maximum_fusion.refs_4_
  2.3 3.1 %collective-permute-start.3 = (bf16[144,1024]{1,0:T(8,128)(2,1)S(1)}, bf16[144,1024]{1,0:T(8,128)(2,1)S(1)}, u32[]{:S(2)}, u32[]{:S(2)}) collective-permute-start(bf16[144,1024]{1,0:T(8,128)(2,1)S(1)} %pad_maximum_fusion.refs_4_), channel_id=1, source_target_pairs={{0,2},{1,3},{2,0},{3,1},{4,6},{5,7},{6,4},{7,5},{8,10},{9,11},{10,... | collective-permute-start | bytes 884744 | tf_op jit(solution)/shard_map/ppermute | solution.py:22
  6.8 1.6 %collective-permute-start.1 = (bf16[128,1024]{1,0:T(8,128)(2,1)S(1)}, bf16[128,1024]{1,0:T(8,128)(2,1)S(1)}, u32[]{:S(2)}, u32[]{:S(2)}) collective-permute-start(bf16[128,1024]{1,0:T(8,128)(2,1)S(1)} %copy-done.14), channel_id=1, source_target_pairs={{0,16},{8,24},{16,0},{24,8},{1,17},{9,25},{17,1},{25,9},{2,18},{10... | collective-permute-start | bytes 786440 | tf_op jit(solution)/shard_map/ppermute | solution.py:22
  8.3 5.6 %collective-permute-start = (bf16[128,1024]{1,0:T(8,128)(2,1)S(1)}, bf16[128,1024]{1,0:T(8,128)(2,1)S(1)}, u32[]{:S(2)}, u32[]{:S(2)}) collective-permute-start(bf16[128,1024]{1,0:T(8,128)(2,1)S(1)} %copy-done.14), channel_id=1, source_target_pairs={{0,2},{1,3},{2,0},{3,1},{4,6},{5,7},{6,4},{7,5},{8,10},{9,11},{10,... | collective-permute-start | bytes 786440 | tf_op jit(solution)/shard_map/ppermute | solution.py:22
  15.3 4.1 %collective-permute-done.refs_1_ = bf16[128,1024]{1,0:T(8,128)(2,1)S(1)} collective-permute-done((bf16[128,1024]{1,0:T(8,128)(2,1)S(1)}, bf16[128,1024]{1,0:T(8,128)(2,1)S(1)}, u32[]{:S(2)}, u32[]{:S(2)}) %collective-permute-start) | collective-permute-done | bytes 262176 | tf_op jit(solution)/shard_map/ppermute | solution.py:22
  19.4 1.5 %collective-permute-start.13 = (bf16[128,1024]{1,0:T(8,128)(2,1)S(1)}, bf16[128,1024]{1,0:T(8,128)(2,1)}, u32[]{:S(2)}, u32[]{:S(2)}) collective-permute-start(bf16[128,1024]{1,0:T(8,128)(2,1)S(1)} %broadcast_select_fusion.2.refs_4_), channel_id=1, source_target_pairs={{0,1},{1,0},{2,3},{3,2},{4,5},{5,4},{6,7},{7,6},{8,9},{9,8},{10,11... | collective-permute-start | bytes 786440 | tf_op jit(solution)/shard_map/ppermute | solution.py:22
  23.2 1.5 %collective-permute-start.16 = (bf16[144,1024]{1,0:T(8,128)(2,1)S(1)}, bf16[144,1024]{1,0:T(8,128)(2,1)}, u32[]{:S(2)}, u32[]{:S(2)}) collective-permute-start(bf16[144,1024]{1,0:T(8,128)(2,1)S(1)} %broadcast_select_fusion.refs_6_), channel_id=1, source_target_pairs={{0,1},{1,0},{2,3},{3,2},{4,5},{5,4},{6,7},{7,6},{8,9},{9,8},{10,11... | collective-permute-start | bytes 884744 | tf_op jit(solution)/shard_map/ppermute | solution.py:22
  24.8 1.3 collective-permute-done.13.refs_4_
  26.6 1.5 %collective-permute-start.10 = (bf16[144,1024]{1,0:T(8,128)(2,1)S(1)}, bf16[144,1024]{1,0:T(8,128)(2,1)}, u32[]{:S(2)}, u32[]{:S(2)}) collective-permute-start(bf16[144,1024]{1,0:T(8,128)(2,1)S(1)} %broadcast_select_fusion.1.refs_6_), channel_id=1, source_target_pairs={{0,1},{1,0},{2,3},{3,2},{4,5},{5,4},{6,7},{7,6},{8,9},{9,8},{10,11... | collective-permute-start | bytes 884744 | tf_op jit(solution)/shard_map/ppermute | solution.py:22
  29.4 2.2 %collective-permute-start.7 = (bf16[128,1024]{1,0:T(8,128)(2,1)S(1)}, bf16[128,1024]{1,0:T(8,128)(2,1)}, u32[]{:S(2)}, u32[]{:S(2)}) collective-permute-start(bf16[128,1024]{1,0:T(8,128)(2,1)S(1)} %broadcast_select_fusion.3.refs_4_), channel_id=1, source_target_pairs={{0,1},{1,0},{2,3},{3,2},{4,5},{5,4},{6,7},{7,6},{8,9},{9,8},{10,11... | collective-permute-start | bytes 786440 | tf_op jit(solution)/shard_map/ppermute | solution.py:22
  31.6 1.6 %collective-permute-done.16.refs_6_ = bf16[144,1024]{1,0:T(8,128)(2,1)} collective-permute-done((bf16[144,1024]{1,0:T(8,128)(2,1)S(1)}, bf16[144,1024]{1,0:T(8,128)(2,1)}, u32[]{:S(2)}, u32[]{:S(2)}) %collective-permute-start.16) | collective-permute-done | bytes 294944 | tf_op jit(solution)/shard_map/ppermute | solution.py:22
  33.2 1.3 collective-permute-done.5.refs_7_
  36.4 3.0 %collective-permute-done.10.refs_6_ = bf16[144,1024]{1,0:T(8,128)(2,1)} collective-permute-done((bf16[144,1024]{1,0:T(8,128)(2,1)S(1)}, bf16[144,1024]{1,0:T(8,128)(2,1)}, u32[]{:S(2)}, u32[]{:S(2)}) %collective-permute-start.10) | collective-permute-done | bytes 294944 | tf_op jit(solution)/shard_map/ppermute | solution.py:22
  39.5 5.2 %collective-permute-done.7.refs_4_ = bf16[128,1024]{1,0:T(8,128)(2,1)} collective-permute-done((bf16[128,1024]{1,0:T(8,128)(2,1)S(1)}, bf16[128,1024]{1,0:T(8,128)(2,1)}, u32[]{:S(2)}, u32[]{:S(2)}) %collective-permute-start.7) | collective-permute-done | bytes 262176 | tf_op jit(solution)/shard_map/ppermute | solution.py:22
  46.7 1.0 copy-done.25
  47.7 0.9 copy-done.29
  49.6 1.9 %tile.4 = (bf16[256,1024]{1,0:T(8,128)(2,1)S(1)}, f32[512,256]{1,0:T(8,128)S(1)}, f32[512,256]{1,0:T(8,128)S(1)}, f32[8,256]{1,0:T(8,128)S(1)}, f32[512,128]{1,0:T(8,128)S(1)}) custom-call(s32[6]{0:T(128)S(1)} %concatenate.37.refs_0_, bf16[512,1024]{1,0:T(8,128)(2,1)S(1)} %get-tuple-element.29.refs_1_, bf16[512,1024]{1,0:T(8,128)(2,1)S(1)} %get-tuple-element.30.refs_2_, ...), custom_call_target="tpu_custom_call" | custom-call | flops 536870912 | bytes 3473432 | tf_op jit(solution)/shard_map/tile/pallas_call | solution.py:65
  52.1 2.3 %tile.5 = (bf16[256,1024]{1,0:T(8,128)(2,1)S(1)}, f32[512,256]{1,0:T(8,128)S(1)}, f32[512,256]{1,0:T(8,128)S(1)}, f32[8,256]{1,0:T(8,128)S(1)}, f32[512,128]{1,0:T(8,128)S(1)}) custom-call(s32[6]{0:T(128)S(1)} %copy-done.47, bf16[512,1024]{1,0:T(8,128)(2,1)S(1)} %get-tuple-element.29.refs_1_, bf16[512,1024]{1,0:T(8,128)(2,1)S(1)} %get-tuple-element.30.refs_2_, ...), custom_call_target="tpu_custom_call" | custom-call | flops 536870912 | bytes 3735576 | tf_op jit(solution)/shard_map/tile/pallas_call | solution.py:65
  55.0 2.6 %tile.6 = (bf16[256,1024]{1,0:T(8,128)(2,1)S(1)}, f32[512,256]{1,0:T(8,128)S(1)}, f32[512,256]{1,0:T(8,128)S(1)}, f32[8,256]{1,0:T(8,128)S(1)}, f32[512,128]{1,0:T(8,128)S(1)}) custom-call(s32[6]{0:T(128)S(1)} %copy-done.46, bf16[512,1024]{1,0:T(8,128)(2,1)S(1)} %get-tuple-element.29.refs_1_, bf16[512,1024]{1,0:T(8,128)(2,1)S(1)} %get-tuple-element.30.refs_2_, ...), custom_call_target="tpu_custom_call" | custom-call | flops 536870912 | bytes 3735576 | tf_op jit(solution)/shard_map/tile/pallas_call | solution.py:65
  57.7 0.8 copy-done
  61.3 3.4 %tile.7 = (bf16[256,1024]{1,0:T(8,128)(2,1)S(1)}, f32[512,256]{1,0:T(8,128)S(1)}, f32[512,256]{1,0:T(8,128)S(1)}, f32[8,256]{1,0:T(8,128)S(1)}, f32[512,128]{1,0:T(8,128)}, /*index=5*/f32[8,512]{1,0:T(8,128)S(1)}) custom-call(s32[6]{0:T(128)S(1)} %copy-done.45, bf16[512,1024]{1,0:T(8,128)(2,1)S(1)} %get-tuple-element.29.refs_1_, ...), custom_call_target="tpu_custom_call" | custom-call | flops 536870912 | bytes 3735576 | tf_op jit(solution)/shard_map/tile/pallas_call | solution.py:65
  64.7 0.8 copy-done.6
  65.5 0.8 copy-done.8
  66.3 0.8 copy-done.10
  68.4 11.7 %all-to-all-start = ((f32[32,8,128]{2,1,0:T(8,128)}), f32[32,8,128]{2,1,0:T(8,128)S(1)}, u32[]{:S(2)}, u32[]{:S(2)}) async-start(f32[32,8,128]{2,1,0:T(8,128)} %bitcast.29), calls=%async_computation | async-start | bytes 262144 | tf_op jit(solution)/shard_map/all_to_all | solution.py:345
  80.1 2.7 %collective-permute-start.24 = (f32[8,512]{1,0:T(8,128)}, f32[8,512]{1,0:T(8,128)S(1)}, u32[]{:S(2)}, u32[]{:S(2)}) collective-permute-start(f32[8,512]{1,0:T(8,128)} %copy-done.36), channel_id=1, source_target_pairs={{0,18},{1,19},{2,16},{3,17},{4,22},{5,23},{6,20},{7,21},{8,26},{9,... | collective-permute-start | bytes 49160 | tf_op jit(solution)/shard_map/ppermute | solution.py:341
  85.7 1.3 collective-permute-done.23.refs_4_
  89.5 0.9 copy-done.23
  95.4 4.9 %all-to-all-start.1 = ((f32[32,8,128]{2,1,0:T(8,128)}), f32[32,8,128]{2,1,0:T(8,128)}, u32[]{:S(2)}, u32[]{:S(2)}) async-start(f32[32,8,128]{2,1,0:T(8,128)} %broadcast_in_dim.15), calls=%async_computation.1 | async-start | bytes 262144 | tf_op jit(solution)/shard_map/all_to_all | solution.py:372
  101.0 1.0 copy-done.1
  102.1 1.0 copy-done.3
  103.1 1.0 copy-done.5
  104.2 1.0 copy-done.7
  105.2 1.0 copy-done.9
  106.2 1.0 copy-done.11
  107.3 0.9 copy-done.13
  108.2 2.2 %grads.7 = f32[128,1024]{1,0:T(8,128)} custom-call(s32[12]{0:T(128)S(1)} %stack.91.refs_0_, f32[512,128]{1,0:T(8,128)S(1)} %get-tuple-element.31.refs_3_.refs_1_, f32[512,128]{1,0:T(8,128)S(1)} %copy-done.13, f32[8,1024]{1,0:T(8,128)S(1)} %get-tuple-element.38.refs_3_, f32[512,256]{1,0:T(8,128)S(1)} %get-tuple-element.39.refs_4_, ...), custom_call_target="tpu_custom_call" | custom-call | flops 536870912 | bytes 6881328 | tf_op jit(solution)/shard_map/grads/pallas_call | solution.py:65
  110.5 2.2 %grads.6 = f32[128,1024]{1,0:T(8,128)} custom-call(s32[12]{0:T(128)S(1)} %stack.91.refs_0_, f32[512,128]{1,0:T(8,128)S(1)} %get-tuple-element.31.refs_3_.refs_1_, f32[512,128]{1,0:T(8,128)S(1)} %copy-done.13, f32[8,1024]{1,0:T(8,128)S(1)} %get-tuple-element.38.refs_3_, f32[512,256]{1,0:T(8,128)S(1)} %get-tuple-element.39.refs_4_, ...), custom_call_target="tpu_custom_call" | custom-call | flops 536870912 | bytes 6881328 | tf_op jit(solution)/shard_map/grads/pallas_call | solution.py:65
  112.7 2.2 %grads.5 = f32[128,1024]{1,0:T(8,128)} custom-call(s32[12]{0:T(128)S(1)} %stack.91.refs_0_, f32[512,128]{1,0:T(8,128)S(1)} %get-tuple-element.31.refs_3_.refs_1_, f32[512,128]{1,0:T(8,128)S(1)} %copy-done.13, f32[8,1024]{1,0:T(8,128)S(1)} %get-tuple-element.38.refs_3_, f32[512,256]{1,0:T(8,128)S(1)} %get-tuple-element.39.refs_4_, ...), custom_call_target="tpu_custom_call" | custom-call | flops 536870912 | bytes 6881328 | tf_op jit(solution)/shard_map/grads/pallas_call | solution.py:65
  114.9 1.5 %collective-permute-start.25 = (f32[128,1024]{1,0:T(8,128)}, f32[128,1024]{1,0:T(8,128)}, u32[]{:S(2)}, u32[]{:S(2)}) collective-permute-start(f32[128,1024]{1,0:T(8,128)} %grads.5), channel_id=1, source_target_pairs={{0,2},{1,3},{2,0},{3,1},{4,6},{5,7},{6,4},{7,5},{8,10},{9,11},{10,... | collective-permute-start | bytes 1572872 | tf_op jit(solution)/shard_map/ppermute | solution.py:370
  116.4 1.5 %collective-permute-start.26 = (f32[128,1024]{1,0:T(8,128)}, f32[128,1024]{1,0:T(8,128)}, u32[]{:S(2)}, u32[]{:S(2)}) collective-permute-start(f32[128,1024]{1,0:T(8,128)} %grads.6), channel_id=1, source_target_pairs={{0,16},{1,17},{2,18},{3,19},{4,20},{5,21},{6,22},{7,23},{8,24},{9,... | collective-permute-start | bytes 1572872 | tf_op jit(solution)/shard_map/ppermute | solution.py:370
  118.4 1.4 grads.4.refs_0_
  120.6 1.1 slice_reduce_fusion
  122.3 7.7 %collective-permute-done.25.refs_1_ = f32[128,1024]{1,0:T(8,128)} collective-permute-done((f32[128,1024]{1,0:T(8,128)}, f32[128,1024]{1,0:T(8,128)}, u32[]{:S(2)}, u32[]{:S(2)}) %collective-permute-start.25) | collective-permute-done | bytes 524320 | tf_op jit(solution)/shard_map/ppermute | solution.py:370
  130.0 11.7 %collective-permute-done.26.refs_2_ = f32[128,1024]{1,0:T(8,128)} collective-permute-done((f32[128,1024]{1,0:T(8,128)}, f32[128,1024]{1,0:T(8,128)}, u32[]{:S(2)}, u32[]{:S(2)}) %collective-permute-start.26) | collective-permute-done | bytes 524320 | tf_op jit(solution)/shard_map/ppermute | solution.py:370
  141.7 0.9 copy-done.15
  142.6 1.0 copy-done.17
  143.7 2.4 %final.1 = f32[128,1024]{1,0:T(8,128)} custom-call(bf16[128,1024]{1,0:T(8,128)(2,1)S(1)} %copy-done.15, f32[128,1024]{1,0:T(8,128)S(1)} %copy-done.17, f32[128,1024]{1,0:T(8,128)} %collective-permute-done.25.refs_1_, f32[128,1024]{1,0:T(8,128)} %collective-permute-done.26.refs_2_, f32[128,1024]{1,0:T(8,128)} %collective-permute-done.27.refs_3_), custom_call_target="tpu_custom_call" | custom-call | flops 1048576 | bytes 2359296 | tf_op jit(solution)/shard_map/final/pallas_call | solution.py:65
  (146 shorter events, 30.5 us)
Async XLA Ops:
  1.3 4.1 %copy-start.14 = (bf16[128,1024]{1,0:T(8,128)(2,1)S(1)}, bf16[128,1024]{1,0:T(8,128)(2,1)}, u32[]{:S(2)}) copy-start(bf16[128,1024]{1,0:T(8,128)(2,1)} %student_ref.1) | copy-start | bytes 786436
  2.3 12.2 %collective-permute-start.3 = (bf16[144,1024]{1,0:T(8,128)(2,1)S(1)}, bf16[144,1024]{1,0:T(8,128)(2,1)S(1)}, u32[]{:S(2)}, u32[]{:S(2)}) collective-permute-start(bf16[144,1024]{1,0:T(8,128)(2,1)S(1)} %pad_maximum_fusion.refs_4_), channel_id=1, source_target_pairs={{0,2},{1,3},{2,0},{3,1},{4,6},{5,7},{6,4},{7,5},{8,10},{9,11},{10,... | collective-permute-start | bytes 884744 | tf_op jit(solution)/shard_map/ppermute | solution.py:22
  5.4 8.5 %collective-permute-start.12 = (bf16[128,1024]{1,0:T(8,128)(2,1)S(1)}, bf16[128,1024]{1,0:T(8,128)(2,1)S(1)}, u32[]{:S(2)}, u32[]{:S(2)}) collective-permute-start(bf16[128,1024]{1,0:T(8,128)(2,1)S(1)} %copy-done.14), channel_id=1, source_target_pairs={{2,4},{3,5},{4,2},{5,3},{10,12},{11,13},{12,10},{13,11},{18,20},{1... | collective-permute-start | bytes 786440 | tf_op jit(solution)/shard_map/ppermute | solution.py:276
  6.1 14.9 %collective-permute-start.15 = (bf16[144,1024]{1,0:T(8,128)(2,1)S(1)}, bf16[144,1024]{1,0:T(8,128)(2,1)S(1)}, u32[]{:S(2)}, u32[]{:S(2)}) collective-permute-start(bf16[144,1024]{1,0:T(8,128)(2,1)S(1)} %pad_maximum_fusion.refs_4_), channel_id=1, source_target_pairs={{2,4},{3,5},{4,2},{5,3},{10,12},{11,13},{12,10},{13,11},{18,20},{1... | collective-permute-start | bytes 884744 | tf_op jit(solution)/shard_map/ppermute | solution.py:276
  6.8 8.4 %collective-permute-start.1 = (bf16[128,1024]{1,0:T(8,128)(2,1)S(1)}, bf16[128,1024]{1,0:T(8,128)(2,1)S(1)}, u32[]{:S(2)}, u32[]{:S(2)}) collective-permute-start(bf16[128,1024]{1,0:T(8,128)(2,1)S(1)} %copy-done.14), channel_id=1, source_target_pairs={{0,16},{8,24},{16,0},{24,8},{1,17},{9,25},{17,1},{25,9},{2,18},{10... | collective-permute-start | bytes 786440 | tf_op jit(solution)/shard_map/ppermute | solution.py:22
  8.3 11.1 %collective-permute-start = (bf16[128,1024]{1,0:T(8,128)(2,1)S(1)}, bf16[128,1024]{1,0:T(8,128)(2,1)S(1)}, u32[]{:S(2)}, u32[]{:S(2)}) collective-permute-start(bf16[128,1024]{1,0:T(8,128)(2,1)S(1)} %copy-done.14), channel_id=1, source_target_pairs={{0,2},{1,3},{2,0},{3,1},{4,6},{5,7},{6,4},{7,5},{8,10},{9,11},{10,... | collective-permute-start | bytes 786440 | tf_op jit(solution)/shard_map/ppermute | solution.py:22
  14.0 7.7 %copy-start.48 = (bf16[128,1024]{1,0:T(8,128)(2,1)S(1)}, bf16[128,1024]{1,0:T(8,128)(2,1)}, u32[]{:S(2)}) copy-start(bf16[128,1024]{1,0:T(8,128)(2,1)} %param.4) | copy-start | bytes 786436
  14.0 7.8 %collective-permute-start.4 = (bf16[144,1024]{1,0:T(8,128)(2,1)S(1)}, bf16[144,1024]{1,0:T(8,128)(2,1)S(1)}, u32[]{:S(2)}, u32[]{:S(2)}) collective-permute-start(bf16[144,1024]{1,0:T(8,128)(2,1)S(1)} %pad_maximum_fusion.refs_4_), channel_id=1, source_target_pairs={{0,16},{8,24},{16,0},{24,8},{1,17},{9,25},{17,1},{25,9},{2,18},{10... | collective-permute-start | bytes 884744 | tf_op jit(solution)/shard_map/ppermute | solution.py:22
  14.5 7.9 %collective-permute-start.9 = (bf16[144,1024]{1,0:T(8,128)(2,1)S(1)}, bf16[144,1024]{1,0:T(8,128)(2,1)S(1)}, u32[]{:S(2)}, u32[]{:S(2)}) collective-permute-start(bf16[144,1024]{1,0:T(8,128)(2,1)S(1)} %collective-permute-done.3.refs_5_), channel_id=1, source_target_pairs={{2,4},{3,5},{4,2},{5,3},{10,12},{11,13},{12,10},{13,11},{18,20},{1... | collective-permute-start | bytes 884744 | tf_op jit(solution)/shard_map/ppermute | solution.py:280
  15.2 7.2 %collective-permute-start.20 = (bf16[128,1024]{1,0:T(8,128)(2,1)S(1)}, bf16[128,1024]{1,0:T(8,128)(2,1)S(1)}, u32[]{:S(2)}, u32[]{:S(2)}) collective-permute-start(bf16[128,1024]{1,0:T(8,128)(2,1)S(1)} %broadcast_select_fusion.2.refs_4_), channel_id=1, source_target_pairs={{0,8},{8,0},{16,24},{24,16},{1,9},{9,1},{17,25},{25,17},{2,10},{10... | collective-permute-start | bytes 786440 | tf_op jit(solution)/shard_map/ppermute | solution.py:22
  19.4 6.7 %collective-permute-start.13 = (bf16[128,1024]{1,0:T(8,128)(2,1)S(1)}, bf16[128,1024]{1,0:T(8,128)(2,1)}, u32[]{:S(2)}, u32[]{:S(2)}) collective-permute-start(bf16[128,1024]{1,0:T(8,128)(2,1)S(1)} %broadcast_select_fusion.2.refs_4_), channel_id=1, source_target_pairs={{0,1},{1,0},{2,3},{3,2},{4,5},{5,4},{6,7},{7,6},{8,9},{9,8},{10,11... | collective-permute-start | bytes 786440 | tf_op jit(solution)/shard_map/ppermute | solution.py:22
  21.0 5.7 %collective-permute-start.6 = (bf16[128,1024]{1,0:T(8,128)(2,1)S(1)}, bf16[128,1024]{1,0:T(8,128)(2,1)S(1)}, u32[]{:S(2)}, u32[]{:S(2)}) collective-permute-start(bf16[128,1024]{1,0:T(8,128)(2,1)S(1)} %collective-permute-done.refs_1_), channel_id=1, source_target_pairs={{2,4},{3,5},{4,2},{5,3},{10,12},{11,13},{12,10},{13,11},{18,20},{1... | collective-permute-start | bytes 786440 | tf_op jit(solution)/shard_map/ppermute | solution.py:280
  21.7 7.0 %collective-permute-start.2 = (bf16[128,1024]{1,0:T(8,128)(2,1)S(1)}, bf16[128,1024]{1,0:T(8,128)(2,1)S(1)}, u32[]{:S(2)}, u32[]{:S(2)}) collective-permute-start(bf16[128,1024]{1,0:T(8,128)(2,1)S(1)} %collective-permute-done.refs_1_), channel_id=1, source_target_pairs={{0,16},{8,24},{16,0},{24,8},{1,17},{9,25},{17,1},{25,9},{2,18},{10... | collective-permute-start | bytes 786440 | tf_op jit(solution)/shard_map/ppermute | solution.py:22
  22.4 7.0 %collective-permute-start.21 = (bf16[144,1024]{1,0:T(8,128)(2,1)S(1)}, bf16[144,1024]{1,0:T(8,128)(2,1)S(1)}, u32[]{:S(2)}, u32[]{:S(2)}) collective-permute-start(bf16[144,1024]{1,0:T(8,128)(2,1)S(1)} %broadcast_select_fusion.refs_6_), channel_id=1, source_target_pairs={{0,8},{8,0},{16,24},{24,16},{1,9},{9,1},{17,25},{25,17},{2,10},{10... | collective-permute-start | bytes 884744 | tf_op jit(solution)/shard_map/ppermute | solution.py:22
  22.5 10.7 %copy-start.18 = (bf16[144,1024]{1,0:T(8,128)(2,1)}, bf16[144,1024]{1,0:T(8,128)(2,1)S(1)}, u32[]{:S(2)}) copy-start(bf16[144,1024]{1,0:T(8,128)(2,1)S(1)} %broadcast_select_fusion.1.refs_6_) | copy-start | bytes 884740
  23.2 9.9 %collective-permute-start.16 = (bf16[144,1024]{1,0:T(8,128)(2,1)S(1)}, bf16[144,1024]{1,0:T(8,128)(2,1)}, u32[]{:S(2)}, u32[]{:S(2)}) collective-permute-start(bf16[144,1024]{1,0:T(8,128)(2,1)S(1)} %broadcast_select_fusion.refs_6_), channel_id=1, source_target_pairs={{0,1},{1,0},{2,3},{3,2},{4,5},{5,4},{6,7},{7,6},{8,9},{9,8},{10,11... | collective-permute-start | bytes 884744 | tf_op jit(solution)/shard_map/ppermute | solution.py:22
  26.1 8.4 %collective-permute-start.5 = (bf16[144,1024]{1,0:T(8,128)(2,1)S(1)}, bf16[144,1024]{1,0:T(8,128)(2,1)S(1)}, u32[]{:S(2)}, u32[]{:S(2)}) collective-permute-start(bf16[144,1024]{1,0:T(8,128)(2,1)S(1)} %collective-permute-done.3.refs_5_), channel_id=1, source_target_pairs={{0,16},{8,24},{16,0},{24,8},{1,17},{9,25},{17,1},{25,9},{2,18},{10... | collective-permute-start | bytes 884744 | tf_op jit(solution)/shard_map/ppermute | solution.py:22
  26.6 12.8 %collective-permute-start.10 = (bf16[144,1024]{1,0:T(8,128)(2,1)S(1)}, bf16[144,1024]{1,0:T(8,128)(2,1)}, u32[]{:S(2)}, u32[]{:S(2)}) collective-permute-start(bf16[144,1024]{1,0:T(8,128)(2,1)S(1)} %broadcast_select_fusion.1.refs_6_), channel_id=1, source_target_pairs={{0,1},{1,0},{2,3},{3,2},{4,5},{5,4},{6,7},{7,6},{8,9},{9,8},{10,11... | collective-permute-start | bytes 884744 | tf_op jit(solution)/shard_map/ppermute | solution.py:22
  28.2 21.1 %copy-start.20 = (bf16[128,1024]{1,0:T(8,128)(2,1)}, bf16[128,1024]{1,0:T(8,128)(2,1)S(1)}, u32[]{:S(2)}) copy-start(bf16[128,1024]{1,0:T(8,128)(2,1)S(1)} %broadcast_select_fusion.3.refs_4_) | copy-start | bytes 786436
  29.4 5.8 %collective-permute-start.18 = (bf16[128,1024]{1,0:T(8,128)(2,1)S(1)}, bf16[128,1024]{1,0:T(8,128)(2,1)S(1)}, u32[]{:S(2)}, u32[]{:S(2)}) collective-permute-start(bf16[128,1024]{1,0:T(8,128)(2,1)S(1)} %broadcast_select_fusion.3.refs_4_), channel_id=1, source_target_pairs={{0,8},{8,0},{16,24},{24,16},{1,9},{9,1},{17,25},{25,17},{2,10},{10... | collective-permute-start | bytes 786440 | tf_op jit(solution)/shard_map/ppermute | solution.py:22
  29.4 15.3 %collective-permute-start.7 = (bf16[128,1024]{1,0:T(8,128)(2,1)S(1)}, bf16[128,1024]{1,0:T(8,128)(2,1)}, u32[]{:S(2)}, u32[]{:S(2)}) collective-permute-start(bf16[128,1024]{1,0:T(8,128)(2,1)S(1)} %broadcast_select_fusion.3.refs_4_), channel_id=1, source_target_pairs={{0,1},{1,0},{2,3},{3,2},{4,5},{5,4},{6,7},{7,6},{8,9},{9,8},{10,11... | collective-permute-start | bytes 786440 | tf_op jit(solution)/shard_map/ppermute | solution.py:22
  33.2 18.3 %collective-permute-start.19 = (bf16[144,1024]{1,0:T(8,128)(2,1)S(1)}, bf16[144,1024]{1,0:T(8,128)(2,1)}, u32[]{:S(2)}, u32[]{:S(2)}) collective-permute-start(bf16[144,1024]{1,0:T(8,128)(2,1)S(1)} %broadcast_select_fusion.1.refs_6_), channel_id=1, source_target_pairs={{0,8},{8,0},{16,24},{24,16},{1,9},{9,1},{17,25},{25,17},{2,10},{10... | collective-permute-start | bytes 884744 | tf_op jit(solution)/shard_map/ppermute | solution.py:22
  35.2 19.2 %collective-permute-start.17 = (bf16[144,1024]{1,0:T(8,128)(2,1)}, bf16[144,1024]{1,0:T(8,128)(2,1)}, u32[]{:S(2)}, u32[]{:S(2)}) collective-permute-start(bf16[144,1024]{1,0:T(8,128)(2,1)} %collective-permute-done.16.refs_6_), channel_id=1, source_target_pairs={{0,8},{8,0},{16,24},{24,16},{1,9},{9,1},{17,25},{25,17},{2,10},{10... | collective-permute-start | bytes 884744 | tf_op jit(solution)/shard_map/ppermute | solution.py:22
  35.9 18.5 %collective-permute-start.14 = (bf16[128,1024]{1,0:T(8,128)(2,1)}, bf16[128,1024]{1,0:T(8,128)(2,1)}, u32[]{:S(2)}, u32[]{:S(2)}) collective-permute-start(bf16[128,1024]{1,0:T(8,128)(2,1)} %collective-permute-done.13.refs_4_), channel_id=1, source_target_pairs={{0,8},{8,0},{16,24},{24,16},{1,9},{9,1},{17,25},{25,17},{2,10},{10... | collective-permute-start | bytes 786440 | tf_op jit(solution)/shard_map/ppermute | solution.py:22
  39.5 21.2 %collective-permute-start.11 = (bf16[144,1024]{1,0:T(8,128)(2,1)}, bf16[144,1024]{1,0:T(8,128)(2,1)}, u32[]{:S(2)}, u32[]{:S(2)}) collective-permute-start(bf16[144,1024]{1,0:T(8,128)(2,1)} %collective-permute-done.10.refs_6_), channel_id=1, source_target_pairs={{0,8},{8,0},{16,24},{24,16},{1,9},{9,1},{17,25},{25,17},{2,10},{10... | collective-permute-start | bytes 884744 | tf_op jit(solution)/shard_map/ppermute | solution.py:22
  44.7 15.9 %collective-permute-start.8 = (bf16[128,1024]{1,0:T(8,128)(2,1)}, bf16[128,1024]{1,0:T(8,128)(2,1)}, u32[]{:S(2)}, u32[]{:S(2)}) collective-permute-start(bf16[128,1024]{1,0:T(8,128)(2,1)} %collective-permute-done.7.refs_4_), channel_id=1, source_target_pairs={{0,8},{8,0},{16,24},{24,16},{1,9},{9,1},{17,25},{25,17},{2,10},{10... | collective-permute-start | bytes 786440 | tf_op jit(solution)/shard_map/ppermute | solution.py:22
  46.7 1.0 copy-start.25
  47.7 0.9 copy-start.29
  48.6 0.9 copy-start.27
  49.6 1.9 %copy-start.19 = (bf16[144,1024]{1,0:T(8,128)(2,1)S(1)}, bf16[144,1024]{1,0:T(8,128)(2,1)}, u32[]{:S(2)}) copy-start(bf16[144,1024]{1,0:T(8,128)(2,1)} %copy-done.18) | copy-start | bytes 884740
  49.6 1.9 %copy-start.21 = (bf16[128,1024]{1,0:T(8,128)(2,1)S(1)}, bf16[128,1024]{1,0:T(8,128)(2,1)}, u32[]{:S(2)}) copy-start(bf16[128,1024]{1,0:T(8,128)(2,1)} %copy-done.20) | copy-start | bytes 786436
  49.6 1.9 %copy-start.31 = (bf16[128,1024]{1,0:T(8,128)(2,1)S(1)}, bf16[128,1024]{1,0:T(8,128)(2,1)}, u32[]{:S(2)}) copy-start(bf16[128,1024]{1,0:T(8,128)(2,1)} %copy-done.30) | copy-start | bytes 786436
  68.4 19.7 %all-to-all-start = ((f32[32,8,128]{2,1,0:T(8,128)}), f32[32,8,128]{2,1,0:T(8,128)S(1)}, u32[]{:S(2)}, u32[]{:S(2)}) async-start(f32[32,8,128]{2,1,0:T(8,128)} %bitcast.29), calls=%async_computation | async-start | bytes 262144 | tf_op jit(solution)/shard_map/all_to_all | solution.py:345
  80.1 4.9 %collective-permute-start.24 = (f32[8,512]{1,0:T(8,128)}, f32[8,512]{1,0:T(8,128)S(1)}, u32[]{:S(2)}, u32[]{:S(2)}) collective-permute-start(f32[8,512]{1,0:T(8,128)} %copy-done.36), channel_id=1, source_target_pairs={{0,18},{1,19},{2,16},{3,17},{4,22},{5,23},{6,20},{7,21},{8,26},{9,... | collective-permute-start | bytes 49160 | tf_op jit(solution)/shard_map/ppermute | solution.py:341
  82.9 4.1 %collective-permute-start.23 = (f32[8,512]{1,0:T(8,128)}, f32[8,512]{1,0:T(8,128)S(1)}, u32[]{:S(2)}, u32[]{:S(2)}) collective-permute-start(f32[8,512]{1,0:T(8,128)} %copy-done.36), channel_id=1, source_target_pairs={{0,16},{1,17},{2,18},{3,19},{4,20},{5,21},{6,22},{7,23},{8,24},{9,... | collective-permute-start | bytes 49160 | tf_op jit(solution)/shard_map/ppermute | solution.py:341
  83.4 4.1 %collective-permute-start.22 = (f32[8,512]{1,0:T(8,128)}, f32[8,512]{1,0:T(8,128)S(1)}, u32[]{:S(2)}, u32[]{:S(2)}) collective-permute-start(f32[8,512]{1,0:T(8,128)} %copy-done.36), channel_id=1, source_target_pairs={{0,2},{1,3},{2,0},{3,1},{4,6},{5,7},{6,4},{7,5},{8,10},{9,11},{10,... | collective-permute-start | bytes 49160 | tf_op jit(solution)/shard_map/ppermute | solution.py:341
  95.4 25.3 %all-to-all-start.1 = ((f32[32,8,128]{2,1,0:T(8,128)}), f32[32,8,128]{2,1,0:T(8,128)}, u32[]{:S(2)}, u32[]{:S(2)}) async-start(f32[32,8,128]{2,1,0:T(8,128)} %broadcast_in_dim.15), calls=%async_computation.1 | async-start | bytes 262144 | tf_op jit(solution)/shard_map/all_to_all | solution.py:372
  101.0 1.0 copy-start.1
  102.1 1.0 copy-start.3
  103.1 1.0 copy-start.5
  104.2 1.0 copy-start.7
  105.2 1.0 copy-start.9
  106.2 1.0 copy-start.11
  114.9 15.1 %collective-permute-start.25 = (f32[128,1024]{1,0:T(8,128)}, f32[128,1024]{1,0:T(8,128)}, u32[]{:S(2)}, u32[]{:S(2)}) collective-permute-start(f32[128,1024]{1,0:T(8,128)} %grads.5), channel_id=1, source_target_pairs={{0,2},{1,3},{2,0},{3,1},{4,6},{5,7},{6,4},{7,5},{8,10},{9,11},{10,... | collective-permute-start | bytes 1572872 | tf_op jit(solution)/shard_map/ppermute | solution.py:370
  116.4 25.2 %collective-permute-start.26 = (f32[128,1024]{1,0:T(8,128)}, f32[128,1024]{1,0:T(8,128)}, u32[]{:S(2)}, u32[]{:S(2)}) collective-permute-start(f32[128,1024]{1,0:T(8,128)} %grads.6), channel_id=1, source_target_pairs={{0,16},{1,17},{2,18},{3,19},{4,20},{5,21},{6,22},{7,23},{8,24},{9,... | collective-permute-start | bytes 1572872 | tf_op jit(solution)/shard_map/ppermute | solution.py:370
  117.9 23.8 %collective-permute-start.27 = (f32[128,1024]{1,0:T(8,128)}, f32[128,1024]{1,0:T(8,128)}, u32[]{:S(2)}, u32[]{:S(2)}) collective-permute-start(f32[128,1024]{1,0:T(8,128)} %grads.7), channel_id=1, source_target_pairs={{0,18},{1,19},{2,16},{3,17},{4,22},{5,23},{6,20},{7,21},{8,26},{9,... | collective-permute-start | bytes 1572872 | tf_op jit(solution)/shard_map/ppermute | solution.py:370
  141.7 1.0 copy-start.15
  142.6 1.0 copy-start.17
  (31 other events, 22.2 us)

commit v2 on v1

--- a/solution.py
+++ b/solution.py
@@ -13,8 +13,9 @@
 epsilon = 1e-06
 
 AXES = ("grp", "dev")
+EARLY = 2
 PAD = 16
-VMEM_LIMIT = 40 * 1024 * 1024
+VMEM_LIMIT = 63 * 1024 * 1024
 
 
 def swapped(value, axis, mask):
@@ -48,29 +49,51 @@
     )
 
 
-def call(kernel, out_shape, operands, smem=0, flops=0, name=None):
+def call(kernel, out_shape, operands, flops=0, name=None, blocks=None):
     specs = []
     for i, item in enumerate(operands):
-        if i < smem:
-            specs.append(pl.BlockSpec(memory_space=pltpu.SMEM))
-        else:
-            specs.append(pl.BlockSpec(memory_space=pltpu.VMEM))
+        size, at = (blocks or {}).get(i, (item.shape[0], 0))
+        specs.append(
+            pl.BlockSpec((size, item.shape[1]), functools.partial(lambda at, step: (at, 0), at))
+        )
     many = isinstance(out_shape, (tuple, list))
-    out_specs = (
-        tuple(pl.BlockSpec(memory_space=pltpu.VMEM) for _ in out_shape)
-        if many
-        else pl.BlockSpec(memory_space=pltpu.VMEM)
-    )
+    outs = tuple(out_shape) if many else (out_shape,)
+    out_specs = tuple(pl.BlockSpec(item.shape, lambda step: (0, 0)) for item in outs)
     moved = sum(item.size * item.dtype.itemsize for item in operands)
     return pl.pallas_call(
         kernel,
-        out_shape=tuple(out_shape) if many else out_shape,
+        out_shape=outs if many else out_shape,
+        grid=(1,),
         in_specs=specs,
-        out_specs=out_specs,
+        out_specs=out_specs if many else out_specs[0],
         name=name,
         cost_estimate=pl.CostEstimate(flops=flops, bytes_accessed=moved, transcendentals=0),
         compiler_params=pltpu.CompilerParams(vmem_limit_bytes=VMEM_LIMIT),
     )(*operands)
+
+
+def place():
+    group, member = lax.axis_index("grp"), lax.axis_index("dev")
+    quarter = lax.axis_size("dev") // 4
+    return (
+        group // 2,
+        group % 2,
+        member // (2 * quarter),
+        (member // quarter) % 2,
+        member % quarter,
+    )
+
+
+def key_id(k):
+    h, c, p, q, r = place()
+    members = lax.axis_size("dev")
+    return ((h ^ (k // 2)) * 2 + c) * members + (p * 2 + (q ^ (k % 2))) * (members // 4) + r
+
+
+def anchor_id(i, dc):
+    h, c, p, q, r = place()
+    members = lax.axis_size("dev")
+    return (h * 2 + (c ^ dc)) * members + (q * 2 + (p ^ (i % 2))) * (members // 4) + (r ^ (i // 2))
 
 
 def keys_kernel(count, rows, *refs):
@@ -83,10 +106,11 @@
         label_ref[place, :] = column_of(label_row(teachers[k], rows))
 
 
-def tile_kernel(count, rows, width, first, last, *refs):
-    ids, unit_ref, teacher_ref, label_ref = refs[:4]
-    students, teachers = refs[4:6], refs[6:8]
-    rest = refs[8:]
+def tile_kernel(count, rows, i, last, *refs):
+    unit_ref, teacher_ref, label_ref = refs[:3]
+    students, teachers = refs[3:5], refs[5:7]
+    rest = refs[7:]
+    first = i == 0
     if not first:
         old_ref, rest = rest[0], rest[1:]
     anchor_ref, similar_ref, weight_ref, anchor_label_ref, stats_ref = rest[:5]
@@ -107,7 +131,7 @@
         for n in range(2):
             across = slice(n * rows, (n + 1) * rows)
             similar = similar_ref[down, across]
-            offset = jnp.where(ids[k] == ids[count + n], 0, rows)
+            offset = jnp.where(key_id(k) == anchor_id(i, n), 0, rows)
             distinct = row_at != lane_at - offset
             rel_exp = jnp.where(distinct, jnp.exp((similar - 1.0) / temp_student), 0.0)
             weight = jnp.where(
@@ -126,8 +150,8 @@
             )
             totals = [total + term for total, term in zip(totals, terms)]
         stats = jnp.zeros((rows, rows), jnp.float32)
-        for i, total in enumerate(totals):
-            stats = jnp.where(lane_at == i, jnp.sum(total, axis=1, keepdims=True), stats)
+        for j, total in enumerate(totals):
+            stats = jnp.where(lane_at == j, jnp.sum(total, axis=1, keepdims=True), stats)
         if not first:
             stats = stats + old_ref[down, :]
         stats_ref[down, :] = stats
@@ -136,11 +160,11 @@
 
 
 def merge_kernel(dims, rows, *refs):
-    groups, members, keys, pair_places = dims
-    place, received_ref, own_ref = refs[:3]
-    others = refs[3 : 2 + keys]
-    anchor_ref, key_ref, loss_ref = refs[2 + keys :]
-    c, p, q, r = place[0], place[1], place[2], place[3]
+    groups, members, keys = dims
+    received_ref, own_ref = refs[:2]
+    others = refs[2 : 1 + keys]
+    anchor_ref, key_ref, loss_ref = refs[1 + keys :]
+    _, c, p, q, r = place()
     quarter = members // 4
     for k in range(keys):
         total = own_ref[:, k * rows : (k + 1) * rows]
@@ -186,15 +210,14 @@
                 anchor_ref[:, at : at + rows] = value
 
 
-def grad_kernel(pairs, rows, width, k, count, *refs):
-    ids, label_ref, key_ref, anchor_stats_ref = refs[:4]
-    rest = refs[4:]
+def grad_kernel(pairs, rows, k, *refs):
+    label_ref, key_ref, anchor_stats_ref = refs[:3]
+    rest = refs[3:]
     similar, weights, labels, units = (rest[i * pairs : (i + 1) * pairs] for i in range(4))
     out_ref = rest[4 * pairs]
-    down = slice(k * rows, (k + 1) * rows)
     row_at = lax.broadcasted_iota(jnp.int32, (rows, rows), 0)
     lane_at = lax.broadcasted_iota(jnp.int32, (rows, rows), 1)
-    sup_key, rel_key, teacher_key, pos_key = (key_ref[down, i : i + 1] for i in range(4))
+    sup_key, rel_key, teacher_key, pos_key = (key_ref[:, i : i + 1] for i in range(4))
     total = None
     for i in range(pairs):
         row_parts, column_parts = [], []
@@ -204,14 +227,14 @@
             sup_all, rel_all, teacher_all, pos_all = (
                 anchor_stats_ref[j : j + 1, at : at + rows] for j in range(4)
             )
-            offset = jnp.where(ids[k] == ids[count + i * 2 + n], 0, rows)
+            offset = jnp.where(key_id(k) == anchor_id(i, n), 0, rows)
             distinct = row_at != lane_at - offset
             rel_exp = jnp.where(
-                distinct, jnp.exp((similar[i][down, across] - 1.0) / temp_student), 0.0
+                distinct, jnp.exp((similar[i][:, across] - 1.0) / temp_student), 0.0
             )
             sup_exp = rel_exp * rel_exp
-            weight = weights[i][down, across]
-            same = label_ref[down, :] == labels[i][0:1, across]
+            weight = weights[i][:, across]
+            same = label_ref[...] == labels[i][0:1, across]
             positive = jnp.where(jnp.logical_and(same, distinct), 1.0, 0.0)
             row_parts.append(
                 (
@@ -257,9 +280,7 @@
     rows, width = student.shape
     groups, members = lax.axis_size("grp"), lax.axis_size("dev")
     halves, quarter = groups // 2, members // 4
-    group, member = lax.axis_index("grp"), lax.axis_index("dev")
-    h, c = group // 2, group % 2
-    p, q, r = member // (2 * quarter), (member // quarter) % 2, member % quarter
+    h, c, p, q, r = place()
     inner = p != q
     cross = [
         (d, d ^ (3 * quarter)) for d in range(members) if (d // (2 * quarter)) != (d // quarter) % 2
@@ -284,20 +305,11 @@
     ]
     for bit in bits_of(quarter):
         anchors = anchors + [both(lambda v: swapped(v, "dev", bit), item) for item in anchors]
-    pairs = [(item, both(lambda v: swapped(v, "grp", 1), item)) for item in anchors]
-
-    key_count, pair_count = len(keys), len(pairs)
+    late = len(anchors) - 1
+    pairs = [(item, both(lambda v: swapped(v, "grp", 1), item)) for item in anchors[:late]]
+
+    key_count, pair_count = len(keys), len(anchors)
     key_rows = key_count * rows
-    key_ids = [
-        ((h ^ (k // 2)) * 2 + c) * members + (p * 2 + (q ^ (k % 2))) * quarter + r
-        for k in range(key_count)
-    ]
-    anchor_ids = [
-        (h * 2 + (c ^ dc)) * members + (q * 2 + (p ^ (i % 2))) * quarter + (r ^ (i // 2))
-        for i in range(pair_count)
-        for dc in range(2)
-    ]
-    ids = jnp.stack(key_ids + anchor_ids).astype(jnp.int32)
     f32 = functools.partial(jax.ShapeDtypeStruct, dtype=jnp.float32)
     b16 = functools.partial(jax.ShapeDtypeStruct, dtype=jnp.bfloat16)
 
@@ -310,11 +322,15 @@
     )
     units, similar, weights, anchor_labels = [], [], [], []
     stats = None
-    for i, (first, second) in enumerate(pairs):
+    for i in range(pair_count):
         last = i == pair_count - 1
-        tile_ids = jnp.concatenate([ids[:key_count], ids[key_count + 2 * i : key_count + 2 * i + 2]])
+        if i == EARLY:
+            held_stats, anchors[late] = lax.optimization_barrier((stats, anchors[late]))
+            stats = held_stats
+            pairs.append((anchors[late], both(lambda v: swapped(v, "grp", 1), anchors[late])))
+        first, second = pairs[i]
         outs = call(
-            functools.partial(tile_kernel, key_count, rows, width, stats is None, last),
+            functools.partial(tile_kernel, key_count, rows, i, last),
             (
                 b16((2 * rows, width)),
                 f32((key_rows, 2 * rows)),
@@ -323,9 +339,8 @@
                 f32((key_rows, rows)),
             )
             + ((f32((8, key_rows)),) if last else ()),
-            [tile_ids, key_unit, key_teacher, key_label, first[0], second[0], first[1], second[1]]
+            [key_unit, key_teacher, key_label, first[0], second[0], first[1], second[1]]
             + ([] if stats is None else [stats]),
-            smem=1,
             flops=8 * key_rows * rows * width,
             name="tile",
         )
@@ -344,31 +359,35 @@
     payload = jnp.broadcast_to(blocks, (halves, 2 * members, 8, rows)).reshape(-1, rows)
     received = lax.all_to_all(payload, AXES, 0, 0, tiled=True)
     anchor_stats, key_stats, loss = call(
-        functools.partial(merge_kernel, (groups, members, key_count, pair_count), rows),
+        functools.partial(merge_kernel, (groups, members, key_count), rows),
         (f32((8, members * rows)), f32((key_rows, rows)), f32((8, rows))),
-        [jnp.stack([c, p, q, r]).astype(jnp.int32), received, sums] + others,
-        smem=1,
+        [received, sums] + others,
         name="merge",
     )
 
-    def grads(k):
-        operands = [ids, key_label, key_stats, anchor_stats] + similar + weights + anchor_labels + units
+    def grads(k, key_stats):
+        blocks = {i: (rows, k) for i in (0, 1)}
+        for i in range(2 * pair_count):
+            blocks[3 + i] = (rows, k)
+        operands = [key_label, key_stats, anchor_stats] + similar + weights + anchor_labels + units
         return call(
-            functools.partial(grad_kernel, pair_count, rows, width, k, key_count),
+            functools.partial(grad_kernel, pair_count, rows, k),
             f32((rows, width)),
             operands,
-            smem=1,
             flops=4 * rows * members * rows * width,
             name="grads",
+            blocks=blocks,
         )
 
     parts = []
     for k in range(key_count - 1, -1, -1):
-        part = grads(k)
+        part = grads(k, key_stats)
         if k:
+            key_stats, part = lax.optimization_barrier((key_stats, part))
             mask = (k // 2) * 2 * members + (k % 2) * quarter
             part = lax.ppermute(part, AXES, [(i, i ^ mask) for i in range(groups * members)])
         parts.append(part)
+    loss, parts[0], parts[-1] = lax.optimization_barrier((loss, parts[0], parts[-1]))
     shared = lax.all_to_all(
         jnp.broadcast_to(loss[None], (groups * members, 8, rows)).reshape(-1, rows), AXES, 0, 0, tiled=True
     ).reshape(groups * members, 8, rows)

time: 147 us -> 116 us (0.79)
  local copies, waits for them, and re-layouts: 35.1 us -> 5.63 us
  Pallas kernels: 22.1 us -> 39.3 us
  waiting for transfers between devices: 38.6 us -> 24.1 us
  starting transfers between devices: 45.6 us -> 42.3 us
    unnamed x98 -> x48, local copies, waits for them, and re-layouts: 31.1 us -> 2.25 us
    pallas_call x11, Pallas kernels: 22.1 us -> 39.3 us  [call(): pl.pallas_call(kernel, out_shape=outs if many else out_shape, grid=(1,),...]
    ppermute x3, waiting for transfers between devices: 19.4 us -> 7.8 us  [body(): lax.ppermute(part, AXES, [(i, i ^ mask) for i in range(groups * members)])]
    ppermute x18, waiting for transfers between devices: 17.2 us -> 12.3 us  [swapped(): return lax.ppermute(value, axis, [(i, i ^ mask) for i in range(size)])]
    all_to_all x1, starting transfers between devices: 11.7 us -> 8.22 us  [body(): received = lax.all_to_all(payload, AXES, 0, 0, tiled=True)]
    concatenate x4 -> x0, local copies, waits for them, and re-layouts: 1.98 us -> none  [body(): jnp.concatenate([ids[:key_count], ids[key_count + 2 * i:key_count + 2 * i...]
  transfers between devices with their start and end apart: 30 -> 30, of which waited for: 11 -> 11; matrix products, arithmetic and copies ran while one was open for 3% -> 1% of each run, Pallas kernels for 11% -> 26%
where the time goes in v2:
time: 116 us; the launch traced here: 115 us
  starting transfers between devices  42.3 us (36%)
  Pallas kernels  39.3 us (34%)
  waiting for transfers between devices  24.1 us (21%)
  local copies, waits for them, and re-layouts  5.63 us (5%)
  other arithmetic  2.77 us (2%)
    pallas_call x11, Pallas kernels, call(): pl.pallas_call(kernel, out_shape=outs if many else out_shape, grid=(1,),...  39.3 us
    ppermute x18, starting transfers between devices, swapped(): return lax.ppermute(value, axis, [(i, i ^ mask) for i in range(size)])  20.3 us
    ppermute x18, waiting for transfers between devices, swapped(): return lax.ppermute(value, axis, [(i, i ^ mask) for i in range(size)])  12.3 us
    all_to_all x1, starting transfers between devices, body(): received = lax.all_to_all(payload, AXES, 0, 0, tiled=True)  8.22 us
    ppermute x3, waiting for transfers between devices, body(): lax.ppermute(part, AXES, [(i, i ^ mask) for i in range(groups * members)])  7.8 us
    all_to_all x1, starting transfers between devices, body(): lax.all_to_all(jnp.broadcast_to(loss[None], (groups * members, 8, rows))....  3.98 us
    ppermute x3, starting transfers between devices, body(): lax.ppermute(sums, AXES, [(i, i ^ mask) for i in range(total)])  3.55 us
    ppermute x3, starting transfers between devices, body(): lax.ppermute(part, AXES, [(i, i ^ mask) for i in range(groups * members)])  3.49 us
  transfers between devices with their start and end apart: 30, of which 11 were waited for; matrix products, arithmetic and copies ran while one was open for 1% of the time, Pallas kernels for 26%

profile of v2, /device:TPU:0, one launch (start us, length us, event | category | flops | bytes accessed | tf_op | source)
XLA Modules:
  0.0 115.0 jit_solution(15971571379977950449)
XLA Ops:
  0.6 0.7 convert_bitcast_fusion
  1.3 1.0 pad_maximum_fusion.refs_4_
  2.4 3.1 %collective-permute-start.3 = (bf16[144,1024]{1,0:T(8,128)(2,1)S(1)}, bf16[144,1024]{1,0:T(8,128)(2,1)S(1)}, u32[]{:S(2)}, u32[]{:S(2)}) collective-permute-start(bf16[144,1024]{1,0:T(8,128)(2,1)S(1)} %pad_maximum_fusion.refs_4_), channel_id=1, source_target_pairs={{0,2},{1,3},{2,0},{3,1},{4,6},{5,7},{6,4},{7,5},{8,10},{9,11},{10,... | collective-permute-start | bytes 884744 | tf_op jit(solution)/shard_map/ppermute | solution.py:23
  5.4 0.7 collective-permute-start.10
  6.1 0.7 collective-permute-start.12
  6.8 1.6 %collective-permute-start.1 = (bf16[128,1024]{1,0:T(8,128)(2,1)S(1)}, bf16[128,1024]{1,0:T(8,128)(2,1)S(1)}, u32[]{:S(2)}, u32[]{:S(2)}) collective-permute-start(bf16[128,1024]{1,0:T(8,128)(2,1)S(1)} %copy-done), channel_id=1, source_target_pairs={{0,16},{8,24},{16,0},{24,8},{1,17},{9,25},{17,1},{25,9},{2,18},{10... | collective-permute-start | bytes 786440 | tf_op jit(solution)/shard_map/ppermute | solution.py:23
  8.4 5.6 %collective-permute-start = (bf16[128,1024]{1,0:T(8,128)(2,1)S(1)}, bf16[128,1024]{1,0:T(8,128)(2,1)S(1)}, u32[]{:S(2)}, u32[]{:S(2)}) collective-permute-start(bf16[128,1024]{1,0:T(8,128)(2,1)S(1)} %copy-done), channel_id=1, source_target_pairs={{0,2},{1,3},{2,0},{3,1},{4,6},{5,7},{6,4},{7,5},{8,10},{9,11},{10,... | collective-permute-start | bytes 786440 | tf_op jit(solution)/shard_map/ppermute | solution.py:23
  14.5 0.7 collective-permute-start.8
  15.3 1.6 %collective-permute-start.18 = (bf16[128,1024]{1,0:T(8,128)(2,1)S(1)}, bf16[128,1024]{1,0:T(8,128)(2,1)S(1)}, u32[]{:S(2)}, u32[]{:S(2)}) collective-permute-start(bf16[128,1024]{1,0:T(8,128)(2,1)S(1)} %broadcast_select_fusion.2.refs_3_), channel_id=1, source_target_pairs={{0,1},{1,0},{2,3},{3,2},{4,5},{5,4},{6,7},{7,6},{8,9},{9,8},{10,11... | collective-permute-start | bytes 786440 | tf_op jit(solution)/shard_map/ppermute | solution.py:23
  16.9 2.6 %collective-permute-done.refs_1_ = bf16[128,1024]{1,0:T(8,128)(2,1)S(1)} collective-permute-done((bf16[128,1024]{1,0:T(8,128)(2,1)S(1)}, bf16[128,1024]{1,0:T(8,128)(2,1)S(1)}, u32[]{:S(2)}, u32[]{:S(2)}) %collective-permute-start) | collective-permute-done | bytes 262176 | tf_op jit(solution)/shard_map/ppermute | solution.py:23
  19.5 0.7 collective-permute-start.6
  20.2 0.8 broadcast_select_fusion.refs_5_
  21.0 0.7 collective-permute-done.4.refs_6_
  21.6 0.8 collective-permute-start.2
  22.5 1.3 %collective-permute-start.5 = (bf16[144,1024]{1,0:T(8,128)(2,1)S(1)}, bf16[144,1024]{1,0:T(8,128)(2,1)S(1)}, u32[]{:S(2)}, u32[]{:S(2)}) collective-permute-start(bf16[144,1024]{1,0:T(8,128)(2,1)S(1)} %collective-permute-done.3.refs_5_), channel_id=1, source_target_pairs={{0,16},{8,24},{16,0},{24,8},{1,17},{9,25},{17,1},{25,9},{2,18},{10... | collective-permute-start | bytes 884744 | tf_op jit(solution)/shard_map/ppermute | solution.py:23
  23.8 1.6 %collective-permute-start.20 = (bf16[144,1024]{1,0:T(8,128)(2,1)}, bf16[144,1024]{1,0:T(8,128)(2,1)S(1)}, u32[]{:S(2)}, u32[]{:S(2)}) collective-permute-start(bf16[144,1024]{1,0:T(8,128)(2,1)} %broadcast_select_fusion.refs_5_), channel_id=1, source_target_pairs={{0,1},{1,0},{2,3},{3,2},{4,5},{5,4},{6,7},{7,6},{8,9},{9,8},{10,11... | collective-permute-start | bytes 884744 | tf_op jit(solution)/shard_map/ppermute | solution.py:23
  25.5 5.3 %collective-permute-done.2.refs_3_ = bf16[128,1024]{1,0:T(8,128)(2,1)S(1)} collective-permute-done((bf16[128,1024]{1,0:T(8,128)(2,1)S(1)}, bf16[128,1024]{1,0:T(8,128)(2,1)S(1)}, u32[]{:S(2)}, u32[]{:S(2)}) %collective-permute-start.2) | collective-permute-done | bytes 262176 | tf_op jit(solution)/shard_map/ppermute | solution.py:23
  30.8 1.6 %collective-permute-start.15 = (bf16[144,1024]{1,0:T(8,128)(2,1)S(1)}, bf16[144,1024]{1,0:T(8,128)(2,1)}, u32[]{:S(2)}, u32[]{:S(2)}) collective-permute-start(bf16[144,1024]{1,0:T(8,128)(2,1)S(1)} %broadcast_select_fusion.1.refs_5_), channel_id=1, source_target_pairs={{0,1},{1,0},{2,3},{3,2},{4,5},{5,4},{6,7},{7,6},{8,9},{9,8},{10,11... | collective-permute-start | bytes 884744 | tf_op jit(solution)/shard_map/ppermute | solution.py:23
  32.4 3.6 %collective-permute-done.5.refs_7_ = bf16[144,1024]{1,0:T(8,128)(2,1)S(1)} collective-permute-done((bf16[144,1024]{1,0:T(8,128)(2,1)S(1)}, bf16[144,1024]{1,0:T(8,128)(2,1)S(1)}, u32[]{:S(2)}, u32[]{:S(2)}) %collective-permute-start.5) | collective-permute-done | bytes 294944 | tf_op jit(solution)/shard_map/ppermute | solution.py:23
  36.1 0.7 copy-done.13
  36.8 1.5 %collective-permute-start.14 = (bf16[128,1024]{1,0:T(8,128)(2,1)S(1)}, bf16[128,1024]{1,0:T(8,128)(2,1)}, u32[]{:S(2)}, u32[]{:S(2)}) collective-permute-start(bf16[128,1024]{1,0:T(8,128)(2,1)S(1)} %broadcast_select_fusion.3.refs_3_), channel_id=1, source_target_pairs={{0,1},{1,0},{2,3},{3,2},{4,5},{5,4},{6,7},{7,6},{8,9},{9,8},{10,11... | collective-permute-start | bytes 786440 | tf_op jit(solution)/shard_map/ppermute | solution.py:23
  38.3 3.6 %keys.1 = (bf16[512,1024]{1,0:T(8,128)(2,1)}, bf16[512,1024]{1,0:T(8,128)(2,1)}, f32[512,128]{1,0:T(8,128)}) custom-call(bf16[128,1024]{1,0:T(8,128)(2,1)} %student_ref.1, bf16[128,1024]{1,0:T(8,128)(2,1)} %copy-done.6, bf16[128,1024]{1,0:T(8,128)(2,1)} %copy-done.17, bf16[128,1024]{1,0:T(8,128)(2,1)} %copy-done.18, bf16[144,1024]{1,0:T(8,128)(2,1)} %copy-done.3, ...), custom_call_target="tpu_custom_call" | custom-call | flops 4194304 | bytes 2228224 | tf_op jit(solution)/shard_map/keys/pallas_call | solution.py:63
  41.9 4.0 %tile.4 = (bf16[256,1024]{1,0:T(8,128)(2,1)}, f32[512,256]{1,0:T(8,128)}, f32[512,256]{1,0:T(8,128)}, f32[8,256]{1,0:T(8,128)}, f32[512,128]{1,0:T(8,128)}) custom-call(bf16[512,1024]{1,0:T(8,128)(2,1)} %get-tuple-element.41.refs_0_, bf16[512,1024]{1,0:T(8,128)(2,1)} %get-tuple-element.42.refs_1_, f32[512,128]{1,0:T(8,128)} %get-tuple-element.43.refs_2_.refs_0_, ...), custom_call_target="tpu_custom_call" | custom-call | flops 536870912 | bytes 3473408 | tf_op jit(solution)/shard_map/tile/pallas_call | solution.py:63
  46.5 4.1 %tile.5 = (bf16[256,1024]{1,0:T(8,128)(2,1)}, f32[512,256]{1,0:T(8,128)}, f32[512,256]{1,0:T(8,128)}, f32[8,256]{1,0:T(8,128)}, f32[512,128]{1,0:T(8,128)}) custom-call(bf16[512,1024]{1,0:T(8,128)(2,1)} %get-tuple-element.41.refs_0_, bf16[512,1024]{1,0:T(8,128)(2,1)} %get-tuple-element.42.refs_1_, f32[512,128]{1,0:T(8,128)} %get-tuple-element.43.refs_2_.refs_0_, ...), custom_call_target="tpu_custom_call" | custom-call | flops 536870912 | bytes 3735552 | tf_op jit(solution)/shard_map/tile/pallas_call | solution.py:63
  51.2 4.1 %tile.6 = (bf16[256,1024]{1,0:T(8,128)(2,1)}, f32[512,256]{1,0:T(8,128)}, f32[512,256]{1,0:T(8,128)}, f32[8,256]{1,0:T(8,128)}, f32[512,128]{1,0:T(8,128)}) custom-call(bf16[512,1024]{1,0:T(8,128)(2,1)} %get-tuple-element.41.refs_0_, bf16[512,1024]{1,0:T(8,128)(2,1)} %get-tuple-element.42.refs_1_, f32[512,128]{1,0:T(8,128)} %get-tuple-element.43.refs_2_.refs_0_, ...), custom_call_target="tpu_custom_call" | custom-call | flops 536870912 | bytes 3735552 | tf_op jit(solution)/shard_map/tile/pallas_call | solution.py:63
  55.4 0.7 copy-done.16
  56.1 4.2 %tile.7 = (bf16[256,1024]{1,0:T(8,128)(2,1)}, f32[512,256]{1,0:T(8,128)}, f32[512,256]{1,0:T(8,128)}, f32[8,256]{1,0:T(8,128)}, f32[512,128]{1,0:T(8,128)}, /*index=5*/f32[8,512]{1,0:T(8,128)}) custom-call(bf16[512,1024]{1,0:T(8,128)(2,1)} %get-tuple-element.41.refs_0_, bf16[512,1024]{1,0:T(8,128)(2,1)} %get-tuple-element.42.refs_1_, ...), custom_call_target="tpu_custom_call" | custom-call | flops 536870912 | bytes 3735552 | tf_op jit(solution)/shard_map/tile/pallas_call | solution.py:63
  60.3 0.7 slice.31
  61.1 0.7 slice.30
  61.8 0.7 broadcast_in_dim.14
  62.5 8.2 %all-to-all-start = ((f32[32,8,128]{2,1,0:T(8,128)}), f32[32,8,128]{2,1,0:T(8,128)S(1)}, u32[]{:S(2)}, u32[]{:S(2)}) async-start(f32[32,8,128]{2,1,0:T(8,128)} %bitcast.5), calls=%async_computation | async-start | bytes 262144 | tf_op jit(solution)/shard_map/all_to_all | solution.py:360
  70.8 2.6 %collective-permute-start.24 = (f32[8,512]{1,0:T(8,128)S(1)}, f32[8,512]{1,0:T(8,128)S(1)}, u32[]{:S(2)}, u32[]{:S(2)}) collective-permute-start(f32[8,512]{1,0:T(8,128)S(1)} %copy-done.19), channel_id=1, source_target_pairs={{0,18},{1,19},{2,16},{3,17},{4,22},{5,23},{6,20},{7,21},{8,26},{9,... | collective-permute-start | bytes 49160 | tf_op jit(solution)/shard_map/ppermute | solution.py:356
  74.3 1.2 %collective-permute-done.24.refs_4_ = f32[8,512]{1,0:T(8,128)S(1)} collective-permute-done((f32[8,512]{1,0:T(8,128)S(1)}, f32[8,512]{1,0:T(8,128)S(1)}, u32[]{:S(2)}, u32[]{:S(2)}) %collective-permute-start.24) | collective-permute-done | bytes 16416 | tf_op jit(solution)/shard_map/ppermute | solution.py:356
  75.5 1.7 %collective-permute-done.23.refs_3_ = f32[8,512]{1,0:T(8,128)S(1)} collective-permute-done((f32[8,512]{1,0:T(8,128)S(1)}, f32[8,512]{1,0:T(8,128)S(1)}, u32[]{:S(2)}, u32[]{:S(2)}) %collective-permute-start.23) | collective-permute-done | bytes 16416 | tf_op jit(solution)/shard_map/ppermute | solution.py:356
  78.3 0.7 copy-done.9
  79.0 1.9 %merge.1 = (f32[8,1024]{1,0:T(8,128)}, f32[512,128]{1,0:T(8,128)}, f32[8,128]{1,0:T(8,128)}) custom-call(f32[256,128]{1,0:T(8,128)} %bitcast.12, f32[8,512]{1,0:T(8,128)} %get-tuple-element.50.refs_1_, f32[8,512]{1,0:T(8,128)} %copy-done.22, f32[8,512]{1,0:T(8,128)} %copy-done.21, f32[8,512]{1,0:T(8,128)} %copy-done.20), custom_call_target="tpu_custom_call" | custom-call | bytes 196608 | tf_op jit(solution)/shard_map/merge/pallas_call | solution.py:63
  80.8 3.7 %grads.4 = f32[128,1024]{1,0:T(8,128)} custom-call(f32[512,128]{1,0:T(8,128)} %get-tuple-element.43.refs_2_.refs_0_, f32[512,128]{1,0:T(8,128)} %get-tuple-element.73.refs_1_, f32[8,1024]{1,0:T(8,128)} %get-tuple-element.53.refs_2_, f32[512,256]{1,0:T(8,128)} %get-tuple-element.54.refs_3_, f32[512,256]{1,0:T(8,128)} %get-tuple-element.55.refs_4_, ...), custom_call_target="tpu_custom_call" | custom-call | flops 536870912 | bytes 6881280 | tf_op jit(solution)/shard_map/grads/pallas_call | solution.py:63
  84.6 1.0 collective-permute-start.25
  85.6 3.7 %grads.5 = f32[128,1024]{1,0:T(8,128)} custom-call(f32[512,128]{1,0:T(8,128)} %get-tuple-element.43.refs_2_.refs_0_, f32[512,128]{1,0:T(8,128)} %get-tuple-element.73.refs_1_, f32[8,1024]{1,0:T(8,128)} %get-tuple-element.53.refs_2_, f32[512,256]{1,0:T(8,128)} %get-tuple-element.54.refs_3_, f32[512,256]{1,0:T(8,128)} %get-tuple-element.55.refs_4_, ...), custom_call_target="tpu_custom_call" | custom-call | flops 536870912 | bytes 6881280 | tf_op jit(solution)/shard_map/grads/pallas_call | solution.py:63
  89.2 3.7 %grads.6 = f32[128,1024]{1,0:T(8,128)} custom-call(f32[512,128]{1,0:T(8,128)} %get-tuple-element.43.refs_2_.refs_0_, f32[512,128]{1,0:T(8,128)} %get-tuple-element.73.refs_1_, f32[8,1024]{1,0:T(8,128)} %get-tuple-element.53.refs_2_, f32[512,256]{1,0:T(8,128)} %get-tuple-element.54.refs_3_, f32[512,256]{1,0:T(8,128)} %get-tuple-element.55.refs_4_, ...), custom_call_target="tpu_custom_call" | custom-call | flops 536870912 | bytes 6881280 | tf_op jit(solution)/shard_map/grads/pallas_call | solution.py:63
  93.0 1.6 %collective-permute-start.26 = (f32[128,1024]{1,0:T(8,128)}, f32[128,1024]{1,0:T(8,128)}, u32[]{:S(2)}, u32[]{:S(2)}) collective-permute-start(f32[128,1024]{1,0:T(8,128)} %grads.6), channel_id=1, source_target_pairs={{0,2},{1,3},{2,0},{3,1},{4,6},{5,7},{6,4},{7,5},{8,10},{9,11},{10,... | collective-permute-start | bytes 1572872 | tf_op jit(solution)/shard_map/ppermute | solution.py:388
  94.5 0.9 collective-permute-start.27
  95.5 3.7 %grads.7.refs_0_ = f32[128,1024]{1,0:T(8,128)} custom-call(f32[512,128]{1,0:T(8,128)} %get-tuple-element.43.refs_2_.refs_0_, f32[512,128]{1,0:T(8,128)} %get-tuple-element.73.refs_1_, f32[8,1024]{1,0:T(8,128)} %get-tuple-element.53.refs_2_, f32[512,256]{1,0:T(8,128)} %get-tuple-element.54.refs_3_, f32[512,256]{1,0:T(8,128)} %get-tuple-element.55.refs_4_, ...), custom_call_target="tpu_custom_call" | custom-call | flops 536870912 | bytes 6881280 | tf_op jit(solution)/shard_map/grads/pallas_call | solution.py:63
  99.2 1.4 %collective-permute-done.25.refs_3_ = f32[128,1024]{1,0:T(8,128)} collective-permute-done((f32[128,1024]{1,0:T(8,128)}, f32[128,1024]{1,0:T(8,128)}, u32[]{:S(2)}, u32[]{:S(2)}) %collective-permute-start.25) | collective-permute-done | bytes 524320 | tf_op jit(solution)/shard_map/ppermute | solution.py:388
  100.6 0.7 broadcast_in_dim.15
  101.3 4.0 %all-to-all-start.1 = ((f32[32,8,128]{2,1,0:T(8,128)}), f32[32,8,128]{2,1,0:T(8,128)S(1)}, u32[]{:S(2)}, u32[]{:S(2)}) async-start(f32[32,8,128]{2,1,0:T(8,128)} %broadcast_in_dim.15), calls=%async_computation.1 | async-start | bytes 262144 | tf_op jit(solution)/shard_map/all_to_all | solution.py:391
  105.3 6.1 %collective-permute-done.26.refs_1_ = f32[128,1024]{1,0:T(8,128)} collective-permute-done((f32[128,1024]{1,0:T(8,128)}, f32[128,1024]{1,0:T(8,128)}, u32[]{:S(2)}, u32[]{:S(2)}) %collective-permute-start.26) | collective-permute-done | bytes 524320 | tf_op jit(solution)/shard_map/ppermute | solution.py:388
  111.6 2.7 %final.1 = f32[128,1024]{1,0:T(8,128)} custom-call(bf16[128,1024]{1,0:T(8,128)(2,1)} %student_ref.1, f32[128,1024]{1,0:T(8,128)} %grads.7.refs_0_, f32[128,1024]{1,0:T(8,128)} %collective-permute-done.26.refs_1_, f32[128,1024]{1,0:T(8,128)} %collective-permute-done.27.refs_2_, f32[128,1024]{1,0:T(8,128)} %collective-permute-done.25.refs_3_), custom_call_target="tpu_custom_call" | custom-call | flops 1048576 | bytes 2359296 | tf_op jit(solution)/shard_map/final/pallas_call | solution.py:63
  (90 shorter events, 5.2 us)
Async XLA Ops:
  1.3 4.1 %copy-start = (bf16[128,1024]{1,0:T(8,128)(2,1)S(1)}, bf16[128,1024]{1,0:T(8,128)(2,1)}, u32[]{:S(2)}) copy-start(bf16[128,1024]{1,0:T(8,128)(2,1)} %student_ref.1) | copy-start | bytes 786436
  2.3 12.9 %copy-start.3 = (bf16[144,1024]{1,0:T(8,128)(2,1)}, bf16[144,1024]{1,0:T(8,128)(2,1)S(1)}, u32[]{:S(2)}) copy-start(bf16[144,1024]{1,0:T(8,128)(2,1)S(1)} %pad_maximum_fusion.refs_4_) | copy-start | bytes 884740
  2.4 12.2 %collective-permute-start.3 = (bf16[144,1024]{1,0:T(8,128)(2,1)S(1)}, bf16[144,1024]{1,0:T(8,128)(2,1)S(1)}, u32[]{:S(2)}, u32[]{:S(2)}) collective-permute-start(bf16[144,1024]{1,0:T(8,128)(2,1)S(1)} %pad_maximum_fusion.refs_4_), channel_id=1, source_target_pairs={{0,2},{1,3},{2,0},{3,1},{4,6},{5,7},{6,4},{7,5},{8,10},{9,11},{10,... | collective-permute-start | bytes 884744 | tf_op jit(solution)/shard_map/ppermute | solution.py:23
  5.4 8.5 %collective-permute-start.10 = (bf16[128,1024]{1,0:T(8,128)(2,1)S(1)}, bf16[128,1024]{1,0:T(8,128)(2,1)S(1)}, u32[]{:S(2)}, u32[]{:S(2)}) collective-permute-start(bf16[128,1024]{1,0:T(8,128)(2,1)S(1)} %copy-done), channel_id=1, source_target_pairs={{2,4},{3,5},{4,2},{5,3},{10,12},{11,13},{12,10},{13,11},{18,20},{1... | collective-permute-start | bytes 786440 | tf_op jit(solution)/shard_map/ppermute | solution.py:297
  6.1 13.3 %collective-permute-start.12 = (bf16[144,1024]{1,0:T(8,128)(2,1)S(1)}, bf16[144,1024]{1,0:T(8,128)(2,1)S(1)}, u32[]{:S(2)}, u32[]{:S(2)}) collective-permute-start(bf16[144,1024]{1,0:T(8,128)(2,1)S(1)} %pad_maximum_fusion.refs_4_), channel_id=1, source_target_pairs={{2,4},{3,5},{4,2},{5,3},{10,12},{11,13},{12,10},{13,11},{18,20},{1... | collective-permute-start | bytes 884744 | tf_op jit(solution)/shard_map/ppermute | solution.py:297
  6.8 8.5 %collective-permute-start.1 = (bf16[128,1024]{1,0:T(8,128)(2,1)S(1)}, bf16[128,1024]{1,0:T(8,128)(2,1)S(1)}, u32[]{:S(2)}, u32[]{:S(2)}) collective-permute-start(bf16[128,1024]{1,0:T(8,128)(2,1)S(1)} %copy-done), channel_id=1, source_target_pairs={{0,16},{8,24},{16,0},{24,8},{1,17},{9,25},{17,1},{25,9},{2,18},{10... | collective-permute-start | bytes 786440 | tf_op jit(solution)/shard_map/ppermute | solution.py:23
  8.4 11.1 %collective-permute-start = (bf16[128,1024]{1,0:T(8,128)(2,1)S(1)}, bf16[128,1024]{1,0:T(8,128)(2,1)S(1)}, u32[]{:S(2)}, u32[]{:S(2)}) collective-permute-start(bf16[128,1024]{1,0:T(8,128)(2,1)S(1)} %copy-done), channel_id=1, source_target_pairs={{0,2},{1,3},{2,0},{3,1},{4,6},{5,7},{6,4},{7,5},{8,10},{9,11},{10,... | collective-permute-start | bytes 786440 | tf_op jit(solution)/shard_map/ppermute | solution.py:23
  14.0 6.2 %copy-start.5 = (bf16[128,1024]{1,0:T(8,128)(2,1)S(1)}, bf16[128,1024]{1,0:T(8,128)(2,1)}, u32[]{:S(2)}) copy-start(bf16[128,1024]{1,0:T(8,128)(2,1)} %param.4) | copy-start | bytes 786436
  14.0 7.6 %collective-permute-start.4 = (bf16[144,1024]{1,0:T(8,128)(2,1)S(1)}, bf16[144,1024]{1,0:T(8,128)(2,1)S(1)}, u32[]{:S(2)}, u32[]{:S(2)}) collective-permute-start(bf16[144,1024]{1,0:T(8,128)(2,1)S(1)} %pad_maximum_fusion.refs_4_), channel_id=1, source_target_pairs={{0,16},{8,24},{16,0},{24,8},{1,17},{9,25},{17,1},{25,9},{2,18},{10... | collective-permute-start | bytes 884744 | tf_op jit(solution)/shard_map/ppermute | solution.py:23
  14.5 9.2 %copy-start.1 = (bf16[144,1024]{1,0:T(8,128)(2,1)}, bf16[144,1024]{1,0:T(8,128)(2,1)S(1)}, u32[]{:S(2)}) copy-start(bf16[144,1024]{1,0:T(8,128)(2,1)S(1)} %collective-permute-done.3.refs_5_) | copy-start | bytes 884740
  14.5 7.9 %collective-permute-start.8 = (bf16[144,1024]{1,0:T(8,128)(2,1)S(1)}, bf16[144,1024]{1,0:T(8,128)(2,1)S(1)}, u32[]{:S(2)}, u32[]{:S(2)}) collective-permute-start(bf16[144,1024]{1,0:T(8,128)(2,1)S(1)} %collective-permute-done.3.refs_5_), channel_id=1, source_target_pairs={{2,4},{3,5},{4,2},{5,3},{10,12},{11,13},{12,10},{13,11},{18,20},{1... | collective-permute-start | bytes 884744 | tf_op jit(solution)/shard_map/ppermute | solution.py:301
  15.3 5.7 %copy-start.7 = (bf16[128,1024]{1,0:T(8,128)(2,1)}, bf16[128,1024]{1,0:T(8,128)(2,1)S(1)}, u32[]{:S(2)}) copy-start(bf16[128,1024]{1,0:T(8,128)(2,1)S(1)} %broadcast_select_fusion.2.refs_3_) | copy-start | bytes 786436
  15.3 5.7 %copy-start.17 = (bf16[128,1024]{1,0:T(8,128)(2,1)}, bf16[128,1024]{1,0:T(8,128)(2,1)S(1)}, u32[]{:S(2)}) copy-start(bf16[128,1024]{1,0:T(8,128)(2,1)S(1)} %collective-permute-done.1.refs_2_) | copy-start | bytes 786436
  15.3 7.2 %collective-permute-start.18 = (bf16[128,1024]{1,0:T(8,128)(2,1)S(1)}, bf16[128,1024]{1,0:T(8,128)(2,1)S(1)}, u32[]{:S(2)}, u32[]{:S(2)}) collective-permute-start(bf16[128,1024]{1,0:T(8,128)(2,1)S(1)} %broadcast_select_fusion.2.refs_3_), channel_id=1, source_target_pairs={{0,1},{1,0},{2,3},{3,2},{4,5},{5,4},{6,7},{7,6},{8,9},{9,8},{10,11... | collective-permute-start | bytes 786440 | tf_op jit(solution)/shard_map/ppermute | solution.py:23
  19.4 6.0 %copy-start.6 = (bf16[128,1024]{1,0:T(8,128)(2,1)}, bf16[128,1024]{1,0:T(8,128)(2,1)S(1)}, u32[]{:S(2)}) copy-start(bf16[128,1024]{1,0:T(8,128)(2,1)S(1)} %collective-permute-done.refs_1_) | copy-start | bytes 786436
  19.5 4.4 %collective-permute-start.11 = (bf16[128,1024]{1,0:T(8,128)(2,1)S(1)}, bf16[128,1024]{1,0:T(8,128)(2,1)}, u32[]{:S(2)}, u32[]{:S(2)}) collective-permute-start(bf16[128,1024]{1,0:T(8,128)(2,1)S(1)} %broadcast_select_fusion.2.refs_3_), channel_id=1, source_target_pairs={{0,8},{8,0},{16,24},{24,16},{1,9},{9,1},{17,25},{25,17},{2,10},{10... | collective-permute-start | bytes 786440 | tf_op jit(solution)/shard_map/ppermute | solution.py:23
  19.5 5.9 %collective-permute-start.6 = (bf16[128,1024]{1,0:T(8,128)(2,1)S(1)}, bf16[128,1024]{1,0:T(8,128)(2,1)S(1)}, u32[]{:S(2)}, u32[]{:S(2)}) collective-permute-start(bf16[128,1024]{1,0:T(8,128)(2,1)S(1)} %collective-permute-done.refs_1_), channel_id=1, source_target_pairs={{2,4},{3,5},{4,2},{5,3},{10,12},{11,13},{12,10},{13,11},{18,20},{1... | collective-permute-start | bytes 786440 | tf_op jit(solution)/shard_map/ppermute | solution.py:301
  21.6 2.2 %copy-start.11 = (bf16[144,1024]{1,0:T(8,128)(2,1)}, bf16[144,1024]{1,0:T(8,128)(2,1)S(1)}, u32[]{:S(2)}) copy-start(bf16[144,1024]{1,0:T(8,128)(2,1)S(1)} %collective-permute-done.4.refs_6_) | copy-start | bytes 884740
  21.6 9.2 %collective-permute-start.2 = (bf16[128,1024]{1,0:T(8,128)(2,1)S(1)}, bf16[128,1024]{1,0:T(8,128)(2,1)S(1)}, u32[]{:S(2)}, u32[]{:S(2)}) collective-permute-start(bf16[128,1024]{1,0:T(8,128)(2,1)S(1)} %collective-permute-done.refs_1_), channel_id=1, source_target_pairs={{0,16},{8,24},{16,0},{24,8},{1,17},{9,25},{17,1},{25,9},{2,18},{10... | collective-permute-start | bytes 786440 | tf_op jit(solution)/shard_map/ppermute | solution.py:23
  22.5 1.3 %copy-start.15 = (bf16[128,1024]{1,0:T(8,128)(2,1)}, bf16[128,1024]{1,0:T(8,128)(2,1)S(1)}, u32[]{:S(2)}) copy-start(bf16[128,1024]{1,0:T(8,128)(2,1)S(1)} %collective-permute-done.18.refs_3_) | copy-start | bytes 786436
  22.5 8.4 %collective-permute-start.13 = (bf16[144,1024]{1,0:T(8,128)(2,1)}, bf16[144,1024]{1,0:T(8,128)(2,1)S(1)}, u32[]{:S(2)}, u32[]{:S(2)}) collective-permute-start(bf16[144,1024]{1,0:T(8,128)(2,1)} %broadcast_select_fusion.refs_5_), channel_id=1, source_target_pairs={{0,8},{8,0},{16,24},{24,16},{1,9},{9,1},{17,25},{25,17},{2,10},{10... | collective-permute-start | bytes 884744 | tf_op jit(solution)/shard_map/ppermute | solution.py:23
  22.5 13.6 %collective-permute-start.5 = (bf16[144,1024]{1,0:T(8,128)(2,1)S(1)}, bf16[144,1024]{1,0:T(8,128)(2,1)S(1)}, u32[]{:S(2)}, u32[]{:S(2)}) collective-permute-start(bf16[144,1024]{1,0:T(8,128)(2,1)S(1)} %collective-permute-done.3.refs_5_), channel_id=1, source_target_pairs={{0,16},{8,24},{16,0},{24,8},{1,17},{9,25},{17,1},{25,9},{2,18},{10... | collective-permute-start | bytes 884744 | tf_op jit(solution)/shard_map/ppermute | solution.py:23
  23.8 7.0 %copy-start.2 = (bf16[144,1024]{1,0:T(8,128)(2,1)}, bf16[144,1024]{1,0:T(8,128)(2,1)S(1)}, u32[]{:S(2)}) copy-start(bf16[144,1024]{1,0:T(8,128)(2,1)S(1)} %broadcast_select_fusion.1.refs_5_) | copy-start | bytes 884740
  23.8 22.1 %collective-permute-start.20 = (bf16[144,1024]{1,0:T(8,128)(2,1)}, bf16[144,1024]{1,0:T(8,128)(2,1)S(1)}, u32[]{:S(2)}, u32[]{:S(2)}) collective-permute-start(bf16[144,1024]{1,0:T(8,128)(2,1)} %broadcast_select_fusion.refs_5_), channel_id=1, source_target_pairs={{0,1},{1,0},{2,3},{3,2},{4,5},{5,4},{6,7},{7,6},{8,9},{9,8},{10,11... | collective-permute-start | bytes 884744 | tf_op jit(solution)/shard_map/ppermute | solution.py:23
  25.4 21.1 %collective-permute-start.9 = (bf16[144,1024]{1,0:T(8,128)(2,1)S(1)}, bf16[144,1024]{1,0:T(8,128)(2,1)}, u32[]{:S(2)}, u32[]{:S(2)}) collective-permute-start(bf16[144,1024]{1,0:T(8,128)(2,1)S(1)} %broadcast_select_fusion.1.refs_5_), channel_id=1, source_target_pairs={{0,8},{8,0},{16,24},{24,16},{1,9},{9,1},{17,25},{25,17},{2,10},{10... | collective-permute-start | bytes 884744 | tf_op jit(solution)/shard_map/ppermute | solution.py:23
  25.4 16.5 %copy-start.4 = (bf16[128,1024]{1,0:T(8,128)(2,1)}, bf16[128,1024]{1,0:T(8,128)(2,1)S(1)}, u32[]{:S(2)}) copy-start(bf16[128,1024]{1,0:T(8,128)(2,1)S(1)} %broadcast_select_fusion.3.refs_3_) | copy-start | bytes 786436
  30.8 5.3 %copy-start.18 = (bf16[128,1024]{1,0:T(8,128)(2,1)}, bf16[128,1024]{1,0:T(8,128)(2,1)S(1)}, u32[]{:S(2)}) copy-start(bf16[128,1024]{1,0:T(8,128)(2,1)S(1)} %collective-permute-done.2.refs_3_) | copy-start | bytes 786436
  30.8 15.2 %collective-permute-start.7 = (bf16[128,1024]{1,0:T(8,128)(2,1)S(1)}, bf16[128,1024]{1,0:T(8,128)(2,1)}, u32[]{:S(2)}, u32[]{:S(2)}) collective-permute-start(bf16[128,1024]{1,0:T(8,128)(2,1)S(1)} %broadcast_select_fusion.3.refs_3_), channel_id=1, source_target_pairs={{0,8},{8,0},{16,24},{24,16},{1,9},{9,1},{17,25},{25,17},{2,10},{10... | collective-permute-start | bytes 786440 | tf_op jit(solution)/shard_map/ppermute | solution.py:23
  30.8 5.2 %copy-start.14 = (bf16[144,1024]{1,0:T(8,128)(2,1)}, bf16[144,1024]{1,0:T(8,128)(2,1)S(1)}, u32[]{:S(2)}) copy-start(bf16[144,1024]{1,0:T(8,128)(2,1)S(1)} %collective-permute-done.13.refs_6_) | copy-start | bytes 884740
  30.8 19.8 %collective-permute-start.15 = (bf16[144,1024]{1,0:T(8,128)(2,1)S(1)}, bf16[144,1024]{1,0:T(8,128)(2,1)}, u32[]{:S(2)}, u32[]{:S(2)}) collective-permute-start(bf16[144,1024]{1,0:T(8,128)(2,1)S(1)} %broadcast_select_fusion.1.refs_5_), channel_id=1, source_target_pairs={{0,1},{1,0},{2,3},{3,2},{4,5},{5,4},{6,7},{7,6},{8,9},{9,8},{10,11... | collective-permute-start | bytes 884744 | tf_op jit(solution)/shard_map/ppermute | solution.py:23
  36.8 13.8 %collective-permute-start.14 = (bf16[128,1024]{1,0:T(8,128)(2,1)S(1)}, bf16[128,1024]{1,0:T(8,128)(2,1)}, u32[]{:S(2)}, u32[]{:S(2)}) collective-permute-start(bf16[128,1024]{1,0:T(8,128)(2,1)S(1)} %broadcast_select_fusion.3.refs_3_), channel_id=1, source_target_pairs={{0,1},{1,0},{2,3},{3,2},{4,5},{5,4},{6,7},{7,6},{8,9},{9,8},{10,11... | collective-permute-start | bytes 786440 | tf_op jit(solution)/shard_map/ppermute | solution.py:23
  45.9 4.7 %copy-start.10 = (bf16[144,1024]{1,0:T(8,128)(2,1)}, bf16[144,1024]{1,0:T(8,128)(2,1)S(1)}, u32[]{:S(2)}) copy-start(bf16[144,1024]{1,0:T(8,128)(2,1)S(1)} %collective-permute-done.20.refs_5_) | copy-start | bytes 884740
  45.9 5.3 %collective-permute-start.19 = (bf16[128,1024]{1,0:T(8,128)(2,1)}, bf16[128,1024]{1,0:T(8,128)(2,1)}, u32[]{:S(2)}, u32[]{:S(2)}) collective-permute-start(bf16[128,1024]{1,0:T(8,128)(2,1)} %copy-done.15), channel_id=1, source_target_pairs={{0,8},{8,0},{16,24},{24,16},{1,9},{9,1},{17,25},{25,17},{2,10},{10... | collective-permute-start | bytes 786440 | tf_op jit(solution)/shard_map/ppermute | solution.py:23
  46.0 5.2 %collective-permute-start.21 = (bf16[144,1024]{1,0:T(8,128)(2,1)S(1)}, bf16[144,1024]{1,0:T(8,128)(2,1)}, u32[]{:S(2)}, u32[]{:S(2)}) collective-permute-start(bf16[144,1024]{1,0:T(8,128)(2,1)S(1)} %collective-permute-done.20.refs_5_), channel_id=1, source_target_pairs={{0,8},{8,0},{16,24},{24,16},{1,9},{9,1},{17,25},{25,17},{2,10},{10... | collective-permute-start | bytes 884744 | tf_op jit(solution)/shard_map/ppermute | solution.py:23
  50.6 4.7 %collective-permute-start.17 = (bf16[144,1024]{1,0:T(8,128)(2,1)}, bf16[144,1024]{1,0:T(8,128)(2,1)S(1)}, u32[]{:S(2)}, u32[]{:S(2)}) collective-permute-start(bf16[144,1024]{1,0:T(8,128)(2,1)} %collective-permute-done.15.refs_5_), channel_id=1, source_target_pairs={{0,8},{8,0},{16,24},{24,16},{1,9},{9,1},{17,25},{25,17},{2,10},{10... | collective-permute-start | bytes 884744 | tf_op jit(solution)/shard_map/ppermute | solution.py:23
  50.8 4.6 %collective-permute-start.16 = (bf16[128,1024]{1,0:T(8,128)(2,1)}, bf16[128,1024]{1,0:T(8,128)(2,1)S(1)}, u32[]{:S(2)}, u32[]{:S(2)}) collective-permute-start(bf16[128,1024]{1,0:T(8,128)(2,1)} %collective-permute-done.14.refs_3_), channel_id=1, source_target_pairs={{0,8},{8,0},{16,24},{24,16},{1,9},{9,1},{17,25},{25,17},{2,10},{10... | collective-permute-start | bytes 786440 | tf_op jit(solution)/shard_map/ppermute | solution.py:23
  62.5 8.2 %copy-start.19 = (f32[8,512]{1,0:T(8,128)S(1)}, f32[8,512]{1,0:T(8,128)}, u32[]{:S(2)}) copy-start(f32[8,512]{1,0:T(8,128)} %get-tuple-element.50.refs_1_) | copy-start | bytes 49156
  62.5 15.8 %all-to-all-start = ((f32[32,8,128]{2,1,0:T(8,128)}), f32[32,8,128]{2,1,0:T(8,128)S(1)}, u32[]{:S(2)}, u32[]{:S(2)}) async-start(f32[32,8,128]{2,1,0:T(8,128)} %bitcast.5), calls=%async_computation | async-start | bytes 262144 | tf_op jit(solution)/shard_map/all_to_all | solution.py:360
  70.8 4.7 %collective-permute-start.24 = (f32[8,512]{1,0:T(8,128)S(1)}, f32[8,512]{1,0:T(8,128)S(1)}, u32[]{:S(2)}, u32[]{:S(2)}) collective-permute-start(f32[8,512]{1,0:T(8,128)S(1)} %copy-done.19), channel_id=1, source_target_pairs={{0,18},{1,19},{2,16},{3,17},{4,22},{5,23},{6,20},{7,21},{8,26},{9,... | collective-permute-start | bytes 49160 | tf_op jit(solution)/shard_map/ppermute | solution.py:356
  73.3 3.8 %collective-permute-start.23 = (f32[8,512]{1,0:T(8,128)S(1)}, f32[8,512]{1,0:T(8,128)S(1)}, u32[]{:S(2)}, u32[]{:S(2)}) collective-permute-start(f32[8,512]{1,0:T(8,128)S(1)} %copy-done.19), channel_id=1, source_target_pairs={{0,16},{1,17},{2,18},{3,19},{4,20},{5,21},{6,22},{7,23},{8,24},{9,... | collective-permute-start | bytes 49160 | tf_op jit(solution)/shard_map/ppermute | solution.py:356
  73.9 3.8 %collective-permute-start.22 = (f32[8,512]{1,0:T(8,128)S(1)}, f32[8,512]{1,0:T(8,128)S(1)}, u32[]{:S(2)}, u32[]{:S(2)}) collective-permute-start(f32[8,512]{1,0:T(8,128)S(1)} %copy-done.19), channel_id=1, source_target_pairs={{0,2},{1,3},{2,0},{3,1},{4,6},{5,7},{6,4},{7,5},{8,10},{9,11},{10,... | collective-permute-start | bytes 49160 | tf_op jit(solution)/shard_map/ppermute | solution.py:356
  75.5 2.8 %copy-start.20 = (f32[8,512]{1,0:T(8,128)}, f32[8,512]{1,0:T(8,128)S(1)}, u32[]{:S(2)}) copy-start(f32[8,512]{1,0:T(8,128)S(1)} %collective-permute-done.24.refs_4_) | copy-start | bytes 49156
  84.6 16.0 %collective-permute-start.25 = (f32[128,1024]{1,0:T(8,128)}, f32[128,1024]{1,0:T(8,128)}, u32[]{:S(2)}, u32[]{:S(2)}) collective-permute-start(f32[128,1024]{1,0:T(8,128)} %grads.4), channel_id=1, source_target_pairs={{0,18},{1,19},{2,16},{3,17},{4,22},{5,23},{6,20},{7,21},{8,26},{9,... | collective-permute-start | bytes 1572872 | tf_op jit(solution)/shard_map/ppermute | solution.py:388
  89.2 5.3 %copy-start.8 = (f32[128,1024]{1,0:T(8,128)S(1)}, f32[128,1024]{1,0:T(8,128)}, u32[]{:S(2)}) copy-start(f32[128,1024]{1,0:T(8,128)} %grads.5) | copy-start | bytes 1572868
  93.0 18.4 %collective-permute-start.26 = (f32[128,1024]{1,0:T(8,128)}, f32[128,1024]{1,0:T(8,128)}, u32[]{:S(2)}, u32[]{:S(2)}) collective-permute-start(f32[128,1024]{1,0:T(8,128)} %grads.6), channel_id=1, source_target_pairs={{0,2},{1,3},{2,0},{3,1},{4,6},{5,7},{6,4},{7,5},{8,10},{9,11},{10,... | collective-permute-start | bytes 1572872 | tf_op jit(solution)/shard_map/ppermute | solution.py:388
  94.5 17.1 %collective-permute-start.27 = (f32[128,1024]{1,0:T(8,128)S(1)}, f32[128,1024]{1,0:T(8,128)}, u32[]{:S(2)}, u32[]{:S(2)}) collective-permute-start(f32[128,1024]{1,0:T(8,128)S(1)} %copy-done.8), channel_id=1, source_target_pairs={{0,16},{1,17},{2,18},{3,19},{4,20},{5,21},{6,22},{7,23},{8,24},{9,... | collective-permute-start | bytes 1572872 | tf_op jit(solution)/shard_map/ppermute | solution.py:388
  95.5 5.1 %copy-start.23 = (f32[8,128]{1,0:T(8,128)S(1)}, f32[8,128]{1,0:T(8,128)}, u32[]{:S(2)}) copy-start(f32[8,128]{1,0:T(8,128)} %get-tuple-element.74) | copy-start | bytes 12292
  101.3 13.0 %all-to-all-start.1 = ((f32[32,8,128]{2,1,0:T(8,128)}), f32[32,8,128]{2,1,0:T(8,128)S(1)}, u32[]{:S(2)}, u32[]{:S(2)}) async-start(f32[32,8,128]{2,1,0:T(8,128)} %broadcast_in_dim.15), calls=%async_computation.1 | async-start | bytes 262144 | tf_op jit(solution)/shard_map/all_to_all | solution.py:391
  (6 other events, 4.7 us)

commit v3 on v2

--- a/solution.py
+++ b/solution.py
@@ -13,7 +13,7 @@
 epsilon = 1e-06
 
 AXES = ("grp", "dev")
-EARLY = 2
+GROUP = 2
 PAD = 16
 VMEM_LIMIT = 63 * 1024 * 1024
 
@@ -50,21 +50,20 @@
 
 
 def call(kernel, out_shape, operands, flops=0, name=None, blocks=None):
-    specs = []
-    for i, item in enumerate(operands):
-        size, at = (blocks or {}).get(i, (item.shape[0], 0))
-        specs.append(
-            pl.BlockSpec((size, item.shape[1]), functools.partial(lambda at, step: (at, 0), at))
-        )
+    def spec(shape, given):
+        if given is None:
+            return pl.BlockSpec(shape, lambda step: (0, 0))
+        return pl.BlockSpec(*given)
+
     many = isinstance(out_shape, (tuple, list))
-    outs = tuple(out_shape) if many else (out_shape,)
-    out_specs = tuple(pl.BlockSpec(item.shape, lambda step: (0, 0)) for item in outs)
+    shapes = tuple(out_shape) if many else (out_shape,)
+    out_specs = tuple(spec(item.shape, None) for item in shapes)
     moved = sum(item.size * item.dtype.itemsize for item in operands)
     return pl.pallas_call(
         kernel,
-        out_shape=outs if many else out_shape,
+        out_shape=shapes if many else out_shape,
         grid=(1,),
-        in_specs=specs,
+        in_specs=[spec(item.shape, (blocks or {}).get(i)) for i, item in enumerate(operands)],
         out_specs=out_specs if many else out_specs[0],
         name=name,
         cost_estimate=pl.CostEstimate(flops=flops, bytes_accessed=moved, transcendentals=0),
@@ -106,21 +105,20 @@
         label_ref[place, :] = column_of(label_row(teachers[k], rows))
 
 
-def tile_kernel(count, rows, i, last, *refs):
+def tile_kernel(count, rows, i, n_blocks, last, *refs):
     unit_ref, teacher_ref, label_ref = refs[:3]
-    students, teachers = refs[3:5], refs[5:7]
-    rest = refs[7:]
+    students, teachers = refs[3 : 3 + n_blocks], refs[3 + n_blocks : 3 + 2 * n_blocks]
+    rest = refs[3 + 2 * n_blocks :]
     first = i == 0
     if not first:
         old_ref, rest = rest[0], rest[1:]
     anchor_ref, similar_ref, weight_ref, anchor_label_ref, stats_ref = rest[:5]
     teacher_units = []
-    for n in range(2):
-        anchor_ref[n * rows : (n + 1) * rows, :] = unit_of(students[n][...])
+    for n in range(n_blocks):
+        across = slice(n * rows, (n + 1) * rows)
+        anchor_ref[across, :] = unit_of(students[n][...])
         teacher_units.append(unit_of(teachers[n][0:rows, :]))
-        anchor_label_ref[:, n * rows : (n + 1) * rows] = jnp.broadcast_to(
-            label_row(teachers[n], rows), (8, rows)
-        )
+        anchor_label_ref[:, across] = jnp.broadcast_to(label_row(teachers[n], rows), (8, rows))
     similar_ref[...] = inner_rows(unit_ref[...], anchor_ref[...])
     weight_ref[...] = inner_rows(teacher_ref[...], jnp.concatenate(teacher_units, axis=0))
     row_at = lax.broadcasted_iota(jnp.int32, (rows, rows), 0)
@@ -128,11 +126,11 @@
     for k in range(count):
         down = slice(k * rows, (k + 1) * rows)
         totals = [jnp.zeros((rows, rows), jnp.float32)] * 6
-        for n in range(2):
+        for n in range(n_blocks):
             across = slice(n * rows, (n + 1) * rows)
             similar = similar_ref[down, across]
-            offset = jnp.where(key_id(k) == anchor_id(i, n), 0, rows)
-            distinct = row_at != lane_at - offset
+            same_block = key_id(k) == anchor_id((i * n_blocks + n) // 2, n % 2)
+            distinct = row_at != lane_at - jnp.where(same_block, 0, rows)
             rel_exp = jnp.where(distinct, jnp.exp((similar - 1.0) / temp_student), 0.0)
             weight = jnp.where(
                 distinct, jnp.exp((weight_ref[down, across] - 1.0) / temp_teacher), 0.0
@@ -157,6 +155,20 @@
         stats_ref[down, :] = stats
         if last:
             rest[5][:, down] = jnp.transpose(stats)[0:8, :]
+
+
+def payload_kernel(halves, members, rows, sums_ref, out_ref):
+    h, _, _, q, _ = place()
+    for half in range(halves):
+        both = []
+        for other in range(2):
+            block = (half ^ h) * 2 + (other ^ q)
+            values = sums_ref[:, pl.ds(pl.multiple_of(block * rows, rows), rows)]
+            both += [values[0:3], values[5:6]]
+        tile = jnp.concatenate(both, axis=0)
+        for d in range(2 * members):
+            at = (half * 2 * members + d) * 8
+            out_ref[at : at + 8, :] = tile
 
 
 def merge_kernel(dims, rows, *refs):
@@ -210,25 +222,25 @@
                 anchor_ref[:, at : at + rows] = value
 
 
-def grad_kernel(pairs, rows, k, *refs):
+def grad_kernel(tiles, rows, k, n_blocks, *refs):
     label_ref, key_ref, anchor_stats_ref = refs[:3]
     rest = refs[3:]
-    similar, weights, labels, units = (rest[i * pairs : (i + 1) * pairs] for i in range(4))
-    out_ref = rest[4 * pairs]
+    similar, weights, labels, units = (rest[i * tiles : (i + 1) * tiles] for i in range(4))
+    out_ref = rest[4 * tiles]
     row_at = lax.broadcasted_iota(jnp.int32, (rows, rows), 0)
     lane_at = lax.broadcasted_iota(jnp.int32, (rows, rows), 1)
     sup_key, rel_key, teacher_key, pos_key = (key_ref[:, i : i + 1] for i in range(4))
     total = None
-    for i in range(pairs):
+    for i in range(tiles):
         row_parts, column_parts = [], []
-        for n in range(2):
+        for n in range(n_blocks):
             across = slice(n * rows, (n + 1) * rows)
-            at = (i * 2 + n) * rows
+            at = (i * n_blocks + n) * rows
             sup_all, rel_all, teacher_all, pos_all = (
                 anchor_stats_ref[j : j + 1, at : at + rows] for j in range(4)
             )
-            offset = jnp.where(key_id(k) == anchor_id(i, n), 0, rows)
-            distinct = row_at != lane_at - offset
+            same_block = key_id(k) == anchor_id((i * n_blocks + n) // 2, n % 2)
+            distinct = row_at != lane_at - jnp.where(same_block, 0, rows)
             rel_exp = jnp.where(
                 distinct, jnp.exp((similar[i][:, across] - 1.0) / temp_student), 0.0
             )
@@ -253,27 +265,32 @@
         )
         part = jnp.dot(both, units[i][...], preferred_element_type=jnp.float32)
         total = part if total is None else total + part
-    out_ref[...] = total[0:rows] + total[rows : 2 * rows]
-
-
-def final_kernel(student_ref, *refs):
+    grad = total[0:rows] + total[rows : 2 * rows]
+    if k == 0:
+        out_ref[...] = grad
+        return
+    top = jnp.maximum(jnp.max(jnp.abs(grad), axis=1, keepdims=True), 2.0**-90)
+    power = jnp.floor(jnp.log2(top))
+    scaled = jnp.clip(jnp.floor(grad * jnp.exp2(14.0 - power) + 0.5), -32767.0, 32767.0)
+    out_ref[0:rows, :] = scaled.astype(jnp.int32).astype(jnp.int16)
+    out_ref[rows : rows + PAD, :] = jnp.zeros((PAD, out_ref.shape[1]), jnp.int16)
+    powers = jnp.transpose(jnp.broadcast_to(power, (rows, rows)))[0:PAD]
+    out_ref[rows : rows + PAD, 0:rows] = powers.astype(jnp.int32).astype(jnp.int16)
+
+
+def final_kernel(student_ref, own_ref, *refs):
     out_ref = refs[-1]
-    grad = refs[0][...]
-    for ref in refs[1:-1]:
-        grad = grad + ref[...]
+    rows = own_ref.shape[0]
+    grad = own_ref[...]
+    for ref in refs[:-1]:
+        powers = ref[rows : rows + PAD, 0:rows].astype(jnp.int32).astype(jnp.float32)
+        scale = jnp.exp2(column_of(powers[0:1])[:, 0:1] - 14.0)
+        grad = grad + ref[0:rows, :].astype(jnp.int32).astype(jnp.float32) * scale
     values = student_ref[...].astype(jnp.float32)
     scaling = lax.rsqrt(jnp.sum(values * values, axis=1, keepdims=True) + epsilon)
     unit = values * scaling
     along = jnp.sum(unit * grad, axis=1, keepdims=True)
     out_ref[...] = scaling * (grad - unit * along)
-
-
-def by_xor(value, axis, index):
-    for bit in bits_of(value.shape[axis]):
-        order = [i ^ bit for i in range(value.shape[axis])]
-        turned = jnp.concatenate([lax.slice_in_dim(value, i, i + 1, axis=axis) for i in order], axis=axis)
-        value = jnp.where((index & bit) != 0, turned, value)
-    return value
 
 
 def body(student, teacher, labels):
@@ -322,26 +339,29 @@
     )
     units, similar, weights, anchor_labels = [], [], [], []
     stats = None
-    for i in range(pair_count):
-        last = i == pair_count - 1
-        if i == EARLY:
-            held_stats, anchors[late] = lax.optimization_barrier((stats, anchors[late]))
-            stats = held_stats
+    n_blocks, tiles = 2 * GROUP, pair_count // GROUP
+    for i in range(tiles):
+        last = i == tiles - 1
+        if last:
+            stats, held = lax.optimization_barrier((stats, anchors[late][0]))
+            anchors[late] = (held, anchors[late][1])
             pairs.append((anchors[late], both(lambda v: swapped(v, "grp", 1), anchors[late])))
-        first, second = pairs[i]
+        chosen = [item for pair in pairs[i * GROUP : (i + 1) * GROUP] for item in pair]
         outs = call(
-            functools.partial(tile_kernel, key_count, rows, i, last),
+            functools.partial(tile_kernel, key_count, rows, i, n_blocks, last),
             (
-                b16((2 * rows, width)),
-                f32((key_rows, 2 * rows)),
-                f32((key_rows, 2 * rows)),
-                f32((8, 2 * rows)),
+                b16((n_blocks * rows, width)),
+                f32((key_rows, n_blocks * rows)),
+                f32((key_rows, n_blocks * rows)),
+                f32((8, n_blocks * rows)),
                 f32((key_rows, rows)),
             )
             + ((f32((8, key_rows)),) if last else ()),
-            [key_unit, key_teacher, key_label, first[0], second[0], first[1], second[1]]
+            [key_unit, key_teacher, key_label]
+            + [item[0] for item in chosen]
+            + [item[1] for item in chosen]
             + ([] if stats is None else [stats]),
-            flops=8 * key_rows * rows * width,
+            flops=4 * key_rows * n_blocks * rows * width,
             name="tile",
         )
         for held, value in zip((units, similar, weights, anchor_labels), outs[:4]):
@@ -354,9 +374,12 @@
         mask = (k // 2) * 2 * members + (k % 2) * quarter
         total = groups * members
         others.append(lax.ppermute(sums, AXES, [(i, i ^ mask) for i in range(total)]))
-    blocks = jnp.stack([sums[0], sums[1], sums[2], sums[5]]).reshape(4, halves, 2, rows)
-    blocks = by_xor(by_xor(blocks, 1, h), 2, q).transpose(1, 2, 0, 3).reshape(halves, 1, 8, rows)
-    payload = jnp.broadcast_to(blocks, (halves, 2 * members, 8, rows)).reshape(-1, rows)
+    payload = call(
+        functools.partial(payload_kernel, halves, members, rows),
+        f32((groups * members * 8, rows)),
+        [sums],
+        name="payload",
+    )
     received = lax.all_to_all(payload, AXES, 0, 0, tiled=True)
     anchor_stats, key_stats, loss = call(
         functools.partial(merge_kernel, (groups, members, key_count), rows),
@@ -366,13 +389,13 @@
     )
 
     def grads(k, key_stats):
-        blocks = {i: (rows, k) for i in (0, 1)}
-        for i in range(2 * pair_count):
-            blocks[3 + i] = (rows, k)
+        blocks = {i: ((rows, rows), lambda step: (k, 0)) for i in (0, 1)}
+        for i in range(2 * tiles):
+            blocks[3 + i] = ((rows, n_blocks * rows), lambda step: (k, 0))
         operands = [key_label, key_stats, anchor_stats] + similar + weights + anchor_labels + units
         return call(
-            functools.partial(grad_kernel, pair_count, rows, k),
-            f32((rows, width)),
+            functools.partial(grad_kernel, tiles, rows, k, n_blocks),
+            f32((rows, width)) if k == 0 else jax.ShapeDtypeStruct((rows + PAD, width), jnp.int16),
             operands,
             flops=4 * rows * members * rows * width,
             name="grads",
@@ -392,8 +415,13 @@
         jnp.broadcast_to(loss[None], (groups * members, 8, rows)).reshape(-1, rows), AXES, 0, 0, tiled=True
     ).reshape(groups * members, 8, rows)
     losses = jnp.sum(shared[:, 0:2, 0], axis=0) / (groups * members * rows)
+    shares = [student] + parts[::-1]
     feature_grad = call(
-        final_kernel, f32((rows, width)), [student] + parts[::-1], flops=8 * rows * width, name="final"
+        final_kernel,
+        f32((rows, width)),
+        shares,
+        flops=8 * rows * width,
+        name="final",
     )
     return (losses[0], losses[1], feature_grad)
 

time: 116 us -> 112 us (0.966)
  starting transfers between devices: 42.3 us -> 46.5 us
  waiting for transfers between devices: 24.1 us -> 20.3 us
  Pallas kernels: 39.3 us -> 35.6 us
    ppermute x3, waiting for transfers between devices: 7.8 us -> 0.01 us  [body(): lax.ppermute(part, AXES, [(i, i ^ mask) for i in range(groups * members)])]
    all_to_all x1, waiting for transfers between devices: 0.01 us -> 4.31 us  [body(): lax.all_to_all(jnp.broadcast_to(loss[None], (groups * members, 8, rows))....]
    pallas_call x11 -> x10, Pallas kernels: 39.3 us -> 35.6 us  [call(): pl.pallas_call(kernel, out_shape=shapes if many else out_shape, grid=(1,)...]
    ppermute x18, starting transfers between devices: 20.3 us -> 23.3 us  [swapped(): return lax.ppermute(value, axis, [(i, i ^ mask) for i in range(size)])]
    slice x4 -> x0, local copies, waits for them, and re-layouts: 1.45 us -> none  [the longest x1 0.72 us: body(): sums[5]]
    unnamed x48 -> x52, local copies, waits for them, and re-layouts: 2.25 us -> 3.46 us
  transfers between devices with their start and end apart: 30 -> 30, of which waited for: 11 -> 11; matrix products, arithmetic and copies ran while one was open for 1% -> 1% of each run, Pallas kernels for 26% -> 21%
where the time goes in v3:
time: 112 us
  starting transfers between devices  46.5 us (42%)
  Pallas kernels  35.6 us (32%)
  waiting for transfers between devices  20.3 us (18%)
  local copies, waits for them, and re-layouts  4.76 us (4%)
  other arithmetic  3.64 us (3%)
    pallas_call x10, Pallas kernels, call(): pl.pallas_call(kernel, out_shape=shapes if many else out_shape, grid=(1,)...  35.6 us
    ppermute x18, starting transfers between devices, swapped(): return lax.ppermute(value, axis, [(i, i ^ mask) for i in range(size)])  23.3 us
    ppermute x18, waiting for transfers between devices, swapped(): return lax.ppermute(value, axis, [(i, i ^ mask) for i in range(size)])  11.8 us
    all_to_all x1, starting transfers between devices, body(): received = lax.all_to_all(payload, AXES, 0, 0, tiled=True)  9.33 us
    all_to_all x1, waiting for transfers between devices, body(): lax.all_to_all(jnp.broadcast_to(loss[None], (groups * members, 8, rows))....  4.31 us
    all_to_all x1, starting transfers between devices, body(): lax.all_to_all(jnp.broadcast_to(loss[None], (groups * members, 8, rows))....  4.07 us
    ppermute x3, waiting for transfers between devices, body(): lax.ppermute(sums, AXES, [(i, i ^ mask) for i in range(total)])  3.56 us
    ppermute x3, starting transfers between devices, body(): lax.ppermute(sums, AXES, [(i, i ^ mask) for i in range(total)])  3.55 us
  transfers between devices with their start and end apart: 30, of which 11 were waited for; matrix products, arithmetic and copies ran while one was open for 1% of the time, Pallas kernels for 21%

profile of v3, /device:TPU:0, one launch (start us, length us, event | category | flops | bytes accessed | tf_op | source)
XLA Modules:
  0.0 111.8 jit_solution(1426910615255163488)
XLA Ops:
  0.6 0.7 convert_bitcast_fusion
  1.3 1.0 pad_maximum_fusion.refs_4_
  2.4 3.1 %collective-permute-start.3 = (bf16[144,1024]{1,0:T(8,128)(2,1)S(1)}, bf16[144,1024]{1,0:T(8,128)(2,1)S(1)}, u32[]{:S(2)}, u32[]{:S(2)}) collective-permute-start(bf16[144,1024]{1,0:T(8,128)(2,1)S(1)} %pad_maximum_fusion.refs_4_), channel_id=1, source_target_pairs={{0,2},{1,3},{2,0},{3,1},{4,6},{5,7},{6,4},{7,5},{8,10},{9,11},{10,... | collective-permute-start | bytes 884744 | tf_op jit(solution)/shard_map/ppermute | solution.py:23
  5.4 0.7 collective-permute-start.6
  6.1 0.7 collective-permute-start.12
  6.8 1.6 %collective-permute-start.4 = (bf16[144,1024]{1,0:T(8,128)(2,1)S(1)}, bf16[144,1024]{1,0:T(8,128)(2,1)S(1)}, u32[]{:S(2)}, u32[]{:S(2)}) collective-permute-start(bf16[144,1024]{1,0:T(8,128)(2,1)S(1)} %pad_maximum_fusion.refs_4_), channel_id=1, source_target_pairs={{0,16},{8,24},{16,0},{24,8},{1,17},{9,25},{17,1},{25,9},{2,18},{10... | collective-permute-start | bytes 884744 | tf_op jit(solution)/shard_map/ppermute | solution.py:23
  8.9 8.8 %collective-permute-start = (bf16[128,1024]{1,0:T(8,128)(2,1)S(1)}, bf16[128,1024]{1,0:T(8,128)(2,1)S(1)}, u32[]{:S(2)}, u32[]{:S(2)}) collective-permute-start(bf16[128,1024]{1,0:T(8,128)(2,1)S(1)} %copy-done), channel_id=1, source_target_pairs={{0,2},{1,3},{2,0},{3,1},{4,6},{5,7},{6,4},{7,5},{8,10},{9,11},{10,... | collective-permute-start | bytes 786440 | tf_op jit(solution)/shard_map/ppermute | solution.py:23
  17.7 0.8 collective-permute-start.14
  18.5 2.4 %collective-permute-done.1.refs_2_ = bf16[128,1024]{1,0:T(8,128)(2,1)S(1)} collective-permute-done((bf16[128,1024]{1,0:T(8,128)(2,1)S(1)}, bf16[128,1024]{1,0:T(8,128)(2,1)S(1)}, u32[]{:S(2)}, u32[]{:S(2)}) %collective-permute-start.1) | collective-permute-done | bytes 262176 | tf_op jit(solution)/shard_map/ppermute | solution.py:23
  21.0 1.0 collective-permute-done.refs_1_
  22.0 1.5 %collective-permute-start.7 = (bf16[128,1024]{1,0:T(8,128)(2,1)S(1)}, bf16[128,1024]{1,0:T(8,128)(2,1)S(1)}, u32[]{:S(2)}, u32[]{:S(2)}) collective-permute-start(bf16[128,1024]{1,0:T(8,128)(2,1)S(1)} %broadcast_select_fusion.3.refs_3_), channel_id=1, source_target_pairs={{0,1},{1,0},{2,3},{3,2},{4,5},{5,4},{6,7},{7,6},{8,9},{9,8},{10,11... | collective-permute-start | bytes 786440 | tf_op jit(solution)/shard_map/ppermute | solution.py:23
  23.5 0.7 collective-permute-start.10
  24.2 1.6 %collective-permute-start.2 = (bf16[128,1024]{1,0:T(8,128)(2,1)S(1)}, bf16[128,1024]{1,0:T(8,128)(2,1)S(1)}, u32[]{:S(2)}, u32[]{:S(2)}) collective-permute-start(bf16[128,1024]{1,0:T(8,128)(2,1)S(1)} %collective-permute-done.refs_1_), channel_id=1, source_target_pairs={{0,16},{8,24},{16,0},{24,8},{1,17},{9,25},{17,1},{25,9},{2,18},{10... | collective-permute-start | bytes 786440 | tf_op jit(solution)/shard_map/ppermute | solution.py:23
  26.5 0.7 broadcast_select_fusion.refs_9_
  27.3 3.9 %collective-permute-done.7.refs_3_ = bf16[128,1024]{1,0:T(8,128)(2,1)S(1)} collective-permute-done((bf16[128,1024]{1,0:T(8,128)(2,1)S(1)}, bf16[128,1024]{1,0:T(8,128)(2,1)S(1)}, u32[]{:S(2)}, u32[]{:S(2)}) %collective-permute-start.7) | collective-permute-done | bytes 262176 | tf_op jit(solution)/shard_map/ppermute | solution.py:23
  31.3 1.5 %collective-permute-start.5 = (bf16[144,1024]{1,0:T(8,128)(2,1)S(1)}, bf16[144,1024]{1,0:T(8,128)(2,1)S(1)}, u32[]{:S(2)}, u32[]{:S(2)}) collective-permute-start(bf16[144,1024]{1,0:T(8,128)(2,1)S(1)} %collective-permute-done.3.refs_5_), channel_id=1, source_target_pairs={{0,16},{8,24},{16,0},{24,8},{1,17},{9,25},{17,1},{25,9},{2,18},{10... | collective-permute-start | bytes 884744 | tf_op jit(solution)/shard_map/ppermute | solution.py:23
  32.8 1.5 %collective-permute-start.20 = (bf16[144,1024]{1,0:T(8,128)(2,1)}, bf16[144,1024]{1,0:T(8,128)(2,1)}, u32[]{:S(2)}, u32[]{:S(2)}) collective-permute-start(bf16[144,1024]{1,0:T(8,128)(2,1)} %broadcast_select_fusion.refs_9_), channel_id=1, source_target_pairs={{0,1},{1,0},{2,3},{3,2},{4,5},{5,4},{6,7},{7,6},{8,9},{9,8},{10,11... | collective-permute-start | bytes 884744 | tf_op jit(solution)/shard_map/ppermute | solution.py:23
  34.4 0.6 copy-done.19
  35.0 2.6 %collective-permute-done.18.refs_7_ = bf16[144,1024]{1,0:T(8,128)(2,1)S(1)} collective-permute-done((bf16[144,1024]{1,0:T(8,128)(2,1)S(1)}, bf16[144,1024]{1,0:T(8,128)(2,1)S(1)}, u32[]{:S(2)}, u32[]{:S(2)}) %collective-permute-start.18) | collective-permute-done | bytes 294944 | tf_op jit(solution)/shard_map/ppermute | solution.py:23
  38.0 0.7 copy-done.14
  38.7 1.5 %collective-permute-start.16 = (bf16[128,1024]{1,0:T(8,128)(2,1)S(1)}, bf16[128,1024]{1,0:T(8,128)(2,1)}, u32[]{:S(2)}, u32[]{:S(2)}) collective-permute-start(bf16[128,1024]{1,0:T(8,128)(2,1)S(1)} %broadcast_select_fusion.2.refs_5_), channel_id=1, source_target_pairs={{0,1},{1,0},{2,3},{3,2},{4,5},{5,4},{6,7},{7,6},{8,9},{9,8},{10,11... | collective-permute-start | bytes 786440 | tf_op jit(solution)/shard_map/ppermute | solution.py:23
  40.2 3.6 %keys.1 = (bf16[512,1024]{1,0:T(8,128)(2,1)}, bf16[512,1024]{1,0:T(8,128)(2,1)}, f32[512,128]{1,0:T(8,128)}) custom-call(bf16[128,1024]{1,0:T(8,128)(2,1)} %student_ref.1, bf16[128,1024]{1,0:T(8,128)(2,1)} %copy-done.5, bf16[128,1024]{1,0:T(8,128)(2,1)} %copy-done.16, bf16[128,1024]{1,0:T(8,128)(2,1)} %copy-done.19, bf16[144,1024]{1,0:T(8,128)(2,1)} %copy-done.3, ...), custom_call_target="tpu_custom_call" | custom-call | flops 4194304 | bytes 2228224 | tf_op jit(solution)/shard_map/keys/pallas_call | solution.py:62
  44.5 5.6 %tile.2 = (bf16[512,1024]{1,0:T(8,128)(2,1)}, f32[512,512]{1,0:T(8,128)}, f32[512,512]{1,0:T(8,128)}, f32[8,512]{1,0:T(8,128)}, f32[512,128]{1,0:T(8,128)}) custom-call(bf16[512,1024]{1,0:T(8,128)(2,1)} %get-tuple-element.30.refs_0_, bf16[512,1024]{1,0:T(8,128)(2,1)} %get-tuple-element.31.refs_1_, f32[512,128]{1,0:T(8,128)} %get-tuple-element.32.refs_2_.refs_0_, ...), custom_call_target="tpu_custom_call" | custom-call | flops 1073741824 | bytes 4587520 | tf_op jit(solution)/shard_map/tile/pallas_call | solution.py:62
  50.5 1.4 %collective-permute-done.17.refs_6_ = bf16[128,1024]{1,0:T(8,128)(2,1)S(1)} collective-permute-done((bf16[128,1024]{1,0:T(8,128)(2,1)}, bf16[128,1024]{1,0:T(8,128)(2,1)S(1)}, u32[]{:S(2)}, u32[]{:S(2)}) %collective-permute-start.17) | collective-permute-done | bytes 262176 | tf_op jit(solution)/shard_map/ppermute | solution.py:23
  51.9 0.7 copy-done.20
  52.6 5.6 %tile.3 = (bf16[512,1024]{1,0:T(8,128)(2,1)}, f32[512,512]{1,0:T(8,128)}, f32[512,512]{1,0:T(8,128)}, f32[8,512]{1,0:T(8,128)}, f32[512,128]{1,0:T(8,128)}, /*index=5*/f32[8,512]{1,0:T(8,128)}) custom-call(bf16[512,1024]{1,0:T(8,128)(2,1)} %get-tuple-element.30.refs_0_, bf16[512,1024]{1,0:T(8,128)(2,1)} %get-tuple-element.31.refs_1_, ...), custom_call_target="tpu_custom_call" | custom-call | flops 1073741824 | bytes 4849664 | tf_op jit(solution)/shard_map/tile/pallas_call | solution.py:62
  58.2 1.4 %payload.1 = f32[256,128]{1,0:T(8,128)} custom-call(f32[8,512]{1,0:T(8,128)} %get-tuple-element.36.sums_ref.refs_1_), custom_call_target="tpu_custom_call" | custom-call | bytes 16384 | tf_op jit(solution)/shard_map/payload/pallas_call | solution.py:62
  59.6 9.3 %all-to-all-start = ((f32[32,8,128]{2,1,0:T(8,128)}), f32[32,8,128]{2,1,0:T(8,128)S(1)}, u32[]{:S(2)}, u32[]{:S(2)}) async-start(f32[32,8,128]{2,1,0:T(8,128)} %bitcast.9), calls=%async_computation | async-start | bytes 262144 | tf_op jit(solution)/shard_map/all_to_all | solution.py:383
  69.0 2.7 %collective-permute-start.24 = (f32[8,512]{1,0:T(8,128)S(1)}, f32[8,512]{1,0:T(8,128)S(1)}, u32[]{:S(2)}, u32[]{:S(2)}) collective-permute-start(f32[8,512]{1,0:T(8,128)S(1)} %copy-done.21), channel_id=1, source_target_pairs={{0,18},{1,19},{2,16},{3,17},{4,22},{5,23},{6,20},{7,21},{8,26},{9,... | collective-permute-start | bytes 49160 | tf_op jit(solution)/shard_map/ppermute | solution.py:376
  72.5 1.4 %collective-permute-done.24.refs_4_ = f32[8,512]{1,0:T(8,128)S(1)} collective-permute-done((f32[8,512]{1,0:T(8,128)S(1)}, f32[8,512]{1,0:T(8,128)S(1)}, u32[]{:S(2)}, u32[]{:S(2)}) %collective-permute-start.24) | collective-permute-done | bytes 16416 | tf_op jit(solution)/shard_map/ppermute | solution.py:376
  73.9 1.7 %collective-permute-done.23.refs_3_ = f32[8,512]{1,0:T(8,128)S(1)} collective-permute-done((f32[8,512]{1,0:T(8,128)S(1)}, f32[8,512]{1,0:T(8,128)S(1)}, u32[]{:S(2)}, u32[]{:S(2)}) %collective-permute-start.23) | collective-permute-done | bytes 16416 | tf_op jit(solution)/shard_map/ppermute | solution.py:376
  76.1 0.6 all-to-all-done
  76.7 0.6 copy-done.8
  77.4 1.9 %merge.1 = (f32[8,1024]{1,0:T(8,128)}, f32[512,128]{1,0:T(8,128)}, f32[8,128]{1,0:T(8,128)}) custom-call(f32[256,128]{1,0:T(8,128)} %bitcast.8, f32[8,512]{1,0:T(8,128)} %get-tuple-element.36.sums_ref.refs_1_, f32[8,512]{1,0:T(8,128)} %copy-done.24, f32[8,512]{1,0:T(8,128)} %copy-done.23, f32[8,512]{1,0:T(8,128)} %copy-done.22), custom_call_target="tpu_custom_call" | custom-call | bytes 196608 | tf_op jit(solution)/shard_map/merge/pallas_call | solution.py:62
  79.2 3.8 %grads.4 = s16[144,1024]{1,0:T(8,128)(2,1)} custom-call(f32[512,128]{1,0:T(8,128)} %get-tuple-element.32.refs_2_.refs_0_, f32[512,128]{1,0:T(8,128)} %get-tuple-element.51.refs_1_, f32[8,1024]{1,0:T(8,128)} %get-tuple-element.39.refs_2_, f32[512,512]{1,0:T(8,128)} %get-tuple-element.40.refs_3_, f32[512,512]{1,0:T(8,128)} %get-tuple-element.41.refs_4_, ...), custom_call_target="tpu_custom_call" | custom-call | flops 536870912 | bytes 6881280 | tf_op jit(solution)/shard_map/grads/pallas_call | solution.py:62
  83.0 1.0 collective-permute-start.25
  84.0 3.7 %grads.5 = s16[144,1024]{1,0:T(8,128)(2,1)} custom-call(f32[512,128]{1,0:T(8,128)} %get-tuple-element.32.refs_2_.refs_0_, f32[512,128]{1,0:T(8,128)} %get-tuple-element.51.refs_1_, f32[8,1024]{1,0:T(8,128)} %get-tuple-element.39.refs_2_, f32[512,512]{1,0:T(8,128)} %get-tuple-element.40.refs_3_, f32[512,512]{1,0:T(8,128)} %get-tuple-element.41.refs_4_, ...), custom_call_target="tpu_custom_call" | custom-call | flops 536870912 | bytes 6881280 | tf_op jit(solution)/shard_map/grads/pallas_call | solution.py:62
  87.7 3.8 %grads.6 = s16[144,1024]{1,0:T(8,128)(2,1)} custom-call(f32[512,128]{1,0:T(8,128)} %get-tuple-element.32.refs_2_.refs_0_, f32[512,128]{1,0:T(8,128)} %get-tuple-element.51.refs_1_, f32[8,1024]{1,0:T(8,128)} %get-tuple-element.39.refs_2_, f32[512,512]{1,0:T(8,128)} %get-tuple-element.40.refs_3_, f32[512,512]{1,0:T(8,128)} %get-tuple-element.41.refs_4_, ...), custom_call_target="tpu_custom_call" | custom-call | flops 536870912 | bytes 6881280 | tf_op jit(solution)/shard_map/grads/pallas_call | solution.py:62
  91.5 1.6 %collective-permute-start.26 = (s16[144,1024]{1,0:T(8,128)(2,1)}, s16[144,1024]{1,0:T(8,128)(2,1)S(1)}, u32[]{:S(2)}, u32[]{:S(2)}) collective-permute-start(s16[144,1024]{1,0:T(8,128)(2,1)} %grads.6), channel_id=1, source_target_pairs={{0,2},{1,3},{2,0},{3,1},{4,6},{5,7},{6,4},{7,5},{8,10},{9,11},{10,... | collective-permute-start | bytes 884744 | tf_op jit(solution)/shard_map/ppermute | solution.py:411
  93.1 0.9 collective-permute-start.27
  94.0 3.6 %grads.7.own_ref = f32[128,1024]{1,0:T(8,128)} custom-call(f32[512,128]{1,0:T(8,128)} %get-tuple-element.32.refs_2_.refs_0_, f32[512,128]{1,0:T(8,128)} %get-tuple-element.51.refs_1_, f32[8,1024]{1,0:T(8,128)} %get-tuple-element.39.refs_2_, f32[512,512]{1,0:T(8,128)} %get-tuple-element.40.refs_3_, f32[512,512]{1,0:T(8,128)} %get-tuple-element.41.refs_4_, ...), custom_call_target="tpu_custom_call" | custom-call | flops 536870912 | bytes 6881280 | tf_op jit(solution)/shard_map/grads/pallas_call | solution.py:62
  97.7 0.7 broadcast_in_dim.2
  98.4 4.1 %all-to-all-start.1 = ((f32[32,8,128]{2,1,0:T(8,128)}), f32[32,8,128]{2,1,0:T(8,128)}, u32[]{:S(2)}, u32[]{:S(2)}) async-start(f32[32,8,128]{2,1,0:T(8,128)} %broadcast_in_dim.2), calls=%async_computation.1 | async-start | bytes 262144 | tf_op jit(solution)/shard_map/all_to_all | solution.py:414
  102.5 0.7 copy-done.15
  103.2 2.7 %final.1 = f32[128,1024]{1,0:T(8,128)} custom-call(bf16[128,1024]{1,0:T(8,128)(2,1)} %student_ref.1, f32[128,1024]{1,0:T(8,128)} %grads.7.own_ref, s16[144,1024]{1,0:T(8,128)(2,1)} %copy-done.15, s16[144,1024]{1,0:T(8,128)(2,1)} %collective-permute-done.27.refs_1_, s16[144,1024]{1,0:T(8,128)(2,1)} %copy-done.13), custom_call_target="tpu_custom_call" | custom-call | flops 1048576 | bytes 1671168 | tf_op jit(solution)/shard_map/final/pallas_call | solution.py:62
  105.8 4.3 %all-to-all-done.1 = f32[32,8,128]{2,1,0:T(8,128)} async-done(((f32[32,8,128]{2,1,0:T(8,128)}), f32[32,8,128]{2,1,0:T(8,128)}, u32[]{:S(2)}, u32[]{:S(2)}) %all-to-all-start.1) | async-done | bytes 131104 | tf_op jit(solution)/shard_map/all_to_all | solution.py:414
  110.2 1.1 slice_reduce_fusion
  111.2 0.6 fusion.8
  (85 shorter events, 4.4 us)
Async XLA Ops:
  1.3 4.1 %copy-start = (bf16[128,1024]{1,0:T(8,128)(2,1)S(1)}, bf16[128,1024]{1,0:T(8,128)(2,1)}, u32[]{:S(2)}) copy-start(bf16[128,1024]{1,0:T(8,128)(2,1)} %student_ref.1) | copy-start | bytes 786436
  2.3 16.2 %copy-start.3 = (bf16[144,1024]{1,0:T(8,128)(2,1)}, bf16[144,1024]{1,0:T(8,128)(2,1)S(1)}, u32[]{:S(2)}) copy-start(bf16[144,1024]{1,0:T(8,128)(2,1)S(1)} %pad_maximum_fusion.refs_4_) | copy-start | bytes 884740
  2.4 15.3 %collective-permute-start.3 = (bf16[144,1024]{1,0:T(8,128)(2,1)S(1)}, bf16[144,1024]{1,0:T(8,128)(2,1)S(1)}, u32[]{:S(2)}, u32[]{:S(2)}) collective-permute-start(bf16[144,1024]{1,0:T(8,128)(2,1)S(1)} %pad_maximum_fusion.refs_4_), channel_id=1, source_target_pairs={{0,2},{1,3},{2,0},{3,1},{4,6},{5,7},{6,4},{7,5},{8,10},{9,11},{10,... | collective-permute-start | bytes 884744 | tf_op jit(solution)/shard_map/ppermute | solution.py:23
  5.4 3.5 %collective-permute-start.6 = (bf16[128,1024]{1,0:T(8,128)(2,1)S(1)}, bf16[128,1024]{1,0:T(8,128)(2,1)S(1)}, u32[]{:S(2)}, u32[]{:S(2)}) collective-permute-start(bf16[128,1024]{1,0:T(8,128)(2,1)S(1)} %copy-done), channel_id=1, source_target_pairs={{2,4},{3,5},{4,2},{5,3},{10,12},{11,13},{12,10},{13,11},{18,20},{1... | collective-permute-start | bytes 786440 | tf_op jit(solution)/shard_map/ppermute | solution.py:314
  6.1 17.4 %collective-permute-start.12 = (bf16[144,1024]{1,0:T(8,128)(2,1)S(1)}, bf16[144,1024]{1,0:T(8,128)(2,1)S(1)}, u32[]{:S(2)}, u32[]{:S(2)}) collective-permute-start(bf16[144,1024]{1,0:T(8,128)(2,1)S(1)} %pad_maximum_fusion.refs_4_), channel_id=1, source_target_pairs={{2,4},{3,5},{4,2},{5,3},{10,12},{11,13},{12,10},{13,11},{18,20},{1... | collective-permute-start | bytes 884744 | tf_op jit(solution)/shard_map/ppermute | solution.py:314
  6.8 17.4 %collective-permute-start.4 = (bf16[144,1024]{1,0:T(8,128)(2,1)S(1)}, bf16[144,1024]{1,0:T(8,128)(2,1)S(1)}, u32[]{:S(2)}, u32[]{:S(2)}) collective-permute-start(bf16[144,1024]{1,0:T(8,128)(2,1)S(1)} %pad_maximum_fusion.refs_4_), channel_id=1, source_target_pairs={{0,16},{8,24},{16,0},{24,8},{1,17},{9,25},{17,1},{25,9},{2,18},{10... | collective-permute-start | bytes 884744 | tf_op jit(solution)/shard_map/ppermute | solution.py:23
  8.4 12.6 %collective-permute-start.1 = (bf16[128,1024]{1,0:T(8,128)(2,1)S(1)}, bf16[128,1024]{1,0:T(8,128)(2,1)S(1)}, u32[]{:S(2)}, u32[]{:S(2)}) collective-permute-start(bf16[128,1024]{1,0:T(8,128)(2,1)S(1)} %copy-done), channel_id=1, source_target_pairs={{0,16},{8,24},{16,0},{24,8},{1,17},{9,25},{17,1},{25,9},{2,18},{10... | collective-permute-start | bytes 786440 | tf_op jit(solution)/shard_map/ppermute | solution.py:23
  8.9 13.1 %collective-permute-start = (bf16[128,1024]{1,0:T(8,128)(2,1)S(1)}, bf16[128,1024]{1,0:T(8,128)(2,1)S(1)}, u32[]{:S(2)}, u32[]{:S(2)}) collective-permute-start(bf16[128,1024]{1,0:T(8,128)(2,1)S(1)} %copy-done), channel_id=1, source_target_pairs={{0,2},{1,3},{2,0},{3,1},{4,6},{5,7},{6,4},{7,5},{8,10},{9,11},{10,... | collective-permute-start | bytes 786440 | tf_op jit(solution)/shard_map/ppermute | solution.py:23
  17.7 8.1 %copy-start.4 = (bf16[128,1024]{1,0:T(8,128)(2,1)S(1)}, bf16[128,1024]{1,0:T(8,128)(2,1)}, u32[]{:S(2)}) copy-start(bf16[128,1024]{1,0:T(8,128)(2,1)} %param.4) | copy-start | bytes 786436
  17.7 13.6 %copy-start.1 = (bf16[144,1024]{1,0:T(8,128)(2,1)}, bf16[144,1024]{1,0:T(8,128)(2,1)S(1)}, u32[]{:S(2)}) copy-start(bf16[144,1024]{1,0:T(8,128)(2,1)S(1)} %collective-permute-done.3.refs_5_) | copy-start | bytes 884740
  17.7 8.2 %collective-permute-start.14 = (bf16[144,1024]{1,0:T(8,128)(2,1)S(1)}, bf16[144,1024]{1,0:T(8,128)(2,1)S(1)}, u32[]{:S(2)}, u32[]{:S(2)}) collective-permute-start(bf16[144,1024]{1,0:T(8,128)(2,1)S(1)} %collective-permute-done.3.refs_5_), channel_id=1, source_target_pairs={{2,4},{3,5},{4,2},{5,3},{10,12},{11,13},{12,10},{13,11},{18,20},{1... | collective-permute-start | bytes 884744 | tf_op jit(solution)/shard_map/ppermute | solution.py:318
  18.5 7.3 %copy-start.6 = (bf16[128,1024]{1,0:T(8,128)(2,1)}, bf16[128,1024]{1,0:T(8,128)(2,1)S(1)}, u32[]{:S(2)}) copy-start(bf16[128,1024]{1,0:T(8,128)(2,1)S(1)} %broadcast_select_fusion.3.refs_3_) | copy-start | bytes 786436
  21.0 6.3 %copy-start.16 = (bf16[128,1024]{1,0:T(8,128)(2,1)}, bf16[128,1024]{1,0:T(8,128)(2,1)S(1)}, u32[]{:S(2)}) copy-start(bf16[128,1024]{1,0:T(8,128)(2,1)S(1)} %collective-permute-done.1.refs_2_) | copy-start | bytes 786436
  21.0 6.3 %collective-permute-start.9 = (bf16[128,1024]{1,0:T(8,128)(2,1)S(1)}, bf16[128,1024]{1,0:T(8,128)(2,1)S(1)}, u32[]{:S(2)}, u32[]{:S(2)}) collective-permute-start(bf16[128,1024]{1,0:T(8,128)(2,1)S(1)} %broadcast_select_fusion.3.refs_3_), channel_id=1, source_target_pairs={{0,8},{8,0},{16,24},{24,16},{1,9},{9,1},{17,25},{25,17},{2,10},{10... | collective-permute-start | bytes 786440 | tf_op jit(solution)/shard_map/ppermute | solution.py:23
  22.0 12.3 %copy-start.5 = (bf16[128,1024]{1,0:T(8,128)(2,1)}, bf16[128,1024]{1,0:T(8,128)(2,1)S(1)}, u32[]{:S(2)}) copy-start(bf16[128,1024]{1,0:T(8,128)(2,1)S(1)} %collective-permute-done.refs_1_) | copy-start | bytes 786436
  22.0 9.2 %collective-permute-start.7 = (bf16[128,1024]{1,0:T(8,128)(2,1)S(1)}, bf16[128,1024]{1,0:T(8,128)(2,1)S(1)}, u32[]{:S(2)}, u32[]{:S(2)}) collective-permute-start(bf16[128,1024]{1,0:T(8,128)(2,1)S(1)} %broadcast_select_fusion.3.refs_3_), channel_id=1, source_target_pairs={{0,1},{1,0},{2,3},{3,2},{4,5},{5,4},{6,7},{7,6},{8,9},{9,8},{10,11... | collective-permute-start | bytes 786440 | tf_op jit(solution)/shard_map/ppermute | solution.py:23
  23.5 9.2 %collective-permute-start.10 = (bf16[128,1024]{1,0:T(8,128)(2,1)S(1)}, bf16[128,1024]{1,0:T(8,128)(2,1)S(1)}, u32[]{:S(2)}, u32[]{:S(2)}) collective-permute-start(bf16[128,1024]{1,0:T(8,128)(2,1)S(1)} %collective-permute-done.refs_1_), channel_id=1, source_target_pairs={{2,4},{3,5},{4,2},{5,3},{10,12},{11,13},{12,10},{13,11},{18,20},{1... | collective-permute-start | bytes 786440 | tf_op jit(solution)/shard_map/ppermute | solution.py:318
  24.2 1.7 %copy-start.10 = (bf16[144,1024]{1,0:T(8,128)(2,1)}, bf16[144,1024]{1,0:T(8,128)(2,1)S(1)}, u32[]{:S(2)}) copy-start(bf16[144,1024]{1,0:T(8,128)(2,1)S(1)} %collective-permute-done.4.refs_6_) | copy-start | bytes 884740
  24.2 10.1 %collective-permute-start.2 = (bf16[128,1024]{1,0:T(8,128)(2,1)S(1)}, bf16[128,1024]{1,0:T(8,128)(2,1)S(1)}, u32[]{:S(2)}, u32[]{:S(2)}) collective-permute-start(bf16[128,1024]{1,0:T(8,128)(2,1)S(1)} %collective-permute-done.refs_1_), channel_id=1, source_target_pairs={{0,16},{8,24},{16,0},{24,8},{1,17},{9,25},{17,1},{25,9},{2,18},{10... | collective-permute-start | bytes 786440 | tf_op jit(solution)/shard_map/ppermute | solution.py:23
  25.9 11.7 %collective-permute-start.18 = (bf16[144,1024]{1,0:T(8,128)(2,1)S(1)}, bf16[144,1024]{1,0:T(8,128)(2,1)S(1)}, u32[]{:S(2)}, u32[]{:S(2)}) collective-permute-start(bf16[144,1024]{1,0:T(8,128)(2,1)S(1)} %broadcast_select_fusion.1.refs_7_), channel_id=1, source_target_pairs={{0,1},{1,0},{2,3},{3,2},{4,5},{5,4},{6,7},{7,6},{8,9},{9,8},{10,11... | collective-permute-start | bytes 884744 | tf_op jit(solution)/shard_map/ppermute | solution.py:23
  27.2 7.1 %copy-start.18 = (bf16[128,1024]{1,0:T(8,128)(2,1)}, bf16[128,1024]{1,0:T(8,128)(2,1)S(1)}, u32[]{:S(2)}) copy-start(bf16[128,1024]{1,0:T(8,128)(2,1)S(1)} %collective-permute-done.9.refs_4_) | copy-start | bytes 786436
  27.3 16.6 %collective-permute-start.13 = (bf16[144,1024]{1,0:T(8,128)(2,1)S(1)}, bf16[144,1024]{1,0:T(8,128)(2,1)}, u32[]{:S(2)}, u32[]{:S(2)}) collective-permute-start(bf16[144,1024]{1,0:T(8,128)(2,1)S(1)} %broadcast_select_fusion.1.refs_7_), channel_id=1, source_target_pairs={{0,8},{8,0},{16,24},{24,16},{1,9},{9,1},{17,25},{25,17},{2,10},{10... | collective-permute-start | bytes 884744 | tf_op jit(solution)/shard_map/ppermute | solution.py:23
  31.3 3.1 %copy-start.17 = (bf16[128,1024]{1,0:T(8,128)(2,1)}, bf16[128,1024]{1,0:T(8,128)(2,1)S(1)}, u32[]{:S(2)}) copy-start(bf16[128,1024]{1,0:T(8,128)(2,1)S(1)} %collective-permute-done.7.refs_3_) | copy-start | bytes 786436
  31.3 6.7 %collective-permute-start.5 = (bf16[144,1024]{1,0:T(8,128)(2,1)S(1)}, bf16[144,1024]{1,0:T(8,128)(2,1)S(1)}, u32[]{:S(2)}, u32[]{:S(2)}) collective-permute-start(bf16[144,1024]{1,0:T(8,128)(2,1)S(1)} %collective-permute-done.3.refs_5_), channel_id=1, source_target_pairs={{0,16},{8,24},{16,0},{24,8},{1,17},{9,25},{17,1},{25,9},{2,18},{10... | collective-permute-start | bytes 884744 | tf_op jit(solution)/shard_map/ppermute | solution.py:23
  32.8 11.7 %collective-permute-start.20 = (bf16[144,1024]{1,0:T(8,128)(2,1)}, bf16[144,1024]{1,0:T(8,128)(2,1)}, u32[]{:S(2)}, u32[]{:S(2)}) collective-permute-start(bf16[144,1024]{1,0:T(8,128)(2,1)} %broadcast_select_fusion.refs_9_), channel_id=1, source_target_pairs={{0,1},{1,0},{2,3},{3,2},{4,5},{5,4},{6,7},{7,6},{8,9},{9,8},{10,11... | collective-permute-start | bytes 884744 | tf_op jit(solution)/shard_map/ppermute | solution.py:23
  34.3 10.2 %collective-permute-start.15 = (bf16[144,1024]{1,0:T(8,128)(2,1)}, bf16[144,1024]{1,0:T(8,128)(2,1)}, u32[]{:S(2)}, u32[]{:S(2)}) collective-permute-start(bf16[144,1024]{1,0:T(8,128)(2,1)} %broadcast_select_fusion.refs_9_), channel_id=1, source_target_pairs={{0,8},{8,0},{16,24},{24,16},{1,9},{9,1},{17,25},{25,17},{2,10},{10... | collective-permute-start | bytes 884744 | tf_op jit(solution)/shard_map/ppermute | solution.py:23
  35.0 8.8 %copy-start.7 = (bf16[128,1024]{1,0:T(8,128)(2,1)}, bf16[128,1024]{1,0:T(8,128)(2,1)S(1)}, u32[]{:S(2)}) copy-start(bf16[128,1024]{1,0:T(8,128)(2,1)S(1)} %broadcast_select_fusion.2.refs_5_) | copy-start | bytes 786436
  37.6 6.3 %copy-start.11 = (bf16[144,1024]{1,0:T(8,128)(2,1)}, bf16[144,1024]{1,0:T(8,128)(2,1)S(1)}, u32[]{:S(2)}) copy-start(bf16[144,1024]{1,0:T(8,128)(2,1)S(1)} %collective-permute-done.18.refs_7_) | copy-start | bytes 884740
  37.6 6.3 %collective-permute-start.11 = (bf16[128,1024]{1,0:T(8,128)(2,1)S(1)}, bf16[128,1024]{1,0:T(8,128)(2,1)}, u32[]{:S(2)}, u32[]{:S(2)}) collective-permute-start(bf16[128,1024]{1,0:T(8,128)(2,1)S(1)} %broadcast_select_fusion.2.refs_5_), channel_id=1, source_target_pairs={{0,8},{8,0},{16,24},{24,16},{1,9},{9,1},{17,25},{25,17},{2,10},{10... | collective-permute-start | bytes 786440 | tf_op jit(solution)/shard_map/ppermute | solution.py:23
  38.7 11.4 %collective-permute-start.16 = (bf16[128,1024]{1,0:T(8,128)(2,1)S(1)}, bf16[128,1024]{1,0:T(8,128)(2,1)}, u32[]{:S(2)}, u32[]{:S(2)}) collective-permute-start(bf16[128,1024]{1,0:T(8,128)(2,1)S(1)} %broadcast_select_fusion.2.refs_5_), channel_id=1, source_target_pairs={{0,1},{1,0},{2,3},{3,2},{4,5},{5,4},{6,7},{7,6},{8,9},{9,8},{10,11... | collective-permute-start | bytes 786440 | tf_op jit(solution)/shard_map/ppermute | solution.py:23
  43.8 6.7 %collective-permute-start.8 = (bf16[128,1024]{1,0:T(8,128)(2,1)}, bf16[128,1024]{1,0:T(8,128)(2,1)}, u32[]{:S(2)}, u32[]{:S(2)}) collective-permute-start(bf16[128,1024]{1,0:T(8,128)(2,1)} %copy-done.17), channel_id=1, source_target_pairs={{0,8},{8,0},{16,24},{24,16},{1,9},{9,1},{17,25},{25,17},{2,10},{10... | collective-permute-start | bytes 786440 | tf_op jit(solution)/shard_map/ppermute | solution.py:23
  43.9 6.6 %collective-permute-start.19 = (bf16[144,1024]{1,0:T(8,128)(2,1)S(1)}, bf16[144,1024]{1,0:T(8,128)(2,1)S(1)}, u32[]{:S(2)}, u32[]{:S(2)}) collective-permute-start(bf16[144,1024]{1,0:T(8,128)(2,1)S(1)} %collective-permute-done.18.refs_7_), channel_id=1, source_target_pairs={{0,8},{8,0},{16,24},{24,16},{1,9},{9,1},{17,25},{25,17},{2,10},{10... | collective-permute-start | bytes 884744 | tf_op jit(solution)/shard_map/ppermute | solution.py:23
  44.4 7.5 %collective-permute-start.21 = (bf16[144,1024]{1,0:T(8,128)(2,1)}, bf16[144,1024]{1,0:T(8,128)(2,1)}, u32[]{:S(2)}, u32[]{:S(2)}) collective-permute-start(bf16[144,1024]{1,0:T(8,128)(2,1)} %collective-permute-done.20.refs_9_), channel_id=1, source_target_pairs={{0,8},{8,0},{16,24},{24,16},{1,9},{9,1},{17,25},{25,17},{2,10},{10... | collective-permute-start | bytes 884744 | tf_op jit(solution)/shard_map/ppermute | solution.py:23
  50.1 1.8 %collective-permute-start.17 = (bf16[128,1024]{1,0:T(8,128)(2,1)}, bf16[128,1024]{1,0:T(8,128)(2,1)S(1)}, u32[]{:S(2)}, u32[]{:S(2)}) collective-permute-start(bf16[128,1024]{1,0:T(8,128)(2,1)} %collective-permute-done.16.refs_5_), channel_id=1, source_target_pairs={{0,8},{8,0},{16,24},{24,16},{1,9},{9,1},{17,25},{25,17},{2,10},{10... | collective-permute-start | bytes 786440 | tf_op jit(solution)/shard_map/ppermute | solution.py:23
  50.5 1.4 %copy-start.12 = (bf16[144,1024]{1,0:T(8,128)(2,1)}, bf16[144,1024]{1,0:T(8,128)(2,1)S(1)}, u32[]{:S(2)}) copy-start(bf16[144,1024]{1,0:T(8,128)(2,1)S(1)} %collective-permute-done.19.refs_8_) | copy-start | bytes 884740
  59.6 9.3 %copy-start.21 = (f32[8,512]{1,0:T(8,128)S(1)}, f32[8,512]{1,0:T(8,128)}, u32[]{:S(2)}) copy-start(f32[8,512]{1,0:T(8,128)} %get-tuple-element.36.sums_ref.refs_1_) | copy-start | bytes 49156
  59.6 17.1 %all-to-all-start = ((f32[32,8,128]{2,1,0:T(8,128)}), f32[32,8,128]{2,1,0:T(8,128)S(1)}, u32[]{:S(2)}, u32[]{:S(2)}) async-start(f32[32,8,128]{2,1,0:T(8,128)} %bitcast.9), calls=%async_computation | async-start | bytes 262144 | tf_op jit(solution)/shard_map/all_to_all | solution.py:383
  69.0 4.9 %collective-permute-start.24 = (f32[8,512]{1,0:T(8,128)S(1)}, f32[8,512]{1,0:T(8,128)S(1)}, u32[]{:S(2)}, u32[]{:S(2)}) collective-permute-start(f32[8,512]{1,0:T(8,128)S(1)} %copy-done.21), channel_id=1, source_target_pairs={{0,18},{1,19},{2,16},{3,17},{4,22},{5,23},{6,20},{7,21},{8,26},{9,... | collective-permute-start | bytes 49160 | tf_op jit(solution)/shard_map/ppermute | solution.py:376
  71.7 3.8 %collective-permute-start.23 = (f32[8,512]{1,0:T(8,128)S(1)}, f32[8,512]{1,0:T(8,128)S(1)}, u32[]{:S(2)}, u32[]{:S(2)}) collective-permute-start(f32[8,512]{1,0:T(8,128)S(1)} %copy-done.21), channel_id=1, source_target_pairs={{0,16},{1,17},{2,18},{3,19},{4,20},{5,21},{6,22},{7,23},{8,24},{9,... | collective-permute-start | bytes 49160 | tf_op jit(solution)/shard_map/ppermute | solution.py:376
  72.3 3.8 %collective-permute-start.22 = (f32[8,512]{1,0:T(8,128)S(1)}, f32[8,512]{1,0:T(8,128)S(1)}, u32[]{:S(2)}, u32[]{:S(2)}) collective-permute-start(f32[8,512]{1,0:T(8,128)S(1)} %copy-done.21), channel_id=1, source_target_pairs={{0,2},{1,3},{2,0},{3,1},{4,6},{5,7},{6,4},{7,5},{8,10},{9,11},{10,... | collective-permute-start | bytes 49160 | tf_op jit(solution)/shard_map/ppermute | solution.py:376
  73.9 2.8 %copy-start.22 = (f32[8,512]{1,0:T(8,128)}, f32[8,512]{1,0:T(8,128)S(1)}, u32[]{:S(2)}) copy-start(f32[8,512]{1,0:T(8,128)S(1)} %collective-permute-done.24.refs_4_) | copy-start | bytes 49156
  83.0 14.7 %collective-permute-start.25 = (s16[144,1024]{1,0:T(8,128)(2,1)}, s16[144,1024]{1,0:T(8,128)(2,1)S(1)}, u32[]{:S(2)}, u32[]{:S(2)}) collective-permute-start(s16[144,1024]{1,0:T(8,128)(2,1)} %grads.4), channel_id=1, source_target_pairs={{0,18},{1,19},{2,16},{3,17},{4,22},{5,23},{6,20},{7,21},{8,26},{9,... | collective-permute-start | bytes 884744 | tf_op jit(solution)/shard_map/ppermute | solution.py:411
  87.7 5.4 %copy-start.9 = (s16[144,1024]{1,0:T(8,128)(2,1)S(1)}, s16[144,1024]{1,0:T(8,128)(2,1)}, u32[]{:S(2)}) copy-start(s16[144,1024]{1,0:T(8,128)(2,1)} %grads.5) | copy-start | bytes 884740
  91.5 10.9 %collective-permute-start.26 = (s16[144,1024]{1,0:T(8,128)(2,1)}, s16[144,1024]{1,0:T(8,128)(2,1)S(1)}, u32[]{:S(2)}, u32[]{:S(2)}) collective-permute-start(s16[144,1024]{1,0:T(8,128)(2,1)} %grads.6), channel_id=1, source_target_pairs={{0,2},{1,3},{2,0},{3,1},{4,6},{5,7},{6,4},{7,5},{8,10},{9,11},{10,... | collective-permute-start | bytes 884744 | tf_op jit(solution)/shard_map/ppermute | solution.py:411
  93.1 9.4 %collective-permute-start.27 = (s16[144,1024]{1,0:T(8,128)(2,1)S(1)}, s16[144,1024]{1,0:T(8,128)(2,1)}, u32[]{:S(2)}, u32[]{:S(2)}) collective-permute-start(s16[144,1024]{1,0:T(8,128)(2,1)S(1)} %copy-done.9), channel_id=1, source_target_pairs={{0,16},{1,17},{2,18},{3,19},{4,20},{5,21},{6,22},{7,23},{8,24},{9,... | collective-permute-start | bytes 884744 | tf_op jit(solution)/shard_map/ppermute | solution.py:411
  94.0 3.6 %copy-start.25 = (f32[8,128]{1,0:T(8,128)S(1)}, f32[8,128]{1,0:T(8,128)}, u32[]{:S(2)}) copy-start(f32[8,128]{1,0:T(8,128)} %get-tuple-element.52) | copy-start | bytes 12292
  97.6 4.8 %copy-start.13 = (s16[144,1024]{1,0:T(8,128)(2,1)}, s16[144,1024]{1,0:T(8,128)(2,1)S(1)}, u32[]{:S(2)}) copy-start(s16[144,1024]{1,0:T(8,128)(2,1)S(1)} %collective-permute-done.25.refs_2_) | copy-start | bytes 884740
  98.4 11.8 %all-to-all-start.1 = ((f32[32,8,128]{2,1,0:T(8,128)}), f32[32,8,128]{2,1,0:T(8,128)}, u32[]{:S(2)}, u32[]{:S(2)}) async-start(f32[32,8,128]{2,1,0:T(8,128)} %broadcast_in_dim.2), calls=%async_computation.1 | async-start | bytes 262144 | tf_op jit(solution)/shard_map/all_to_all | solution.py:414
  (8 other events, 6.6 us)

commit v4 on v3

--- a/solution.py
+++ b/solution.py
@@ -34,7 +34,7 @@
 
 
 def label_row(block, rows):
-    tail = block[rows : rows + PAD, 0:rows].astype(jnp.float32)
+    tail = block[2 * rows : 2 * rows + PAD, 0:rows].astype(jnp.float32)
     return tail[0:1] * 256.0 + tail[1:2]
 
 
@@ -96,19 +96,18 @@
 
 
 def keys_kernel(count, rows, *refs):
-    students, teachers = refs[:count], refs[count : 2 * count]
-    unit_ref, teacher_ref, label_ref = refs[2 * count :]
+    blocks = refs[:count]
+    unit_ref, teacher_ref, label_ref = refs[count:]
     for k in range(count):
         place = slice(k * rows, (k + 1) * rows)
-        unit_ref[place, :] = unit_of(students[k][...])
-        teacher_ref[place, :] = unit_of(teachers[k][0:rows, :])
-        label_ref[place, :] = column_of(label_row(teachers[k], rows))
+        unit_ref[place, :] = unit_of(blocks[k][0:rows, :])
+        teacher_ref[place, :] = unit_of(blocks[k][rows : 2 * rows, :])
+        label_ref[place, :] = column_of(label_row(blocks[k], rows))
 
 
 def tile_kernel(count, rows, i, n_blocks, last, *refs):
     unit_ref, teacher_ref, label_ref = refs[:3]
-    students, teachers = refs[3 : 3 + n_blocks], refs[3 + n_blocks : 3 + 2 * n_blocks]
-    rest = refs[3 + 2 * n_blocks :]
+    blocks, rest = refs[3 : 3 + n_blocks], refs[3 + n_blocks :]
     first = i == 0
     if not first:
         old_ref, rest = rest[0], rest[1:]
@@ -116,9 +115,9 @@
     teacher_units = []
     for n in range(n_blocks):
         across = slice(n * rows, (n + 1) * rows)
-        anchor_ref[across, :] = unit_of(students[n][...])
-        teacher_units.append(unit_of(teachers[n][0:rows, :]))
-        anchor_label_ref[:, across] = jnp.broadcast_to(label_row(teachers[n], rows), (8, rows))
+        anchor_ref[across, :] = unit_of(blocks[n][0:rows, :])
+        teacher_units.append(unit_of(blocks[n][rows : 2 * rows, :]))
+        anchor_label_ref[:, across] = jnp.broadcast_to(label_row(blocks[n], rows), (8, rows))
     similar_ref[...] = inner_rows(unit_ref[...], anchor_ref[...])
     weight_ref[...] = inner_rows(teacher_ref[...], jnp.concatenate(teacher_units, axis=0))
     row_at = lax.broadcasted_iota(jnp.int32, (rows, rows), 0)
@@ -222,60 +221,66 @@
                 anchor_ref[:, at : at + rows] = value
 
 
-def grad_kernel(tiles, rows, k, n_blocks, *refs):
+def grad_kernel(tiles, rows, chosen, n_blocks, *refs):
     label_ref, key_ref, anchor_stats_ref = refs[:3]
     rest = refs[3:]
     similar, weights, labels, units = (rest[i * tiles : (i + 1) * tiles] for i in range(4))
-    out_ref = rest[4 * tiles]
+    outs = rest[4 * tiles :]
     row_at = lax.broadcasted_iota(jnp.int32, (rows, rows), 0)
     lane_at = lax.broadcasted_iota(jnp.int32, (rows, rows), 1)
-    sup_key, rel_key, teacher_key, pos_key = (key_ref[:, i : i + 1] for i in range(4))
     total = None
     for i in range(tiles):
-        row_parts, column_parts = [], []
-        for n in range(n_blocks):
-            across = slice(n * rows, (n + 1) * rows)
-            at = (i * n_blocks + n) * rows
-            sup_all, rel_all, teacher_all, pos_all = (
-                anchor_stats_ref[j : j + 1, at : at + rows] for j in range(4)
-            )
-            same_block = key_id(k) == anchor_id((i * n_blocks + n) // 2, n % 2)
-            distinct = row_at != lane_at - jnp.where(same_block, 0, rows)
-            rel_exp = jnp.where(
-                distinct, jnp.exp((similar[i][:, across] - 1.0) / temp_student), 0.0
-            )
-            sup_exp = rel_exp * rel_exp
-            weight = weights[i][:, across]
-            same = label_ref[...] == labels[i][0:1, across]
-            positive = jnp.where(jnp.logical_and(same, distinct), 1.0, 0.0)
-            row_parts.append(
-                (
-                    (sup_exp * sup_key - positive * pos_key)
-                    + (rel_exp * rel_key - weight * teacher_key)
-                ).astype(jnp.bfloat16)
-            )
-            column_parts.append(
-                (
-                    (sup_exp * sup_all - positive * pos_all)
-                    + (rel_exp * rel_all - weight * teacher_all)
-                ).astype(jnp.bfloat16)
-            )
-        both = jnp.concatenate(
-            [jnp.concatenate(row_parts, axis=1), jnp.concatenate(column_parts, axis=1)], axis=0
+        lines = []
+        for j, k in enumerate(chosen):
+            down = slice(j * rows, (j + 1) * rows)
+            sup_key, rel_key, teacher_key, pos_key = (key_ref[down, f : f + 1] for f in range(4))
+            row_parts, column_parts = [], []
+            for n in range(n_blocks):
+                across = slice(n * rows, (n + 1) * rows)
+                at = (i * n_blocks + n) * rows
+                sup_all, rel_all, teacher_all, pos_all = (
+                    anchor_stats_ref[f : f + 1, at : at + rows] for f in range(4)
+                )
+                same_block = key_id(k) == anchor_id((i * n_blocks + n) // 2, n % 2)
+                distinct = row_at != lane_at - jnp.where(same_block, 0, rows)
+                rel_exp = jnp.where(
+                    distinct, jnp.exp((similar[i][down, across] - 1.0) / temp_student), 0.0
+                )
+                sup_exp = rel_exp * rel_exp
+                weight = weights[i][down, across]
+                same = label_ref[down, :] == labels[i][0:1, across]
+                positive = jnp.where(jnp.logical_and(same, distinct), 1.0, 0.0)
+                row_parts.append(
+                    (
+                        (sup_exp * sup_key - positive * pos_key)
+                        + (rel_exp * rel_key - weight * teacher_key)
+                    ).astype(jnp.bfloat16)
+                )
+                column_parts.append(
+                    (
+                        (sup_exp * sup_all - positive * pos_all)
+                        + (rel_exp * rel_all - weight * teacher_all)
+                    ).astype(jnp.bfloat16)
+                )
+            lines += [jnp.concatenate(row_parts, axis=1), jnp.concatenate(column_parts, axis=1)]
+        part = jnp.dot(
+            jnp.concatenate(lines, axis=0), units[i][...], preferred_element_type=jnp.float32
         )
-        part = jnp.dot(both, units[i][...], preferred_element_type=jnp.float32)
         total = part if total is None else total + part
-    grad = total[0:rows] + total[rows : 2 * rows]
-    if k == 0:
-        out_ref[...] = grad
-        return
-    top = jnp.maximum(jnp.max(jnp.abs(grad), axis=1, keepdims=True), 2.0**-90)
-    power = jnp.floor(jnp.log2(top))
-    scaled = jnp.clip(jnp.floor(grad * jnp.exp2(14.0 - power) + 0.5), -32767.0, 32767.0)
-    out_ref[0:rows, :] = scaled.astype(jnp.int32).astype(jnp.int16)
-    out_ref[rows : rows + PAD, :] = jnp.zeros((PAD, out_ref.shape[1]), jnp.int16)
-    powers = jnp.transpose(jnp.broadcast_to(power, (rows, rows)))[0:PAD]
-    out_ref[rows : rows + PAD, 0:rows] = powers.astype(jnp.int32).astype(jnp.int16)
+    for j, k in enumerate(chosen):
+        at = 2 * j * rows
+        grad = total[at : at + rows] + total[at + rows : at + 2 * rows]
+        out_ref = outs[j]
+        if k == 0:
+            out_ref[...] = grad
+            continue
+        top = jnp.maximum(jnp.max(jnp.abs(grad), axis=1, keepdims=True), 2.0**-90)
+        power = jnp.floor(jnp.log2(top))
+        scaled = jnp.clip(jnp.floor(grad * jnp.exp2(14.0 - power) + 0.5), -32767.0, 32767.0)
+        out_ref[0:rows, :] = scaled.astype(jnp.int32).astype(jnp.int16)
+        out_ref[rows : rows + PAD, :] = jnp.zeros((PAD, out_ref.shape[1]), jnp.int16)
+        powers = jnp.transpose(jnp.broadcast_to(power, (rows, rows)))[0:PAD]
+        out_ref[rows : rows + PAD, 0:rows] = powers.astype(jnp.int32).astype(jnp.int16)
 
 
 def final_kernel(student_ref, own_ref, *refs):
@@ -293,6 +298,11 @@
     out_ref[...] = scaling * (grad - unit * along)
 
 
+def ordered(items, at, value):
+    first, value = lax.optimization_barrier((items[at], value))
+    return items[:at] + [first] + items[at + 1 :], value
+
+
 def body(student, teacher, labels):
     rows, width = student.shape
     groups, members = lax.axis_size("grp"), lax.axis_size("dev")
@@ -305,25 +315,21 @@
 
     digits = jnp.stack([labels // 256, labels % 256]).astype(jnp.bfloat16)
     tail = jnp.pad(digits, ((0, PAD - 2), (0, width - rows)))
-    own = (student, jnp.concatenate([teacher, tail], axis=0))
-
-    def both(move, block):
-        return tuple(move(part) for part in block)
-
-    near = both(lambda v: swapped(v, "dev", quarter), own)
-    crossed = both(lambda v: lax.ppermute(v, "dev", cross), own)
+    own = jnp.concatenate([student, teacher, tail], axis=0)
+
+    near = swapped(own, "dev", quarter)
+    crossed = lax.ppermute(own, "dev", cross)
     keys = [own, near]
     for bit in bits_of(halves):
-        keys = keys + [both(lambda v: swapped(v, "grp", 2 * bit), item) for item in keys]
-    far = both(lambda v: lax.ppermute(v, "dev", cross), near)
-    anchors = [
-        tuple(jnp.where(inner, a, b) for a, b in zip(crossed, own)),
-        tuple(jnp.where(inner, a, b) for a, b in zip(far, near)),
-    ]
+        keys = keys + [swapped(item, "grp", 2 * bit) for item in keys]
+    far = lax.ppermute(near, "dev", cross)
+    keys, far = ordered(keys, 2, far)
+    anchors = [jnp.where(inner, crossed, own), jnp.where(inner, far, near)]
     for bit in bits_of(quarter):
-        anchors = anchors + [both(lambda v: swapped(v, "dev", bit), item) for item in anchors]
+        anchors = anchors + [swapped(item, "dev", bit) for item in anchors]
     late = len(anchors) - 1
-    pairs = [(item, both(lambda v: swapped(v, "grp", 1), item)) for item in anchors[:late]]
+    keys, anchors[late - 1] = ordered(keys, len(keys) - 1, anchors[late - 1])
+    pairs = [(item, swapped(item, "grp", 1)) for item in anchors[:late]]
 
     key_count, pair_count = len(keys), len(anchors)
     key_rows = key_count * rows
@@ -333,7 +339,7 @@
     key_unit, key_teacher, key_label = call(
         functools.partial(keys_kernel, key_count, rows),
         (b16((key_rows, width)), b16((key_rows, width)), f32((key_rows, rows))),
-        [k[0] for k in keys] + [k[1] for k in keys],
+        keys,
         flops=8 * key_rows * width,
         name="keys",
     )
@@ -343,9 +349,8 @@
     for i in range(tiles):
         last = i == tiles - 1
         if last:
-            stats, held = lax.optimization_barrier((stats, anchors[late][0]))
-            anchors[late] = (held, anchors[late][1])
-            pairs.append((anchors[late], both(lambda v: swapped(v, "grp", 1), anchors[late])))
+            stats, anchors[late] = lax.optimization_barrier((stats, anchors[late]))
+            pairs.append((anchors[late], swapped(anchors[late], "grp", 1)))
         chosen = [item for pair in pairs[i * GROUP : (i + 1) * GROUP] for item in pair]
         outs = call(
             functools.partial(tile_kernel, key_count, rows, i, n_blocks, last),
@@ -358,8 +363,7 @@
             )
             + ((f32((8, key_rows)),) if last else ()),
             [key_unit, key_teacher, key_label]
-            + [item[0] for item in chosen]
-            + [item[1] for item in chosen]
+            + chosen
             + ([] if stats is None else [stats]),
             flops=4 * key_rows * n_blocks * rows * width,
             name="tile",
@@ -388,34 +392,41 @@
         name="merge",
     )
 
-    def grads(k, key_stats):
-        blocks = {i: ((rows, rows), lambda step: (k, 0)) for i in (0, 1)}
+    def grads(which, key_stats):
+        chosen = (2 * which, 2 * which + 1)
+        blocks = {i: ((2 * rows, rows), lambda step: (which, 0)) for i in (0, 1)}
         for i in range(2 * tiles):
-            blocks[3 + i] = ((rows, n_blocks * rows), lambda step: (k, 0))
+            blocks[3 + i] = ((2 * rows, n_blocks * rows), lambda step: (which, 0))
         operands = [key_label, key_stats, anchor_stats] + similar + weights + anchor_labels + units
         return call(
-            functools.partial(grad_kernel, tiles, rows, k, n_blocks),
-            f32((rows, width)) if k == 0 else jax.ShapeDtypeStruct((rows + PAD, width), jnp.int16),
+            functools.partial(grad_kernel, tiles, rows, chosen, n_blocks),
+            [
+                f32((rows, width)) if k == 0 else jax.ShapeDtypeStruct((rows + PAD, width), jnp.int16)
+                for k in chosen
+            ],
             operands,
-            flops=4 * rows * members * rows * width,
+            flops=8 * rows * members * rows * width,
             name="grads",
             blocks=blocks,
         )
 
-    parts = []
-    for k in range(key_count - 1, -1, -1):
-        part = grads(k, key_stats)
-        if k:
-            key_stats, part = lax.optimization_barrier((key_stats, part))
-            mask = (k // 2) * 2 * members + (k % 2) * quarter
-            part = lax.ppermute(part, AXES, [(i, i ^ mask) for i in range(groups * members)])
-        parts.append(part)
-    loss, parts[0], parts[-1] = lax.optimization_barrier((loss, parts[0], parts[-1]))
+    parts = [None] * key_count
+    for which in range(key_count // 2 - 1, -1, -1):
+        both = list(grads(which, key_stats))
+        for j in (1, 0):
+            k = 2 * which + j
+            if k:
+                mask = (k // 2) * 2 * members + (k % 2) * quarter
+                if which:
+                    key_stats, both[j] = lax.optimization_barrier((key_stats, both[j]))
+                both[j] = lax.ppermute(both[j], AXES, [(i, i ^ mask) for i in range(groups * members)])
+            parts[k] = both[j]
+    loss, parts[-1], parts[0] = lax.optimization_barrier((loss, parts[-1], parts[0]))
     shared = lax.all_to_all(
         jnp.broadcast_to(loss[None], (groups * members, 8, rows)).reshape(-1, rows), AXES, 0, 0, tiled=True
     ).reshape(groups * members, 8, rows)
     losses = jnp.sum(shared[:, 0:2, 0], axis=0) / (groups * members * rows)
-    shares = [student] + parts[::-1]
+    shares = [student] + parts
     feature_grad = call(
         final_kernel,
         f32((rows, width)),

time: 112 us -> 105 us (0.938)
  starting transfers between devices: 46.5 us -> 28.8 us
  waiting for transfers between devices: 20.3 us -> 36.1 us
  Pallas kernels: 35.6 us -> 30.4 us
    ppermute x18 -> x9, starting transfers between devices: 23.3 us -> 8.54 us  [swapped(): return lax.ppermute(value, axis, [(i, i ^ mask) for i in range(size)])]
    ppermute x18 -> x9, waiting for transfers between devices: 11.8 us -> 24.9 us  [swapped(): return lax.ppermute(value, axis, [(i, i ^ mask) for i in range(size)])]
    pallas_call x10 -> x8, Pallas kernels: 35.6 us -> 30.4 us  [call(): pl.pallas_call(kernel, out_shape=shapes if many else out_shape, grid=(1,)...]
    ppermute x7 -> x5, waiting for transfers between devices: 0.02 us -> 4.19 us  [the longest x3 4.18 us: body(): lax.ppermute(both[j], AXES, [(i, i ^ mask) for i in range(groups * member...]
    all_to_all x1, waiting for transfers between devices: 4.31 us -> 2.83 us  [body(): lax.all_to_all(jnp.broadcast_to(loss[None], (groups * members, 8, rows))....]
    ppermute x7 -> x5, starting transfers between devices: 6.3 us -> 4.85 us  [the longest x3 3.49 us: body(): lax.ppermute(both[j], AXES, [(i, i ^ mask) for i in range(groups * member...]
    unnamed x52 -> x30, local copies, waits for them, and re-layouts: 3.46 us -> 3.06 us
  transfers between devices with their start and end apart: 30 -> 19, of which waited for: 11 -> 13; matrix products, arithmetic and copies ran while one was open for 1% -> 2% of each run, Pallas kernels for 21% -> 16%
where the time goes in v4:
time: 105 us; the launch traced here: 104 us
  waiting for transfers between devices  36.1 us (34%)
  Pallas kernels  30.4 us (29%)
  starting transfers between devices  28.8 us (27%)
  local copies, waits for them, and re-layouts  4.35 us (4%)
  other arithmetic  3.93 us (4%)
    pallas_call x8, Pallas kernels, call(): pl.pallas_call(kernel, out_shape=shapes if many else out_shape, grid=(1,)...  30.4 us
    ppermute x9, waiting for transfers between devices, swapped(): return lax.ppermute(value, axis, [(i, i ^ mask) for i in range(size)])  24.9 us
    all_to_all x1, starting transfers between devices, body(): received = lax.all_to_all(payload, AXES, 0, 0, tiled=True)  8.57 us
    ppermute x9, starting transfers between devices, swapped(): return lax.ppermute(value, axis, [(i, i ^ mask) for i in range(size)])  8.54 us
    ppermute x3, waiting for transfers between devices, body(): lax.ppermute(both[j], AXES, [(i, i ^ mask) for i in range(groups * member...  4.18 us
    ppermute x3, waiting for transfers between devices, body(): lax.ppermute(sums, AXES, [(i, i ^ mask) for i in range(total)])  3.69 us
    ppermute x3, starting transfers between devices, body(): lax.ppermute(sums, AXES, [(i, i ^ mask) for i in range(total)])  3.55 us
    ppermute x3, starting transfers between devices, body(): lax.ppermute(both[j], AXES, [(i, i ^ mask) for i in range(groups * member...  3.49 us
  transfers between devices with their start and end apart: 19, of which 13 were waited for; matrix products, arithmetic and copies ran while one was open for 2% of the time, Pallas kernels for 16%

profile of v4, /device:TPU:0, one launch (start us, length us, event | category | flops | bytes accessed | tf_op | source)
XLA Modules:
  0.0 104.3 jit_solution(11636658771910472071)
XLA Ops:
  0.7 0.7 convert_bitcast_fusion
  1.4 1.1 %pad_maximum_fusion.refs_0_ = bf16[272,1024]{1,0:T(8,128)(2,1)S(1)} fusion(bf16[16,1024]{1,0:T(8,128)(2,1)S(1)} %fusion.5, bf16[128,1024]{1,0:T(8,128)(2,1)} %param.4, bf16[128,1024]{1,0:T(8,128)(2,1)} %student_ref.1), kind=kLoop, calls=%fused_computation | loop fusion | flops 1671168 | bytes 1114112 | tf_op jit(solution)/shard_map/concatenate | solution.py:318
  2.5 3.1 %collective-permute-start = (bf16[272,1024]{1,0:T(8,128)(2,1)S(1)}, bf16[272,1024]{1,0:T(8,128)(2,1)S(1)}, u32[]{:S(2)}, u32[]{:S(2)}) collective-permute-start(bf16[272,1024]{1,0:T(8,128)(2,1)S(1)} %pad_maximum_fusion.refs_0_), channel_id=1, source_target_pairs={{0,2},{1,3},{2,0},{3,1},{4,6},{5,7},{6,4},{7,5},{8,10},{9,11},{10,... | collective-permute-start | bytes 1671176 | tf_op jit(solution)/shard_map/ppermute | solution.py:23
  5.6 0.7 collective-permute-start.4
  6.3 1.6 %collective-permute-start.1 = (bf16[272,1024]{1,0:T(8,128)(2,1)S(1)}, bf16[272,1024]{1,0:T(8,128)(2,1)}, u32[]{:S(2)}, u32[]{:S(2)}) collective-permute-start(bf16[272,1024]{1,0:T(8,128)(2,1)S(1)} %pad_maximum_fusion.refs_0_), channel_id=1, source_target_pairs={{0,16},{8,24},{16,0},{24,8},{1,17},{9,25},{17,1},{25,9},{2,18},{10... | collective-permute-start | bytes 1671176 | tf_op jit(solution)/shard_map/ppermute | solution.py:23
  7.8 10.4 %collective-permute-done.refs_1_ = bf16[272,1024]{1,0:T(8,128)(2,1)S(1)} collective-permute-done((bf16[272,1024]{1,0:T(8,128)(2,1)S(1)}, bf16[272,1024]{1,0:T(8,128)(2,1)S(1)}, u32[]{:S(2)}, u32[]{:S(2)}) %collective-permute-start) | collective-permute-done | bytes 557088 | tf_op jit(solution)/shard_map/ppermute | solution.py:23
  18.2 0.7 collective-permute-start.2
  18.9 0.2 broadcast_select_fusion.1.refs_3_
  19.2 1.7 %collective-permute-start.5 = (bf16[272,1024]{1,0:T(8,128)(2,1)S(1)}, bf16[272,1024]{1,0:T(8,128)(2,1)}, u32[]{:S(2)}, u32[]{:S(2)}) collective-permute-start(bf16[272,1024]{1,0:T(8,128)(2,1)S(1)} %broadcast_select_fusion.1.refs_3_), channel_id=1, source_target_pairs={{0,1},{1,0},{2,3},{3,2},{4,5},{5,4},{6,7},{7,6},{8,9},{9,8},{10,11... | collective-permute-start | bytes 1671176 | tf_op jit(solution)/shard_map/ppermute | solution.py:23
  21.0 1.5 %collective-permute-start.3 = (bf16[272,1024]{1,0:T(8,128)(2,1)S(1)}, bf16[272,1024]{1,0:T(8,128)(2,1)S(1)}, u32[]{:S(2)}, u32[]{:S(2)}) collective-permute-start(bf16[272,1024]{1,0:T(8,128)(2,1)S(1)} %collective-permute-done.refs_1_), channel_id=1, source_target_pairs={{0,16},{8,24},{16,0},{24,8},{1,17},{9,25},{17,1},{25,9},{2,18},{10... | collective-permute-start | bytes 1671176 | tf_op jit(solution)/shard_map/ppermute | solution.py:23
  22.5 0.9 broadcast_select_fusion.refs_5_
  23.4 0.6 collective-permute-start.9
  23.9 10.9 %collective-permute-done.5.refs_3_ = bf16[272,1024]{1,0:T(8,128)(2,1)} collective-permute-done((bf16[272,1024]{1,0:T(8,128)(2,1)S(1)}, bf16[272,1024]{1,0:T(8,128)(2,1)}, u32[]{:S(2)}, u32[]{:S(2)}) %collective-permute-start.5) | collective-permute-done | bytes 557088 | tf_op jit(solution)/shard_map/ppermute | solution.py:23
  34.8 0.8 collective-permute-done.3.refs_3_
  35.7 0.8 copy-done.6
  36.5 3.6 %keys.1 = (bf16[512,1024]{1,0:T(8,128)(2,1)}, bf16[512,1024]{1,0:T(8,128)(2,1)}, f32[512,128]{1,0:T(8,128)}) custom-call(bf16[272,1024]{1,0:T(8,128)(2,1)} %copy-done.3, bf16[272,1024]{1,0:T(8,128)(2,1)} %copy-done.2, bf16[272,1024]{1,0:T(8,128)(2,1)} %collective-permute-done.1.refs_2_, bf16[272,1024]{1,0:T(8,128)(2,1)} %copy-done.6), custom_call_target="tpu_custom_call" | custom-call | flops 4194304 | bytes 2228224 | tf_op jit(solution)/shard_map/keys/pallas_call | solution.py:62
  40.2 5.6 %tile.2 = (bf16[512,1024]{1,0:T(8,128)(2,1)}, f32[512,512]{1,0:T(8,128)}, f32[512,512]{1,0:T(8,128)}, f32[8,512]{1,0:T(8,128)}, f32[512,128]{1,0:T(8,128)}) custom-call(bf16[512,1024]{1,0:T(8,128)(2,1)} %get-tuple-element.38.refs_0_, bf16[512,1024]{1,0:T(8,128)(2,1)} %get-tuple-element.39.refs_1_, f32[512,128]{1,0:T(8,128)} %get-tuple-element.40.refs_2_.refs_0_, ...), custom_call_target="tpu_custom_call" | custom-call | flops 1073741824 | bytes 4587520 | tf_op jit(solution)/shard_map/tile/pallas_call | solution.py:62
  45.8 0.6 collective-permute-done.9.refs_5_
  46.3 2.2 %collective-permute-done.10.refs_6_ = bf16[272,1024]{1,0:T(8,128)(2,1)S(1)} collective-permute-done((bf16[272,1024]{1,0:T(8,128)(2,1)}, bf16[272,1024]{1,0:T(8,128)(2,1)S(1)}, u32[]{:S(2)}, u32[]{:S(2)}) %collective-permute-start.10) | collective-permute-done | bytes 557088 | tf_op jit(solution)/shard_map/ppermute | solution.py:23
  48.5 0.8 copy-done.5
  49.3 5.6 %tile.3 = (bf16[512,1024]{1,0:T(8,128)(2,1)}, f32[512,512]{1,0:T(8,128)}, f32[512,512]{1,0:T(8,128)}, f32[8,512]{1,0:T(8,128)}, f32[512,128]{1,0:T(8,128)}, /*index=5*/f32[8,512]{1,0:T(8,128)}) custom-call(bf16[512,1024]{1,0:T(8,128)(2,1)} %get-tuple-element.38.refs_0_, bf16[512,1024]{1,0:T(8,128)(2,1)} %get-tuple-element.39.refs_1_, ...), custom_call_target="tpu_custom_call" | custom-call | flops 1073741824 | bytes 4849664 | tf_op jit(solution)/shard_map/tile/pallas_call | solution.py:62
  55.0 1.4 %payload.1 = f32[256,128]{1,0:T(8,128)} custom-call(f32[8,512]{1,0:T(8,128)} %get-tuple-element.46.sums_ref.refs_1_), custom_call_target="tpu_custom_call" | custom-call | bytes 16384 | tf_op jit(solution)/shard_map/payload/pallas_call | solution.py:62
  56.3 8.6 %all-to-all-start = ((f32[32,8,128]{2,1,0:T(8,128)}), f32[32,8,128]{2,1,0:T(8,128)S(1)}, u32[]{:S(2)}, u32[]{:S(2)}) async-start(f32[32,8,128]{2,1,0:T(8,128)} %bitcast.9), calls=%async_computation | async-start | bytes 262144 | tf_op jit(solution)/shard_map/all_to_all | solution.py:387
  64.9 2.7 %collective-permute-start.13 = (f32[8,512]{1,0:T(8,128)}, f32[8,512]{1,0:T(8,128)S(1)}, u32[]{:S(2)}, u32[]{:S(2)}) collective-permute-start(f32[8,512]{1,0:T(8,128)} %get-tuple-element.46.sums_ref.refs_1_), channel_id=1, source_target_pairs={{0,18},{1,19},{2,16},{3,17},{4,22},{5,23},{6,20},{7,21},{8,26},{9,... | collective-permute-start | bytes 49160 | tf_op jit(solution)/shard_map/ppermute | solution.py:380
  67.7 0.6 collective-permute-start.12
  68.2 0.3 collective-permute-start.11
  68.5 1.4 %collective-permute-done.13.refs_4_ = f32[8,512]{1,0:T(8,128)S(1)} collective-permute-done((f32[8,512]{1,0:T(8,128)}, f32[8,512]{1,0:T(8,128)S(1)}, u32[]{:S(2)}, u32[]{:S(2)}) %collective-permute-start.13) | collective-permute-done | bytes 16416 | tf_op jit(solution)/shard_map/ppermute | solution.py:380
  69.8 1.9 %collective-permute-done.12.refs_3_ = f32[8,512]{1,0:T(8,128)S(1)} collective-permute-done((f32[8,512]{1,0:T(8,128)}, f32[8,512]{1,0:T(8,128)S(1)}, u32[]{:S(2)}, u32[]{:S(2)}) %collective-permute-start.12) | collective-permute-done | bytes 16416 | tf_op jit(solution)/shard_map/ppermute | solution.py:380
  71.7 0.4 collective-permute-done.11.refs_2_
  72.2 0.5 all-to-all-done
  72.7 0.1 copy-done.13
  72.8 0.5 copy-done.7
  73.3 1.8 %merge.1 = (f32[8,1024]{1,0:T(8,128)}, f32[512,128]{1,0:T(8,128)}, f32[8,128]{1,0:T(8,128)}) custom-call(f32[256,128]{1,0:T(8,128)} %bitcast.8, f32[8,512]{1,0:T(8,128)} %get-tuple-element.46.sums_ref.refs_1_, f32[8,512]{1,0:T(8,128)} %copy-done.13, f32[8,512]{1,0:T(8,128)} %copy-done.12, f32[8,512]{1,0:T(8,128)} %copy-done.11), custom_call_target="tpu_custom_call" | custom-call | bytes 196608 | tf_op jit(solution)/shard_map/merge/pallas_call | solution.py:62
  75.1 4.9 %grads.2 = (s16[144,1024]{1,0:T(8,128)(2,1)}, s16[144,1024]{1,0:T(8,128)(2,1)}) custom-call(f32[512,128]{1,0:T(8,128)} %get-tuple-element.40.refs_2_.refs_0_, f32[512,128]{1,0:T(8,128)} %get-tuple-element.62.refs_1_, f32[8,1024]{1,0:T(8,128)} %get-tuple-element.49.refs_2_, f32[512,512]{1,0:T(8,128)} %get-tuple-element.50.refs_3_, ...), custom_call_target="tpu_custom_call" | custom-call | flops 1073741824 | bytes 6881280 | tf_op jit(solution)/shard_map/grads/pallas_call | solution.py:62
  80.0 1.0 collective-permute-start.14
  81.0 4.8 %grads.3 = (f32[128,1024]{1,0:T(8,128)}, s16[144,1024]{1,0:T(8,128)(2,1)}) custom-call(f32[512,128]{1,0:T(8,128)} %get-tuple-element.40.refs_2_.refs_0_, f32[512,128]{1,0:T(8,128)} %get-tuple-element.62.refs_1_, f32[8,1024]{1,0:T(8,128)} %get-tuple-element.49.refs_2_, f32[512,512]{1,0:T(8,128)} %get-tuple-element.50.refs_3_, ...), custom_call_target="tpu_custom_call" | custom-call | flops 1073741824 | bytes 6881280 | tf_op jit(solution)/shard_map/grads/pallas_call | solution.py:62
  85.8 1.6 %collective-permute-start.15 = (s16[144,1024]{1,0:T(8,128)(2,1)}, s16[144,1024]{1,0:T(8,128)(2,1)S(1)}, u32[]{:S(2)}, u32[]{:S(2)}) collective-permute-start(s16[144,1024]{1,0:T(8,128)(2,1)} %get-tuple-element.66), channel_id=1, source_target_pairs={{0,2},{1,3},{2,0},{3,1},{4,6},{5,7},{6,4},{7,5},{8,10},{9,11},{10,... | collective-permute-start | bytes 884744 | tf_op jit(solution)/shard_map/ppermute | solution.py:422
  87.3 0.9 collective-permute-start.16
  88.3 2.7 %collective-permute-done.14.refs_2_ = s16[144,1024]{1,0:T(8,128)(2,1)S(1)} collective-permute-done((s16[144,1024]{1,0:T(8,128)(2,1)}, s16[144,1024]{1,0:T(8,128)(2,1)S(1)}, u32[]{:S(2)}, u32[]{:S(2)}) %collective-permute-start.14) | collective-permute-done | bytes 294944 | tf_op jit(solution)/shard_map/ppermute | solution.py:422
  91.0 0.7 broadcast_in_dim.2
  91.7 3.3 %all-to-all-start.1 = ((f32[32,8,128]{2,1,0:T(8,128)}), f32[32,8,128]{2,1,0:T(8,128)}, u32[]{:S(2)}, u32[]{:S(2)}) async-start(f32[32,8,128]{2,1,0:T(8,128)} %broadcast_in_dim.2), calls=%async_computation.1 | async-start | bytes 262144 | tf_op jit(solution)/shard_map/all_to_all | solution.py:425
  95.0 0.7 collective-permute-done.15.refs_0_
  95.6 0.8 collective-permute-done.16.refs_1_
  96.5 0.7 copy-done.10
  97.2 2.7 %final.1 = f32[128,1024]{1,0:T(8,128)} custom-call(bf16[128,1024]{1,0:T(8,128)(2,1)} %student_ref.1, f32[128,1024]{1,0:T(8,128)} %get-tuple-element.65.own_ref, s16[144,1024]{1,0:T(8,128)(2,1)} %copy-done.9, s16[144,1024]{1,0:T(8,128)(2,1)} %copy-done.10, s16[144,1024]{1,0:T(8,128)(2,1)} %copy-done.8), custom_call_target="tpu_custom_call" | custom-call | flops 1048576 | bytes 1671168 | tf_op jit(solution)/shard_map/final/pallas_call | solution.py:62
  99.9 2.8 %all-to-all-done.1 = f32[32,8,128]{2,1,0:T(8,128)} async-done(((f32[32,8,128]{2,1,0:T(8,128)}), f32[32,8,128]{2,1,0:T(8,128)}, u32[]{:S(2)}, u32[]{:S(2)}) %all-to-all-start.1) | async-done | bytes 131104 | tf_op jit(solution)/shard_map/all_to_all | solution.py:425
  102.7 1.1 %slice_reduce_fusion = f32[2]{0:T(128)S(1)} fusion(f32[32,8,128]{2,1,0:T(8,128)} %all-to-all-done.1), kind=kLoop, calls=%fused_computation.11 | loop fusion | flops 62 | bytes 264 | tf_op jit(solution)/shard_map/reduce_sum | solution.py:428
  103.7 0.6 fusion.8
  (37 shorter events, 0.2 us)
Async XLA Ops:
  0.6 18.3 %copy-start = (bf16[128,1024]{1,0:T(8,128)(2,1)S(1)}, bf16[128,1024]{1,0:T(8,128)(2,1)}, u32[]{:S(2)}) copy-start(bf16[128,1024]{1,0:T(8,128)(2,1)} %student_ref.1) | copy-start | bytes 786436
  0.6 18.3 %copy-start.4 = (bf16[128,1024]{1,0:T(8,128)(2,1)S(1)}, bf16[128,1024]{1,0:T(8,128)(2,1)}, u32[]{:S(2)}) copy-start(bf16[128,1024]{1,0:T(8,128)(2,1)} %param.4) | copy-start | bytes 786436
  2.5 20.9 %copy-start.3 = (bf16[272,1024]{1,0:T(8,128)(2,1)}, bf16[272,1024]{1,0:T(8,128)(2,1)S(1)}, u32[]{:S(2)}) copy-start(bf16[272,1024]{1,0:T(8,128)(2,1)S(1)} %pad_maximum_fusion.refs_0_) | copy-start | bytes 1671172
  2.5 15.7 %collective-permute-start = (bf16[272,1024]{1,0:T(8,128)(2,1)S(1)}, bf16[272,1024]{1,0:T(8,128)(2,1)S(1)}, u32[]{:S(2)}, u32[]{:S(2)}) collective-permute-start(bf16[272,1024]{1,0:T(8,128)(2,1)S(1)} %pad_maximum_fusion.refs_0_), channel_id=1, source_target_pairs={{0,2},{1,3},{2,0},{3,1},{4,6},{5,7},{6,4},{7,5},{8,10},{9,11},{10,... | collective-permute-start | bytes 1671176 | tf_op jit(solution)/shard_map/ppermute | solution.py:23
  5.6 13.4 %collective-permute-start.4 = (bf16[272,1024]{1,0:T(8,128)(2,1)S(1)}, bf16[272,1024]{1,0:T(8,128)(2,1)S(1)}, u32[]{:S(2)}, u32[]{:S(2)}) collective-permute-start(bf16[272,1024]{1,0:T(8,128)(2,1)S(1)} %pad_maximum_fusion.refs_0_), channel_id=1, source_target_pairs={{2,4},{3,5},{4,2},{5,3},{10,12},{11,13},{12,10},{13,11},{18,20},{1... | collective-permute-start | bytes 1671176 | tf_op jit(solution)/shard_map/ppermute | solution.py:321
  6.3 16.2 %collective-permute-start.1 = (bf16[272,1024]{1,0:T(8,128)(2,1)S(1)}, bf16[272,1024]{1,0:T(8,128)(2,1)}, u32[]{:S(2)}, u32[]{:S(2)}) collective-permute-start(bf16[272,1024]{1,0:T(8,128)(2,1)S(1)} %pad_maximum_fusion.refs_0_), channel_id=1, source_target_pairs={{0,16},{8,24},{16,0},{24,8},{1,17},{9,25},{17,1},{25,9},{2,18},{10... | collective-permute-start | bytes 1671176 | tf_op jit(solution)/shard_map/ppermute | solution.py:23
  18.2 5.2 %copy-start.2 = (bf16[272,1024]{1,0:T(8,128)(2,1)}, bf16[272,1024]{1,0:T(8,128)(2,1)S(1)}, u32[]{:S(2)}) copy-start(bf16[272,1024]{1,0:T(8,128)(2,1)S(1)} %collective-permute-done.refs_1_) | copy-start | bytes 1671172
  18.2 4.3 %collective-permute-start.2 = (bf16[272,1024]{1,0:T(8,128)(2,1)S(1)}, bf16[272,1024]{1,0:T(8,128)(2,1)S(1)}, u32[]{:S(2)}, u32[]{:S(2)}) collective-permute-start(bf16[272,1024]{1,0:T(8,128)(2,1)S(1)} %collective-permute-done.refs_1_), channel_id=1, source_target_pairs={{2,4},{3,5},{4,2},{5,3},{10,12},{11,13},{12,10},{13,11},{18,20},{1... | collective-permute-start | bytes 1671176 | tf_op jit(solution)/shard_map/ppermute | solution.py:325
  19.2 21.0 %copy-start.1 = (bf16[272,1024]{1,0:T(8,128)(2,1)}, bf16[272,1024]{1,0:T(8,128)(2,1)S(1)}, u32[]{:S(2)}) copy-start(bf16[272,1024]{1,0:T(8,128)(2,1)S(1)} %broadcast_select_fusion.1.refs_3_) | copy-start | bytes 1671172
  19.2 21.0 %collective-permute-start.7 = (bf16[272,1024]{1,0:T(8,128)(2,1)S(1)}, bf16[272,1024]{1,0:T(8,128)(2,1)}, u32[]{:S(2)}, u32[]{:S(2)}) collective-permute-start(bf16[272,1024]{1,0:T(8,128)(2,1)S(1)} %broadcast_select_fusion.1.refs_3_), channel_id=1, source_target_pairs={{0,8},{8,0},{16,24},{24,16},{1,9},{9,1},{17,25},{25,17},{2,10},{10... | collective-permute-start | bytes 1671176 | tf_op jit(solution)/shard_map/ppermute | solution.py:23
  19.2 15.6 %collective-permute-start.5 = (bf16[272,1024]{1,0:T(8,128)(2,1)S(1)}, bf16[272,1024]{1,0:T(8,128)(2,1)}, u32[]{:S(2)}, u32[]{:S(2)}) collective-permute-start(bf16[272,1024]{1,0:T(8,128)(2,1)S(1)} %broadcast_select_fusion.1.refs_3_), channel_id=1, source_target_pairs={{0,1},{1,0},{2,3},{3,2},{4,5},{5,4},{6,7},{7,6},{8,9},{9,8},{10,11... | collective-permute-start | bytes 1671176 | tf_op jit(solution)/shard_map/ppermute | solution.py:23
  21.0 14.7 %collective-permute-start.3 = (bf16[272,1024]{1,0:T(8,128)(2,1)S(1)}, bf16[272,1024]{1,0:T(8,128)(2,1)S(1)}, u32[]{:S(2)}, u32[]{:S(2)}) collective-permute-start(bf16[272,1024]{1,0:T(8,128)(2,1)S(1)} %collective-permute-done.refs_1_), channel_id=1, source_target_pairs={{0,16},{8,24},{16,0},{24,8},{1,17},{9,25},{17,1},{25,9},{2,18},{10... | collective-permute-start | bytes 1671176 | tf_op jit(solution)/shard_map/ppermute | solution.py:23
  23.4 16.8 %collective-permute-start.8 = (bf16[272,1024]{1,0:T(8,128)(2,1)}, bf16[272,1024]{1,0:T(8,128)(2,1)}, u32[]{:S(2)}, u32[]{:S(2)}) collective-permute-start(bf16[272,1024]{1,0:T(8,128)(2,1)} %broadcast_select_fusion.refs_5_), channel_id=1, source_target_pairs={{0,8},{8,0},{16,24},{24,16},{1,9},{9,1},{17,25},{25,17},{2,10},{10... | collective-permute-start | bytes 1671176 | tf_op jit(solution)/shard_map/ppermute | solution.py:23
  23.4 23.0 %collective-permute-start.9 = (bf16[272,1024]{1,0:T(8,128)(2,1)}, bf16[272,1024]{1,0:T(8,128)(2,1)}, u32[]{:S(2)}, u32[]{:S(2)}) collective-permute-start(bf16[272,1024]{1,0:T(8,128)(2,1)} %broadcast_select_fusion.refs_5_), channel_id=1, source_target_pairs={{0,1},{1,0},{2,3},{3,2},{4,5},{5,4},{6,7},{7,6},{8,9},{9,8},{10,11... | collective-permute-start | bytes 1671176 | tf_op jit(solution)/shard_map/ppermute | solution.py:23
  35.7 0.8 copy-start.6
  36.5 9.8 %collective-permute-start.6 = (bf16[272,1024]{1,0:T(8,128)(2,1)}, bf16[272,1024]{1,0:T(8,128)(2,1)}, u32[]{:S(2)}, u32[]{:S(2)}) collective-permute-start(bf16[272,1024]{1,0:T(8,128)(2,1)} %collective-permute-done.5.refs_3_), channel_id=1, source_target_pairs={{0,8},{8,0},{16,24},{24,16},{1,9},{9,1},{17,25},{25,17},{2,10},{10... | collective-permute-start | bytes 1671176 | tf_op jit(solution)/shard_map/ppermute | solution.py:23
  46.3 2.2 %collective-permute-start.10 = (bf16[272,1024]{1,0:T(8,128)(2,1)}, bf16[272,1024]{1,0:T(8,128)(2,1)S(1)}, u32[]{:S(2)}, u32[]{:S(2)}) collective-permute-start(bf16[272,1024]{1,0:T(8,128)(2,1)} %collective-permute-done.9.refs_5_), channel_id=1, source_target_pairs={{0,8},{8,0},{16,24},{24,16},{1,9},{9,1},{17,25},{25,17},{2,10},{10... | collective-permute-start | bytes 1671176 | tf_op jit(solution)/shard_map/ppermute | solution.py:23
  48.5 0.8 copy-start.5
  56.3 16.3 %all-to-all-start = ((f32[32,8,128]{2,1,0:T(8,128)}), f32[32,8,128]{2,1,0:T(8,128)S(1)}, u32[]{:S(2)}, u32[]{:S(2)}) async-start(f32[32,8,128]{2,1,0:T(8,128)} %bitcast.9), calls=%async_computation | async-start | bytes 262144 | tf_op jit(solution)/shard_map/all_to_all | solution.py:387
  64.9 4.9 %collective-permute-start.13 = (f32[8,512]{1,0:T(8,128)}, f32[8,512]{1,0:T(8,128)S(1)}, u32[]{:S(2)}, u32[]{:S(2)}) collective-permute-start(f32[8,512]{1,0:T(8,128)} %get-tuple-element.46.sums_ref.refs_1_), channel_id=1, source_target_pairs={{0,18},{1,19},{2,16},{3,17},{4,22},{5,23},{6,20},{7,21},{8,26},{9,... | collective-permute-start | bytes 49160 | tf_op jit(solution)/shard_map/ppermute | solution.py:380
  67.7 4.1 %collective-permute-start.12 = (f32[8,512]{1,0:T(8,128)}, f32[8,512]{1,0:T(8,128)S(1)}, u32[]{:S(2)}, u32[]{:S(2)}) collective-permute-start(f32[8,512]{1,0:T(8,128)} %get-tuple-element.46.sums_ref.refs_1_), channel_id=1, source_target_pairs={{0,16},{1,17},{2,18},{3,19},{4,20},{5,21},{6,22},{7,23},{8,24},{9,... | collective-permute-start | bytes 49160 | tf_op jit(solution)/shard_map/ppermute | solution.py:380
  68.2 3.9 %collective-permute-start.11 = (f32[8,512]{1,0:T(8,128)}, f32[8,512]{1,0:T(8,128)S(1)}, u32[]{:S(2)}, u32[]{:S(2)}) collective-permute-start(f32[8,512]{1,0:T(8,128)} %get-tuple-element.46.sums_ref.refs_1_), channel_id=1, source_target_pairs={{0,2},{1,3},{2,0},{3,1},{4,6},{5,7},{6,4},{7,5},{8,10},{9,11},{10,... | collective-permute-start | bytes 49160 | tf_op jit(solution)/shard_map/ppermute | solution.py:380
  69.8 2.8 %copy-start.11 = (f32[8,512]{1,0:T(8,128)}, f32[8,512]{1,0:T(8,128)S(1)}, u32[]{:S(2)}) copy-start(f32[8,512]{1,0:T(8,128)S(1)} %collective-permute-done.13.refs_4_) | copy-start | bytes 49156
  71.7 0.9 copy-start.12
  72.2 0.6 copy-start.13
  72.7 0.7 copy-start.7
  80.0 11.0 %collective-permute-start.14 = (s16[144,1024]{1,0:T(8,128)(2,1)}, s16[144,1024]{1,0:T(8,128)(2,1)S(1)}, u32[]{:S(2)}, u32[]{:S(2)}) collective-permute-start(s16[144,1024]{1,0:T(8,128)(2,1)} %get-tuple-element.59), channel_id=1, source_target_pairs={{0,18},{1,19},{2,16},{3,17},{4,22},{5,23},{6,20},{7,21},{8,26},{9,... | collective-permute-start | bytes 884744 | tf_op jit(solution)/shard_map/ppermute | solution.py:422
  81.0 10.0 %copy-start.14 = (f32[8,128]{1,0:T(8,128)S(1)}, f32[8,128]{1,0:T(8,128)}, u32[]{:S(2)}) copy-start(f32[8,128]{1,0:T(8,128)} %get-tuple-element.64) | copy-start | bytes 12292
  85.8 9.9 %collective-permute-start.15 = (s16[144,1024]{1,0:T(8,128)(2,1)}, s16[144,1024]{1,0:T(8,128)(2,1)S(1)}, u32[]{:S(2)}, u32[]{:S(2)}) collective-permute-start(s16[144,1024]{1,0:T(8,128)(2,1)} %get-tuple-element.66), channel_id=1, source_target_pairs={{0,2},{1,3},{2,0},{3,1},{4,6},{5,7},{6,4},{7,5},{8,10},{9,11},{10,... | collective-permute-start | bytes 884744 | tf_op jit(solution)/shard_map/ppermute | solution.py:422
  87.3 9.1 %collective-permute-start.16 = (s16[144,1024]{1,0:T(8,128)(2,1)}, s16[144,1024]{1,0:T(8,128)(2,1)S(1)}, u32[]{:S(2)}, u32[]{:S(2)}) collective-permute-start(s16[144,1024]{1,0:T(8,128)(2,1)} %get-tuple-element.67), channel_id=1, source_target_pairs={{0,16},{1,17},{2,18},{3,19},{4,20},{5,21},{6,22},{7,23},{8,24},{9,... | collective-permute-start | bytes 884744 | tf_op jit(solution)/shard_map/ppermute | solution.py:422
  91.0 5.5 %copy-start.8 = (s16[144,1024]{1,0:T(8,128)(2,1)}, s16[144,1024]{1,0:T(8,128)(2,1)S(1)}, u32[]{:S(2)}) copy-start(s16[144,1024]{1,0:T(8,128)(2,1)S(1)} %collective-permute-done.14.refs_2_) | copy-start | bytes 884740
  91.7 11.0 %all-to-all-start.1 = ((f32[32,8,128]{2,1,0:T(8,128)}), f32[32,8,128]{2,1,0:T(8,128)}, u32[]{:S(2)}, u32[]{:S(2)}) async-start(f32[32,8,128]{2,1,0:T(8,128)} %broadcast_in_dim.2), calls=%async_computation.1 | async-start | bytes 262144 | tf_op jit(solution)/shard_map/all_to_all | solution.py:425
  95.6 0.8 copy-start.9
  96.5 0.7 copy-start.10

commit v5 on v4

--- a/solution.py
+++ b/solution.py
@@ -49,7 +49,7 @@
     )
 
 
-def call(kernel, out_shape, operands, flops=0, name=None, blocks=None):
+def call(kernel, out_shape, operands, flops=0, name=None, blocks=None, limit=VMEM_LIMIT):
     def spec(shape, given):
         if given is None:
             return pl.BlockSpec(shape, lambda step: (0, 0))
@@ -67,7 +67,7 @@
         out_specs=out_specs if many else out_specs[0],
         name=name,
         cost_estimate=pl.CostEstimate(flops=flops, bytes_accessed=moved, transcendentals=0),
-        compiler_params=pltpu.CompilerParams(vmem_limit_bytes=VMEM_LIMIT),
+        compiler_params=pltpu.CompilerParams(vmem_limit_bytes=limit),
     )(*operands)
 
 
@@ -93,6 +93,17 @@
     h, c, p, q, r = place()
     members = lax.axis_size("dev")
     return (h * 2 + (c ^ dc)) * members + (q * 2 + (p ^ (i % 2))) * (members // 4) + (r ^ (i // 2))
+
+
+def pack_kernel(rows, student_ref, teacher_ref, label_ref, out_ref):
+    out_ref[0:rows, :] = student_ref[...]
+    out_ref[rows : 2 * rows, :] = teacher_ref[...]
+    out_ref[2 * rows : 2 * rows + PAD, :] = jnp.zeros((PAD, out_ref.shape[1]), out_ref.dtype)
+    high = lax.shift_right_logical(label_ref[...], 8)
+    low = label_ref[...] & 255
+    at = lax.broadcasted_iota(jnp.int32, (PAD, rows), 0)
+    digits = jnp.where(at == 0, high, jnp.where(at == 1, low, 0)).astype(jnp.float32)
+    out_ref[2 * rows : 2 * rows + PAD, 0:rows] = digits.astype(out_ref.dtype)
 
 
 def keys_kernel(count, rows, *refs):
@@ -187,7 +198,9 @@
             contrast = (1.0 - total[4:5] / positives) / temp_sup + jnp.log(total[0:1])
             relation = (1.0 - total[3:4] / total[2:3]) / temp_student + jnp.log(total[1:2])
             both = jnp.concatenate([contrast, relation] + [jnp.zeros((6, rows), jnp.float32)], axis=0)
-            loss_ref[...] = jnp.broadcast_to(jnp.sum(both, axis=1, keepdims=True), (8, rows))
+            loss = jnp.broadcast_to(jnp.sum(both, axis=1, keepdims=True), (8, rows))
+            for d in range(groups * members):
+                loss_ref[d * 8 : d * 8 + 8, :] = loss
         factors = jnp.concatenate(
             [
                 (1.0 / temp_sup) / total[0:1],
@@ -313,9 +326,12 @@
         (d, d ^ (3 * quarter)) for d in range(members) if (d // (2 * quarter)) != (d // quarter) % 2
     ]
 
-    digits = jnp.stack([labels // 256, labels % 256]).astype(jnp.bfloat16)
-    tail = jnp.pad(digits, ((0, PAD - 2), (0, width - rows)))
-    own = jnp.concatenate([student, teacher, tail], axis=0)
+    own = call(
+        functools.partial(pack_kernel, rows),
+        jax.ShapeDtypeStruct((2 * rows + PAD, width), jnp.bfloat16),
+        [student, teacher, labels.reshape(1, rows)],
+        name="pack",
+    )
 
     near = swapped(own, "dev", quarter)
     crossed = lax.ppermute(own, "dev", cross)
@@ -387,7 +403,7 @@
     received = lax.all_to_all(payload, AXES, 0, 0, tiled=True)
     anchor_stats, key_stats, loss = call(
         functools.partial(merge_kernel, (groups, members, key_count), rows),
-        (f32((8, members * rows)), f32((key_rows, rows)), f32((8, rows))),
+        (f32((8, members * rows)), f32((key_rows, rows)), f32((groups * members * 8, rows))),
         [received, sums] + others,
         name="merge",
     )
@@ -422,9 +438,7 @@
                 both[j] = lax.ppermute(both[j], AXES, [(i, i ^ mask) for i in range(groups * members)])
             parts[k] = both[j]
     loss, parts[-1], parts[0] = lax.optimization_barrier((loss, parts[-1], parts[0]))
-    shared = lax.all_to_all(
-        jnp.broadcast_to(loss[None], (groups * members, 8, rows)).reshape(-1, rows), AXES, 0, 0, tiled=True
-    ).reshape(groups * members, 8, rows)
+    shared = lax.all_to_all(loss, AXES, 0, 0, tiled=True).reshape(groups * members, 8, rows)
     losses = jnp.sum(shared[:, 0:2, 0], axis=0) / (groups * members * rows)
     shares = [student] + parts
     feature_grad = call(
@@ -433,6 +447,7 @@
         shares,
         flops=8 * rows * width,
         name="final",
+        limit=VMEM_LIMIT // 4,
     )
     return (losses[0], losses[1], feature_grad)
 

time: 105 us -> 103 us (0.981)
  other arithmetic: 3.93 us -> 2.23 us
  starting transfers between devices: 28.8 us -> 27.1 us
  waiting for transfers between devices: 36.1 us -> 37.2 us
    ppermute x3, waiting for transfers between devices: 4.18 us -> 5.44 us  [body(): lax.ppermute(both[j], AXES, [(i, i ^ mask) for i in range(groups * member...]
    concatenate x1 -> x0, other arithmetic: 1.07 us -> none  [body(): own = jnp.concatenate([student, teacher, tail], axis=0)]
    pallas_call x8 -> x9, Pallas kernels: 30.4 us -> 31 us  [call(): pl.pallas_call(kernel, out_shape=shapes if many else out_shape, grid=(1,)...]
    unnamed x30 -> x26, local copies, waits for them, and re-layouts: 3.06 us -> 3.39 us
  transfers between devices with their start and end apart: 19 -> 19, of which waited for: 13 -> 13; matrix products, arithmetic and copies ran while one was open for 2% -> 2% of each run, Pallas kernels for 16% -> 15%
where the time goes in v5:
time: 103 us; the launch traced here: 102 us
  waiting for transfers between devices  37.2 us (36%)
  Pallas kernels  31 us (30%)
  starting transfers between devices  27.1 us (26%)
  local copies, waits for them, and re-layouts  3.98 us (4%)
  other arithmetic  2.23 us (2%)
    pallas_call x9, Pallas kernels, call(): pl.pallas_call(kernel, out_shape=shapes if many else out_shape, grid=(1,)...  31 us
    ppermute x9, waiting for transfers between devices, swapped(): return lax.ppermute(value, axis, [(i, i ^ mask) for i in range(size)])  25 us
    ppermute x9, starting transfers between devices, swapped(): return lax.ppermute(value, axis, [(i, i ^ mask) for i in range(size)])  8.43 us
    all_to_all x1, starting transfers between devices, body(): received = lax.all_to_all(payload, AXES, 0, 0, tiled=True)  7.59 us
    ppermute x3, waiting for transfers between devices, body(): lax.ppermute(both[j], AXES, [(i, i ^ mask) for i in range(groups * member...  5.44 us
    ppermute x3, waiting for transfers between devices, body(): lax.ppermute(sums, AXES, [(i, i ^ mask) for i in range(total)])  3.56 us
    ppermute x3, starting transfers between devices, body(): lax.ppermute(sums, AXES, [(i, i ^ mask) for i in range(total)])  3.55 us
    ppermute x3, starting transfers between devices, body(): lax.ppermute(both[j], AXES, [(i, i ^ mask) for i in range(groups * member...  3.49 us
  transfers between devices with their start and end apart: 19, of which 13 were waited for; matrix products, arithmetic and copies ran while one was open for 2% of the time, Pallas kernels for 15%

profile of v5, /device:TPU:0, one launch (start us, length us, event | category | flops | bytes accessed | tf_op | source)
XLA Modules:
  0.0 102.3 jit_solution(10536836302049491960)
XLA Ops:
  0.6 1.9 %pack.1.refs_0_ = bf16[272,1024]{1,0:T(8,128)(2,1)} custom-call(bf16[128,1024]{1,0:T(8,128)(2,1)} %student_ref.3, bf16[128,1024]{1,0:T(8,128)(2,1)} %teacher_ref.1, s32[1,128]{1,0:T(1,128)} %bitcast.8), custom_call_target="tpu_custom_call" | custom-call | bytes 524800 | tf_op jit(solution)/shard_map/pack/pallas_call | solution.py:62
  2.5 3.0 %collective-permute-start = (bf16[272,1024]{1,0:T(8,128)(2,1)}, bf16[272,1024]{1,0:T(8,128)(2,1)S(1)}, u32[]{:S(2)}, u32[]{:S(2)}) collective-permute-start(bf16[272,1024]{1,0:T(8,128)(2,1)} %pack.1.refs_0_), channel_id=1, source_target_pairs={{0,2},{1,3},{2,0},{3,1},{4,6},{5,7},{6,4},{7,5},{8,10},{9,11},{10,... | collective-permute-start | bytes 1671176 | tf_op jit(solution)/shard_map/ppermute | solution.py:23
  5.6 0.7 collective-permute-start.4
  6.2 1.6 %collective-permute-start.1 = (bf16[272,1024]{1,0:T(8,128)(2,1)}, bf16[272,1024]{1,0:T(8,128)(2,1)S(1)}, u32[]{:S(2)}, u32[]{:S(2)}) collective-permute-start(bf16[272,1024]{1,0:T(8,128)(2,1)} %pack.1.refs_0_), channel_id=1, source_target_pairs={{0,16},{8,24},{16,0},{24,8},{1,17},{9,25},{17,1},{25,9},{2,18},{10... | collective-permute-start | bytes 1671176 | tf_op jit(solution)/shard_map/ppermute | solution.py:23
  7.8 10.6 %collective-permute-done.refs_1_ = bf16[272,1024]{1,0:T(8,128)(2,1)S(1)} collective-permute-done((bf16[272,1024]{1,0:T(8,128)(2,1)}, bf16[272,1024]{1,0:T(8,128)(2,1)S(1)}, u32[]{:S(2)}, u32[]{:S(2)}) %collective-permute-start) | collective-permute-done | bytes 557088 | tf_op jit(solution)/shard_map/ppermute | solution.py:23
  18.4 0.7 collective-permute-start.2
  19.1 0.0 collective-permute-done.4
  19.1 1.1 %broadcast_select_fusion.1.refs_3_ = bf16[272,1024]{1,0:T(8,128)(2,1)S(1)} fusion(bf16[272,1024]{1,0:T(8,128)(2,1)S(1)} %collective-permute-done.4, bf16[272,1024]{1,0:T(8,128)(2,1)} %pack.1.refs_0_, pred[]{:T(512)S(6)} %ne.25), kind=kLoop, calls=%fused_computation.1 | loop fusion | flops 278528 | bytes 1671169 | tf_op jit(solution)/shard_map/jit(_where)/select_n | solution.py:343
  20.3 0.1 collective-permute-start.7
  20.3 1.8 %collective-permute-start.5 = (bf16[272,1024]{1,0:T(8,128)(2,1)S(1)}, bf16[272,1024]{1,0:T(8,128)(2,1)}, u32[]{:S(2)}, u32[]{:S(2)}) collective-permute-start(bf16[272,1024]{1,0:T(8,128)(2,1)S(1)} %broadcast_select_fusion.1.refs_3_), channel_id=1, source_target_pairs={{0,1},{1,0},{2,3},{3,2},{4,5},{5,4},{6,7},{7,6},{8,9},{9,8},{10,11... | collective-permute-start | bytes 1671176 | tf_op jit(solution)/shard_map/ppermute | solution.py:23
  22.1 1.5 %collective-permute-start.3 = (bf16[272,1024]{1,0:T(8,128)(2,1)S(1)}, bf16[272,1024]{1,0:T(8,128)(2,1)S(1)}, u32[]{:S(2)}, u32[]{:S(2)}) collective-permute-start(bf16[272,1024]{1,0:T(8,128)(2,1)S(1)} %collective-permute-done.refs_1_), channel_id=1, source_target_pairs={{0,16},{8,24},{16,0},{24,8},{1,17},{9,25},{17,1},{25,9},{2,18},{10... | collective-permute-start | bytes 1671176 | tf_op jit(solution)/shard_map/ppermute | solution.py:23
  23.6 1.0 broadcast_select_fusion.refs_5_
  24.6 0.1 copy-done.5
  24.6 0.5 collective-permute-start.9
  25.1 10.8 %collective-permute-done.5.refs_3_ = bf16[272,1024]{1,0:T(8,128)(2,1)} collective-permute-done((bf16[272,1024]{1,0:T(8,128)(2,1)S(1)}, bf16[272,1024]{1,0:T(8,128)(2,1)}, u32[]{:S(2)}, u32[]{:S(2)}) %collective-permute-start.5) | collective-permute-done | bytes 557088 | tf_op jit(solution)/shard_map/ppermute | solution.py:23
  35.9 0.9 collective-permute-done.3.refs_3_
  36.8 0.8 copy-done.6
  37.6 3.6 %keys.1 = (bf16[512,1024]{1,0:T(8,128)(2,1)}, bf16[512,1024]{1,0:T(8,128)(2,1)}, f32[512,128]{1,0:T(8,128)}) custom-call(bf16[272,1024]{1,0:T(8,128)(2,1)} %pack.1.refs_0_, bf16[272,1024]{1,0:T(8,128)(2,1)} %copy-done.3, bf16[272,1024]{1,0:T(8,128)(2,1)} %copy-done.5, bf16[272,1024]{1,0:T(8,128)(2,1)} %copy-done.6), custom_call_target="tpu_custom_call" | custom-call | flops 4194304 | bytes 2228224 | tf_op jit(solution)/shard_map/keys/pallas_call | solution.py:62
  41.2 5.6 %tile.2 = (bf16[512,1024]{1,0:T(8,128)(2,1)}, f32[512,512]{1,0:T(8,128)}, f32[512,512]{1,0:T(8,128)}, f32[8,512]{1,0:T(8,128)}, f32[512,128]{1,0:T(8,128)}) custom-call(bf16[512,1024]{1,0:T(8,128)(2,1)} %get-tuple-element.38.refs_0_, bf16[512,1024]{1,0:T(8,128)(2,1)} %get-tuple-element.39.refs_1_, f32[512,128]{1,0:T(8,128)} %get-tuple-element.40.refs_2_.refs_0_, ...), custom_call_target="tpu_custom_call" | custom-call | flops 1073741824 | bytes 4587520 | tf_op jit(solution)/shard_map/tile/pallas_call | solution.py:62
  46.8 0.6 collective-permute-done.9.refs_5_
  47.4 2.2 %collective-permute-done.10.refs_6_ = bf16[272,1024]{1,0:T(8,128)(2,1)S(1)} collective-permute-done((bf16[272,1024]{1,0:T(8,128)(2,1)}, bf16[272,1024]{1,0:T(8,128)(2,1)S(1)}, u32[]{:S(2)}, u32[]{:S(2)}) %collective-permute-start.10) | collective-permute-done | bytes 557088 | tf_op jit(solution)/shard_map/ppermute | solution.py:23
  49.6 0.8 copy-done.4
  50.4 5.7 %tile.3 = (bf16[512,1024]{1,0:T(8,128)(2,1)}, f32[512,512]{1,0:T(8,128)}, f32[512,512]{1,0:T(8,128)}, f32[8,512]{1,0:T(8,128)}, f32[512,128]{1,0:T(8,128)}, /*index=5*/f32[8,512]{1,0:T(8,128)}) custom-call(bf16[512,1024]{1,0:T(8,128)(2,1)} %get-tuple-element.38.refs_0_, bf16[512,1024]{1,0:T(8,128)(2,1)} %get-tuple-element.39.refs_1_, ...), custom_call_target="tpu_custom_call" | custom-call | flops 1073741824 | bytes 4849664 | tf_op jit(solution)/shard_map/tile/pallas_call | solution.py:62
  56.1 1.4 %payload.1 = f32[256,128]{1,0:T(8,128)} custom-call(f32[8,512]{1,0:T(8,128)} %get-tuple-element.46.sums_ref.refs_1_), custom_call_target="tpu_custom_call" | custom-call | bytes 16384 | tf_op jit(solution)/shard_map/payload/pallas_call | solution.py:62
  57.4 7.6 %all-to-all-start = ((f32[32,8,128]{2,1,0:T(8,128)}), f32[32,8,128]{2,1,0:T(8,128)S(1)}, u32[]{:S(2)}, u32[]{:S(2)}) async-start(f32[32,8,128]{2,1,0:T(8,128)} %bitcast.7), calls=%async_computation | async-start | bytes 262144 | tf_op jit(solution)/shard_map/all_to_all | solution.py:403
  65.1 2.7 %collective-permute-start.13 = (f32[8,512]{1,0:T(8,128)S(1)}, f32[8,512]{1,0:T(8,128)S(1)}, u32[]{:S(2)}, u32[]{:S(2)}) collective-permute-start(f32[8,512]{1,0:T(8,128)S(1)} %copy-done.8), channel_id=1, source_target_pairs={{0,18},{1,19},{2,16},{3,17},{4,22},{5,23},{6,20},{7,21},{8,26},{9,... | collective-permute-start | bytes 49160 | tf_op jit(solution)/shard_map/ppermute | solution.py:396
  67.8 0.6 collective-permute-start.12
  68.4 0.3 collective-permute-start.11
  68.6 1.4 %collective-permute-done.13.refs_4_ = f32[8,512]{1,0:T(8,128)S(1)} collective-permute-done((f32[8,512]{1,0:T(8,128)S(1)}, f32[8,512]{1,0:T(8,128)S(1)}, u32[]{:S(2)}, u32[]{:S(2)}) %collective-permute-start.13) | collective-permute-done | bytes 16416 | tf_op jit(solution)/shard_map/ppermute | solution.py:396
  70.0 1.7 %collective-permute-done.12.refs_3_ = f32[8,512]{1,0:T(8,128)S(1)} collective-permute-done((f32[8,512]{1,0:T(8,128)S(1)}, f32[8,512]{1,0:T(8,128)S(1)}, u32[]{:S(2)}, u32[]{:S(2)}) %collective-permute-start.12) | collective-permute-done | bytes 16416 | tf_op jit(solution)/shard_map/ppermute | solution.py:396
  71.6 0.5 collective-permute-done.11.refs_2_
  72.2 0.6 all-to-all-done
  72.8 0.6 copy-done.7
  73.4 1.9 %merge.1 = (f32[8,1024]{1,0:T(8,128)}, f32[512,128]{1,0:T(8,128)}, f32[256,128]{1,0:T(8,128)}) custom-call(f32[256,128]{1,0:T(8,128)} %bitcast.6, f32[8,512]{1,0:T(8,128)} %get-tuple-element.46.sums_ref.refs_1_, f32[8,512]{1,0:T(8,128)} %copy-done.11, f32[8,512]{1,0:T(8,128)} %copy-done.10, f32[8,512]{1,0:T(8,128)} %copy-done.9), custom_call_target="tpu_custom_call" | custom-call | bytes 196608 | tf_op jit(solution)/shard_map/merge/pallas_call | solution.py:62
  75.3 4.9 %grads.2 = (s16[144,1024]{1,0:T(8,128)(2,1)}, s16[144,1024]{1,0:T(8,128)(2,1)}) custom-call(f32[512,128]{1,0:T(8,128)} %get-tuple-element.40.refs_2_.refs_0_, f32[512,128]{1,0:T(8,128)} %get-tuple-element.62.refs_1_, f32[8,1024]{1,0:T(8,128)} %get-tuple-element.49.refs_2_, f32[512,512]{1,0:T(8,128)} %get-tuple-element.50.refs_3_, ...), custom_call_target="tpu_custom_call" | custom-call | flops 1073741824 | bytes 6881280 | tf_op jit(solution)/shard_map/grads/pallas_call | solution.py:62
  80.2 1.0 collective-permute-start.14
  81.2 4.8 %grads.3 = (f32[128,1024]{1,0:T(8,128)}, s16[144,1024]{1,0:T(8,128)(2,1)}) custom-call(f32[512,128]{1,0:T(8,128)} %get-tuple-element.40.refs_2_.refs_0_, f32[512,128]{1,0:T(8,128)} %get-tuple-element.62.refs_1_, f32[8,1024]{1,0:T(8,128)} %get-tuple-element.49.refs_2_, f32[512,512]{1,0:T(8,128)} %get-tuple-element.50.refs_3_, ...), custom_call_target="tpu_custom_call" | custom-call | flops 1073741824 | bytes 6881280 | tf_op jit(solution)/shard_map/grads/pallas_call | solution.py:62
  86.0 1.6 %collective-permute-start.15 = (s16[144,1024]{1,0:T(8,128)(2,1)}, s16[144,1024]{1,0:T(8,128)(2,1)S(1)}, u32[]{:S(2)}, u32[]{:S(2)}) collective-permute-start(s16[144,1024]{1,0:T(8,128)(2,1)} %get-tuple-element.66), channel_id=1, source_target_pairs={{0,2},{1,3},{2,0},{3,1},{4,6},{5,7},{6,4},{7,5},{8,10},{9,11},{10,... | collective-permute-start | bytes 884744 | tf_op jit(solution)/shard_map/ppermute | solution.py:438
  87.6 0.9 collective-permute-start.16
  88.5 2.7 %collective-permute-done.14.refs_2_ = s16[144,1024]{1,0:T(8,128)(2,1)S(1)} collective-permute-done((s16[144,1024]{1,0:T(8,128)(2,1)}, s16[144,1024]{1,0:T(8,128)(2,1)S(1)}, u32[]{:S(2)}, u32[]{:S(2)}) %collective-permute-start.14) | collective-permute-done | bytes 294944 | tf_op jit(solution)/shard_map/ppermute | solution.py:438
  91.2 2.7 %all-to-all-start.1 = ((f32[32,8,128]{2,1,0:T(8,128)}), f32[32,8,128]{2,1,0:T(8,128)S(1)}, u32[]{:S(2)}, u32[]{:S(2)}) async-start(f32[32,8,128]{2,1,0:T(8,128)} %bitcast.3), calls=%async_computation.1 | async-start | bytes 262144 | tf_op jit(solution)/shard_map/all_to_all | solution.py:441
  93.9 2.0 %collective-permute-done.15.refs_0_ = s16[144,1024]{1,0:T(8,128)(2,1)S(1)} collective-permute-done((s16[144,1024]{1,0:T(8,128)(2,1)}, s16[144,1024]{1,0:T(8,128)(2,1)S(1)}, u32[]{:S(2)}, u32[]{:S(2)}) %collective-permute-start.15) | collective-permute-done | bytes 294944 | tf_op jit(solution)/shard_map/ppermute | solution.py:438
  95.8 0.8 collective-permute-done.16.refs_1_
  96.6 1.0 %copy-done.1 = f32[128,1024]{1,0:T(8,128)S(1)} copy-done((f32[128,1024]{1,0:T(8,128)S(1)}, f32[128,1024]{1,0:T(8,128)}, u32[]{:S(2)}) %copy-start.1) | copy-done | bytes 524312
  97.7 1.3 %final.1 = f32[128,1024]{1,0:T(8,128)} custom-call(bf16[128,1024]{1,0:T(8,128)(2,1)S(1)} %copy-done, f32[128,1024]{1,0:T(8,128)S(1)} %copy-done.1, s16[144,1024]{1,0:T(8,128)(2,1)S(1)} %collective-permute-done.15.refs_0_, s16[144,1024]{1,0:T(8,128)(2,1)S(1)} %collective-permute-done.16.refs_1_, s16[144,1024]{1,0:T(8,128)(2,1)S(1)} %collective-permute-done.14.refs_2_), custom_call_target="tpu_custom_call" | custom-call | flops 1048576 | bytes 1671168 | tf_op jit(solution)/shard_map/final/pallas_call | solution.py:62
  99.0 2.6 %all-to-all-done.1 = f32[32,8,128]{2,1,0:T(8,128)S(1)} async-done(((f32[32,8,128]{2,1,0:T(8,128)}), f32[32,8,128]{2,1,0:T(8,128)S(1)}, u32[]{:S(2)}, u32[]{:S(2)}) %all-to-all-start.1) | async-done | bytes 131104 | tf_op jit(solution)/shard_map/all_to_all | solution.py:441
  101.6 0.1 slice_reduce_fusion
  101.7 0.6 fusion
  (30 shorter events, 0.1 us)
Async XLA Ops:
  2.5 15.9 %collective-permute-start = (bf16[272,1024]{1,0:T(8,128)(2,1)}, bf16[272,1024]{1,0:T(8,128)(2,1)S(1)}, u32[]{:S(2)}, u32[]{:S(2)}) collective-permute-start(bf16[272,1024]{1,0:T(8,128)(2,1)} %pack.1.refs_0_), channel_id=1, source_target_pairs={{0,2},{1,3},{2,0},{3,1},{4,6},{5,7},{6,4},{7,5},{8,10},{9,11},{10,... | collective-permute-start | bytes 1671176 | tf_op jit(solution)/shard_map/ppermute | solution.py:23
  5.6 13.6 %collective-permute-start.4 = (bf16[272,1024]{1,0:T(8,128)(2,1)}, bf16[272,1024]{1,0:T(8,128)(2,1)S(1)}, u32[]{:S(2)}, u32[]{:S(2)}) collective-permute-start(bf16[272,1024]{1,0:T(8,128)(2,1)} %pack.1.refs_0_), channel_id=1, source_target_pairs={{2,4},{3,5},{4,2},{5,3},{10,12},{11,13},{12,10},{13,11},{18,20},{1... | collective-permute-start | bytes 1671176 | tf_op jit(solution)/shard_map/ppermute | solution.py:337
  6.2 17.3 %collective-permute-start.1 = (bf16[272,1024]{1,0:T(8,128)(2,1)}, bf16[272,1024]{1,0:T(8,128)(2,1)S(1)}, u32[]{:S(2)}, u32[]{:S(2)}) collective-permute-start(bf16[272,1024]{1,0:T(8,128)(2,1)} %pack.1.refs_0_), channel_id=1, source_target_pairs={{0,16},{8,24},{16,0},{24,8},{1,17},{9,25},{17,1},{25,9},{2,18},{10... | collective-permute-start | bytes 1671176 | tf_op jit(solution)/shard_map/ppermute | solution.py:23
  18.4 5.2 %copy-start.3 = (bf16[272,1024]{1,0:T(8,128)(2,1)}, bf16[272,1024]{1,0:T(8,128)(2,1)S(1)}, u32[]{:S(2)}) copy-start(bf16[272,1024]{1,0:T(8,128)(2,1)S(1)} %collective-permute-done.refs_1_) | copy-start | bytes 1671172
  18.4 5.2 %collective-permute-start.2 = (bf16[272,1024]{1,0:T(8,128)(2,1)S(1)}, bf16[272,1024]{1,0:T(8,128)(2,1)S(1)}, u32[]{:S(2)}, u32[]{:S(2)}) collective-permute-start(bf16[272,1024]{1,0:T(8,128)(2,1)S(1)} %collective-permute-done.refs_1_), channel_id=1, source_target_pairs={{2,4},{3,5},{4,2},{5,3},{10,12},{11,13},{12,10},{13,11},{18,20},{1... | collective-permute-start | bytes 1671176 | tf_op jit(solution)/shard_map/ppermute | solution.py:341
  20.3 4.3 %copy-start.2 = (bf16[272,1024]{1,0:T(8,128)(2,1)}, bf16[272,1024]{1,0:T(8,128)(2,1)S(1)}, u32[]{:S(2)}) copy-start(bf16[272,1024]{1,0:T(8,128)(2,1)S(1)} %broadcast_select_fusion.1.refs_3_) | copy-start | bytes 1671172
  20.3 21.0 %collective-permute-start.7 = (bf16[272,1024]{1,0:T(8,128)(2,1)S(1)}, bf16[272,1024]{1,0:T(8,128)(2,1)}, u32[]{:S(2)}, u32[]{:S(2)}) collective-permute-start(bf16[272,1024]{1,0:T(8,128)(2,1)S(1)} %broadcast_select_fusion.1.refs_3_), channel_id=1, source_target_pairs={{0,8},{8,0},{16,24},{24,16},{1,9},{9,1},{17,25},{25,17},{2,10},{10... | collective-permute-start | bytes 1671176 | tf_op jit(solution)/shard_map/ppermute | solution.py:23
  20.3 15.6 %collective-permute-start.5 = (bf16[272,1024]{1,0:T(8,128)(2,1)S(1)}, bf16[272,1024]{1,0:T(8,128)(2,1)}, u32[]{:S(2)}, u32[]{:S(2)}) collective-permute-start(bf16[272,1024]{1,0:T(8,128)(2,1)S(1)} %broadcast_select_fusion.1.refs_3_), channel_id=1, source_target_pairs={{0,1},{1,0},{2,3},{3,2},{4,5},{5,4},{6,7},{7,6},{8,9},{9,8},{10,11... | collective-permute-start | bytes 1671176 | tf_op jit(solution)/shard_map/ppermute | solution.py:23
  22.1 14.7 %collective-permute-start.3 = (bf16[272,1024]{1,0:T(8,128)(2,1)S(1)}, bf16[272,1024]{1,0:T(8,128)(2,1)S(1)}, u32[]{:S(2)}, u32[]{:S(2)}) collective-permute-start(bf16[272,1024]{1,0:T(8,128)(2,1)S(1)} %collective-permute-done.refs_1_), channel_id=1, source_target_pairs={{0,16},{8,24},{16,0},{24,8},{1,17},{9,25},{17,1},{25,9},{2,18},{10... | collective-permute-start | bytes 1671176 | tf_op jit(solution)/shard_map/ppermute | solution.py:23
  23.6 1.0 %copy-start.5 = (bf16[272,1024]{1,0:T(8,128)(2,1)}, bf16[272,1024]{1,0:T(8,128)(2,1)S(1)}, u32[]{:S(2)}) copy-start(bf16[272,1024]{1,0:T(8,128)(2,1)S(1)} %collective-permute-done.1.refs_2_) | copy-start | bytes 1671172
  24.6 16.6 %collective-permute-start.8 = (bf16[272,1024]{1,0:T(8,128)(2,1)}, bf16[272,1024]{1,0:T(8,128)(2,1)}, u32[]{:S(2)}, u32[]{:S(2)}) collective-permute-start(bf16[272,1024]{1,0:T(8,128)(2,1)} %broadcast_select_fusion.refs_5_), channel_id=1, source_target_pairs={{0,8},{8,0},{16,24},{24,16},{1,9},{9,1},{17,25},{25,17},{2,10},{10... | collective-permute-start | bytes 1671176 | tf_op jit(solution)/shard_map/ppermute | solution.py:23
  24.6 22.8 %collective-permute-start.9 = (bf16[272,1024]{1,0:T(8,128)(2,1)}, bf16[272,1024]{1,0:T(8,128)(2,1)}, u32[]{:S(2)}, u32[]{:S(2)}) collective-permute-start(bf16[272,1024]{1,0:T(8,128)(2,1)} %broadcast_select_fusion.refs_5_), channel_id=1, source_target_pairs={{0,1},{1,0},{2,3},{3,2},{4,5},{5,4},{6,7},{7,6},{8,9},{9,8},{10,11... | collective-permute-start | bytes 1671176 | tf_op jit(solution)/shard_map/ppermute | solution.py:23
  36.8 0.8 copy-start.6
  37.6 9.8 %collective-permute-start.6 = (bf16[272,1024]{1,0:T(8,128)(2,1)}, bf16[272,1024]{1,0:T(8,128)(2,1)}, u32[]{:S(2)}, u32[]{:S(2)}) collective-permute-start(bf16[272,1024]{1,0:T(8,128)(2,1)} %collective-permute-done.5.refs_3_), channel_id=1, source_target_pairs={{0,8},{8,0},{16,24},{24,16},{1,9},{9,1},{17,25},{25,17},{2,10},{10... | collective-permute-start | bytes 1671176 | tf_op jit(solution)/shard_map/ppermute | solution.py:23
  47.4 2.2 %collective-permute-start.10 = (bf16[272,1024]{1,0:T(8,128)(2,1)}, bf16[272,1024]{1,0:T(8,128)(2,1)S(1)}, u32[]{:S(2)}, u32[]{:S(2)}) collective-permute-start(bf16[272,1024]{1,0:T(8,128)(2,1)} %collective-permute-done.9.refs_5_), channel_id=1, source_target_pairs={{0,8},{8,0},{16,24},{24,16},{1,9},{9,1},{17,25},{25,17},{2,10},{10... | collective-permute-start | bytes 1671176 | tf_op jit(solution)/shard_map/ppermute | solution.py:23
  49.6 0.8 copy-start.4
  57.4 7.6 %copy-start.8 = (f32[8,512]{1,0:T(8,128)S(1)}, f32[8,512]{1,0:T(8,128)}, u32[]{:S(2)}) copy-start(f32[8,512]{1,0:T(8,128)} %get-tuple-element.46.sums_ref.refs_1_) | copy-start | bytes 49156
  57.4 15.3 %all-to-all-start = ((f32[32,8,128]{2,1,0:T(8,128)}), f32[32,8,128]{2,1,0:T(8,128)S(1)}, u32[]{:S(2)}, u32[]{:S(2)}) async-start(f32[32,8,128]{2,1,0:T(8,128)} %bitcast.7), calls=%async_computation | async-start | bytes 262144 | tf_op jit(solution)/shard_map/all_to_all | solution.py:403
  65.1 4.9 %collective-permute-start.13 = (f32[8,512]{1,0:T(8,128)S(1)}, f32[8,512]{1,0:T(8,128)S(1)}, u32[]{:S(2)}, u32[]{:S(2)}) collective-permute-start(f32[8,512]{1,0:T(8,128)S(1)} %copy-done.8), channel_id=1, source_target_pairs={{0,18},{1,19},{2,16},{3,17},{4,22},{5,23},{6,20},{7,21},{8,26},{9,... | collective-permute-start | bytes 49160 | tf_op jit(solution)/shard_map/ppermute | solution.py:396
  67.8 3.8 %collective-permute-start.12 = (f32[8,512]{1,0:T(8,128)S(1)}, f32[8,512]{1,0:T(8,128)S(1)}, u32[]{:S(2)}, u32[]{:S(2)}) collective-permute-start(f32[8,512]{1,0:T(8,128)S(1)} %copy-done.8), channel_id=1, source_target_pairs={{0,16},{1,17},{2,18},{3,19},{4,20},{5,21},{6,22},{7,23},{8,24},{9,... | collective-permute-start | bytes 49160 | tf_op jit(solution)/shard_map/ppermute | solution.py:396
  68.4 3.8 %collective-permute-start.11 = (f32[8,512]{1,0:T(8,128)S(1)}, f32[8,512]{1,0:T(8,128)S(1)}, u32[]{:S(2)}, u32[]{:S(2)}) collective-permute-start(f32[8,512]{1,0:T(8,128)S(1)} %copy-done.8), channel_id=1, source_target_pairs={{0,2},{1,3},{2,0},{3,1},{4,6},{5,7},{6,4},{7,5},{8,10},{9,11},{10,... | collective-permute-start | bytes 49160 | tf_op jit(solution)/shard_map/ppermute | solution.py:396
  70.0 2.8 %copy-start.9 = (f32[8,512]{1,0:T(8,128)}, f32[8,512]{1,0:T(8,128)S(1)}, u32[]{:S(2)}) copy-start(f32[8,512]{1,0:T(8,128)S(1)} %collective-permute-done.13.refs_4_) | copy-start | bytes 49156
  71.6 1.2 %copy-start.10 = (f32[8,512]{1,0:T(8,128)}, f32[8,512]{1,0:T(8,128)S(1)}, u32[]{:S(2)}) copy-start(f32[8,512]{1,0:T(8,128)S(1)} %collective-permute-done.12.refs_3_) | copy-start | bytes 49156
  72.2 0.6 copy-start.11
  72.8 0.7 copy-start.7
  80.2 11.0 %collective-permute-start.14 = (s16[144,1024]{1,0:T(8,128)(2,1)}, s16[144,1024]{1,0:T(8,128)(2,1)S(1)}, u32[]{:S(2)}, u32[]{:S(2)}) collective-permute-start(s16[144,1024]{1,0:T(8,128)(2,1)} %get-tuple-element.59), channel_id=1, source_target_pairs={{0,18},{1,19},{2,16},{3,17},{4,22},{5,23},{6,20},{7,21},{8,26},{9,... | collective-permute-start | bytes 884744 | tf_op jit(solution)/shard_map/ppermute | solution.py:438
  81.2 6.4 %copy-start.12 = (s16[144,1024]{1,0:T(8,128)(2,1)S(1)}, s16[144,1024]{1,0:T(8,128)(2,1)}, u32[]{:S(2)}) copy-start(s16[144,1024]{1,0:T(8,128)(2,1)} %get-tuple-element.67) | copy-start | bytes 884740
  86.0 10.6 %copy-start = (bf16[128,1024]{1,0:T(8,128)(2,1)S(1)}, bf16[128,1024]{1,0:T(8,128)(2,1)}, u32[]{:S(2)}) copy-start(bf16[128,1024]{1,0:T(8,128)(2,1)} %student_ref.3) | copy-start | bytes 786436
  86.0 9.8 %collective-permute-start.15 = (s16[144,1024]{1,0:T(8,128)(2,1)}, s16[144,1024]{1,0:T(8,128)(2,1)S(1)}, u32[]{:S(2)}, u32[]{:S(2)}) collective-permute-start(s16[144,1024]{1,0:T(8,128)(2,1)} %get-tuple-element.66), channel_id=1, source_target_pairs={{0,2},{1,3},{2,0},{3,1},{4,6},{5,7},{6,4},{7,5},{8,10},{9,11},{10,... | collective-permute-start | bytes 884744 | tf_op jit(solution)/shard_map/ppermute | solution.py:438
  87.6 9.1 %collective-permute-start.16 = (s16[144,1024]{1,0:T(8,128)(2,1)S(1)}, s16[144,1024]{1,0:T(8,128)(2,1)S(1)}, u32[]{:S(2)}, u32[]{:S(2)}) collective-permute-start(s16[144,1024]{1,0:T(8,128)(2,1)S(1)} %copy-done.12), channel_id=1, source_target_pairs={{0,16},{1,17},{2,18},{3,19},{4,20},{5,21},{6,22},{7,23},{8,24},{9,... | collective-permute-start | bytes 884744 | tf_op jit(solution)/shard_map/ppermute | solution.py:438
  91.2 10.4 %all-to-all-start.1 = ((f32[32,8,128]{2,1,0:T(8,128)}), f32[32,8,128]{2,1,0:T(8,128)S(1)}, u32[]{:S(2)}, u32[]{:S(2)}) async-start(f32[32,8,128]{2,1,0:T(8,128)} %bitcast.3), calls=%async_computation.1 | async-start | bytes 262144 | tf_op jit(solution)/shard_map/all_to_all | solution.py:441
  96.6 1.0 %copy-start.1 = (f32[128,1024]{1,0:T(8,128)S(1)}, f32[128,1024]{1,0:T(8,128)}, u32[]{:S(2)}) copy-start(f32[128,1024]{1,0:T(8,128)} %get-tuple-element.65.own_ref) | copy-start | bytes 1572868
